TPU v7x, 256 devices: a whole 4x4x8 slice. The times are simulated.
256 devices in a mesh: gz: 16 (over z, core), gy: 8 (over y, x_hi), orb: 2 (over x_lo).
Axes of the slice: x: 4 (x_hi: 2, x_lo: 2; x = x_hi * 2 + x_lo), y: 4, z: 8, core: 2. Of those that a mesh axis runs over, the one named last changes fastest.
Arguments:
- orbitals: bfloat16 [4096, 24, 576], P(('gz', 'gy', 'orb')), may hold values from -6 to 6
- occupation: float32 [4096], P(('gz', 'gy', 'orb')), may hold values from 0.5 to 2
- corners: int32 [4096, 3], P(('gz', 'gy', 'orb')), may hold values from 0 to 383, as said below
- kernel_widths: float32 [8], replicated, may hold values from 0.7 to 2.5
- w_in: float32 [8, 64], replicated, may hold values from -2 to 2
- b_in: float32 [64], replicated, may hold values from -3 to 3
- w_mid: float32 [64, 64], replicated, may hold values from -0.75 to 0.75
- b_mid: float32 [64], replicated, may hold values from -3 to 3
- w_out: float32 [64], replicated, may hold values from -0.75 to 0.75
- b_out: float32 [1], replicated, may hold values from -3 to 3
Outputs:
- potential: bfloat16 [384, 192, 128], P('gz', 'gy')
- applied: bfloat16 [4096, 24, 576], P(('gz', 'gy', 'orb'))
Inputs may be any that keep to these rules, and one draw needn't show every extreme that they name: Orbital i is held by device i // 16 of the axes gz, gy, orb taken together. Its row corners[i,1] lies in the 24 rows of that device's gy index. Among the 16 orbitals of one device, at most 2 have their plane corners[i,0] in the same slab of 24 planes, and on every device some slab holds exactly 2 of them. Columns lie in 0 to 127, rows in 0 to 191, planes in 0 to 383; the first and the last plane are taken in every draw.
All inputs are finite; a program needn't handle non-finite values.
Results may differ from a plain program's by a relative error of at most 0.0055.
Values may be sent and summed in bfloat16 or wider, within the bound.
No kernel may reach another device: no remote copies, remote signals or barrier semaphores. Data moves between devices by JAX's collectives and lax.ppermute only.
A program may use at most 64 MiB of HBM per device.

v0:
```python
import jax
import jax.numpy as jnp
from jax import lax
from jax.sharding import PartitionSpec as P

BOX = 24
CHAN = 8
RAD = 6
CZ = 24
CY = 24
NX = 128
CAP = 2
CELL_BLOCK = 12288


exact_mode = lax.Precision.HIGHEST


def shifted(x, axis, by):
    count = lax.axis_size(axis)
    return lax.ppermute(x, axis, [(i, (i + by) % count) for i in range(count)])


def extended_2(cells, sides, width):
    for axis, dim in sides:
        count = lax.axis_size(axis)
        head = lax.slice_in_dim(cells, 0, width, axis=dim)
        tail = lax.slice_in_dim(cells, cells.shape[dim] - width, cells.shape[dim], axis=dim)
        cells = jnp.concatenate(
            [
                lax.ppermute(tail, axis, [(i, (i + 1) % count) for i in range(count)]),
                cells,
                lax.ppermute(head, axis, [((i + 1) % count, i) for i in range(count)]),
            ],
            axis=dim,
        )
    return cells


def for_sending(x):
    return jax.tree.map(lambda a: a.astype(jnp.bfloat16) if a.dtype == jnp.float32 else a, x)


def kernel_taps(kernel_widths):
    offsets = jnp.arange(-RAD, RAD + 1).astype(jnp.float32)
    raw = jnp.exp(-offsets[None, :] ** 2 / (2.0 * kernel_widths[:, None] ** 2))
    return raw / jnp.sum(raw, axis=1, keepdims=True)


def tap_table(taps, distance):
    table = jnp.zeros((taps.shape[0],) + distance.shape, jnp.float32)
    for step in range(2 * RAD + 1):
        table = table + taps[:, step][:, None, None] * (distance == step).astype(jnp.float32)[None]
    return table


def smooth_all(padded, taps, planes, rows):
    columns = padded.shape[2]
    source = jnp.arange(columns, dtype=jnp.int32)
    circular = (source[:, None] - source[None, :] + RAD) % columns
    across_table = tap_table(taps, circular)
    across = jnp.einsum("prs,kst->kprt", padded, across_table, precision=exact_mode)
    row_out = jnp.arange(rows, dtype=jnp.int32)
    row_in = jnp.arange(rows + 2 * RAD, dtype=jnp.int32)
    row_table = tap_table(taps, row_in[None, :] - row_out[:, None])
    lines = jnp.einsum("kqr,kprt->kpqt", row_table, across, precision=exact_mode)
    plane_out = jnp.arange(planes, dtype=jnp.int32)
    plane_in = jnp.arange(planes + 2 * RAD, dtype=jnp.int32)
    plane_table = tap_table(taps, plane_in[None, :] - plane_out[:, None])
    return jnp.einsum("kop,kpqt->koqt", plane_table, lines, precision=exact_mode)


def network(features, w_in, b_in, w_mid, b_mid, w_out, b_out):
    count = features.shape[1]
    blocks = features.reshape(CHAN, count // CELL_BLOCK, CELL_BLOCK).transpose(1, 0, 2)

    def layer_stack(block):
        hidden = jax.nn.silu(jnp.dot(w_in.T, block, precision=exact_mode) + b_in[:, None])
        hidden = jax.nn.silu(jnp.dot(w_mid.T, hidden, precision=exact_mode) + b_mid[:, None])
        return jnp.dot(w_out, hidden, precision=exact_mode) + b_out[0]

    return lax.map(layer_stack, blocks).reshape(count)


def local(orbitals, occupation, corners, kernel_widths, w_in, b_in, w_mid, b_mid, w_out, b_out):
    slab_count = lax.axis_size("gz")
    slot_count = slab_count * CAP
    held = orbitals.shape[0]
    orbital_vals = orbitals.astype(jnp.float32)
    box_density = (occupation[:, None, None] * orbital_vals * orbital_vals).astype(jnp.bfloat16)
    box_density = box_density.reshape(held, BOX**3)
    target = corners[:, 0] // CZ
    orbital_ids = jnp.arange(held, dtype=jnp.int32)
    earlier = (target[:, None] == target[None, :]) & (orbital_ids[None, :] < orbital_ids[:, None])
    slot_rank = jnp.sum(earlier.astype(jnp.int32), axis=1)
    slot_of = target * CAP + slot_rank
    placer = (jnp.arange(slot_count, dtype=jnp.int32)[:, None] == slot_of[None, :]).astype(
        jnp.bfloat16
    )
    local_offsets = jnp.stack(
        [corners[:, 0] % CZ, corners[:, 1] % CY, corners[:, 2]], axis=1
    ).astype(jnp.bfloat16)
    sent = jnp.dot(placer, box_density, preferred_element_type=jnp.float32).astype(jnp.bfloat16)
    sent_offsets = jnp.dot(placer, local_offsets, preferred_element_type=jnp.float32).astype(
        jnp.bfloat16
    )
    received, received_offsets = (
        lax.all_to_all(
            sent.reshape(slab_count, CAP, BOX**3), "gz", split_axis=0, concat_axis=0, tiled=True
        ),
        lax.all_to_all(
            sent_offsets.reshape(slab_count, CAP, 3), "gz", split_axis=0, concat_axis=0, tiled=True
        ),
    )
    offsets = received_offsets.astype(jnp.float32).astype(jnp.int32)

    def deposit(source, grid):
        for column in range(CAP):
            piece = received[source, column].astype(jnp.float32).reshape(BOX, BOX, BOX)
            start = (
                offsets[source, column, 0],
                offsets[source, column, 1],
                offsets[source, column, 2],
            )
            region = lax.dynamic_slice(grid, start, (BOX, BOX, BOX))
            grid = lax.dynamic_update_slice(grid, region + piece, start)
        return grid

    extended = lax.fori_loop(
        0, slab_count, deposit, jnp.zeros((CZ + BOX, CY + BOX, NX + BOX), jnp.float32)
    )
    extended = extended[:, :, :NX].at[:, :, :BOX].add(extended[:, :, NX:])
    from_below = shifted(extended[CZ:].astype(jnp.bfloat16), "gz", 1).astype(jnp.float32)
    core = extended[:CZ].at[:BOX].add(from_below)
    from_left = shifted(core[:, CY:].astype(jnp.bfloat16), "gy", 1).astype(jnp.float32)
    tile = core[:, :CY].at[:, :BOX].add(from_left)
    density = lax.psum(tile.astype(jnp.bfloat16), "orb").astype(jnp.float32)
    padded = extended_2(density.astype(jnp.bfloat16), (("gz", 0), ("gy", 1)), RAD).astype(
        density.dtype
    )
    taps = kernel_taps(kernel_widths)
    features = jnp.log1p(smooth_all(padded, taps, CZ, CY))
    values = network(features.reshape(CHAN, CZ * CY * NX), w_in, b_in, w_mid, b_mid, w_out, b_out)
    potential = values.reshape(CZ, CY, NX).astype(jnp.bfloat16)
    next_rows = shifted(potential, "gy", -1)
    wide = jnp.concatenate([potential, next_rows], axis=1)
    next_planes = shifted(wide, "gz", -1)
    reach = jnp.concatenate([wide, next_planes], axis=0)
    reach = jnp.concatenate([reach, reach[:, :, :BOX]], axis=2)

    def cut(offset_row):
        windows = []
        for column in range(CAP):
            start = (offset_row[column, 0], offset_row[column, 1], offset_row[column, 2])
            window = lax.dynamic_slice(reach, start, (BOX, BOX, BOX))
            windows.append(window.reshape(BOX**3))
        return jnp.stack(windows)

    windows = lax.map(cut, offsets)
    returned = jax.tree.map(
        lambda part, own: part.astype(own.dtype),
        lax.all_to_all(for_sending(windows), "gz", split_axis=0, concat_axis=0, tiled=True),
        windows,
    )
    on_boxes = jnp.dot(
        placer.T, returned.reshape(slot_count, BOX**3), preferred_element_type=jnp.float32
    )
    applied = (on_boxes.reshape(held, BOX, BOX * BOX) * orbital_vals).astype(jnp.bfloat16)
    return (potential, applied)


def solution(mesh):
    return jax.shard_map(
        local,
        mesh=mesh,
        in_specs=(
            P(("gz", "gy", "orb"), None, None),
            P(("gz", "gy", "orb")),
            P(("gz", "gy", "orb"), None),
            P(),
            P(),
            P(),
            P(),
            P(),
            P(),
            P(),
        ),
        out_specs=(P("gz", "gy", None), P(("gz", "gy", "orb"), None, None)),
        check_vma=False,
    )
```

profile of v0, /device:TPU:1, one launch (start us, length us, event | category | flops | bytes accessed | tf_op | source)
XLA Modules:
  0.0 1366.8 jit_solution(875957933590389903)
XLA Ops:
  10.4 10.0 all-to-all-start
  27.3 4.7 all-to-all-start.1
  37.6 19.2 %all-to-all-done.1 = bf16[16,2,13824]{2,1,0:T(2,128)(2,1)} async-done(((bf16[16,2,13824]{2,1,0:T(2,128)(2,1)}), bf16[16,2,13824]{2,1,0:T(2,128)(2,1)}, u32[]{:S(2)}, u32[]{:S(2)}) %all-to-all-start.1) | async-done | bytes 884768 | tf_op jit(solution)/shard_map/all_to_all | solution.py:108
  57.1 809.6 %while.38 = (s32[]{:T(128)}, f32[48,48,152]{2,1,0:T(8,128)S(1)}, s32[16,2,3]{0,1,2:T(2,128)S(1)}, bf16[16,2,13824]{2,1,0:T(2,128)(2,1)}, s32[]{:T(128)}, /*index=5*/s32[]{:T(128)}, s32[]{:T(128)}, s32[]{:T(128)}) while((s32[]{:T(128)}, f32[48,48,152]{2,1,0:T(8,128)S(1)}, s32[16,2,3]{0,1,2:T(2,128)S(1)}, bf16[16,2,13824]{2,1,0:T(2,128)(2,1)}, ...), condition=%wide.region_3.4_spmd, body=%wide.region_2.3_spmd.sunk | while | flops 55316 | bytes 940409 | solution.py:129
  65.0 16.8 %dynamic_update_slice.27 = f32[48,48,152]{2,1,0:T(8,128)S(1)} dynamic-update-slice(f32[48,48,152]{2,1,0:T(8,128)S(1)} %get-tuple-element.505, f32[24,24,24]{2,1,0:T(8,128)S(1)} %dynamic-slice_add_fusion.4, s32[]{:T(128)S(6)} %select_n.230, s32[]{:T(128)S(6)} %select_n.231, s32[]{:T(128)S(6)} %select_n.232) | dynamic-update-slice | bytes 110596 | tf_op jit(solution)/shard_map/while/body/eval_jaxpr/dynamic_update_slice | solution.py:126
  88.3 16.8 %dynamic_update_slice.28 = f32[48,48,152]{2,1,0:T(8,128)S(1)} dynamic-update-slice(f32[48,48,152]{2,1,0:T(8,128)S(1)} %dynamic_update_slice.27, f32[24,24,24]{2,1,0:T(8,128)S(1)} %dynamic-slice_add_fusion.5, s32[]{:T(128)S(6)} %select_n.233, s32[]{:T(128)S(6)} %select_n.234, s32[]{:T(128)S(6)} %select_n.235) | dynamic-update-slice | bytes 110596 | tf_op jit(solution)/shard_map/while/body/eval_jaxpr/dynamic_update_slice | solution.py:126
  113.0 19.7 %dynamic_update_slice.27 = f32[48,48,152]{2,1,0:T(8,128)S(1)} dynamic-update-slice(f32[48,48,152]{2,1,0:T(8,128)S(1)} %get-tuple-element.505, f32[24,24,24]{2,1,0:T(8,128)S(1)} %dynamic-slice_add_fusion.4, s32[]{:T(128)S(6)} %select_n.230, s32[]{:T(128)S(6)} %select_n.231, s32[]{:T(128)S(6)} %select_n.232) | dynamic-update-slice | bytes 110596 | tf_op jit(solution)/shard_map/while/body/eval_jaxpr/dynamic_update_slice | solution.py:126
  139.2 16.8 %dynamic_update_slice.28 = f32[48,48,152]{2,1,0:T(8,128)S(1)} dynamic-update-slice(f32[48,48,152]{2,1,0:T(8,128)S(1)} %dynamic_update_slice.27, f32[24,24,24]{2,1,0:T(8,128)S(1)} %dynamic-slice_add_fusion.5, s32[]{:T(128)S(6)} %select_n.233, s32[]{:T(128)S(6)} %select_n.234, s32[]{:T(128)S(6)} %select_n.235) | dynamic-update-slice | bytes 110596 | tf_op jit(solution)/shard_map/while/body/eval_jaxpr/dynamic_update_slice | solution.py:126
  163.9 16.8 %dynamic_update_slice.27 = f32[48,48,152]{2,1,0:T(8,128)S(1)} dynamic-update-slice(f32[48,48,152]{2,1,0:T(8,128)S(1)} %get-tuple-element.505, f32[24,24,24]{2,1,0:T(8,128)S(1)} %dynamic-slice_add_fusion.4, s32[]{:T(128)S(6)} %select_n.230, s32[]{:T(128)S(6)} %select_n.231, s32[]{:T(128)S(6)} %select_n.232) | dynamic-update-slice | bytes 110596 | tf_op jit(solution)/shard_map/while/body/eval_jaxpr/dynamic_update_slice | solution.py:126
  187.3 16.8 %dynamic_update_slice.28 = f32[48,48,152]{2,1,0:T(8,128)S(1)} dynamic-update-slice(f32[48,48,152]{2,1,0:T(8,128)S(1)} %dynamic_update_slice.27, f32[24,24,24]{2,1,0:T(8,128)S(1)} %dynamic-slice_add_fusion.5, s32[]{:T(128)S(6)} %select_n.233, s32[]{:T(128)S(6)} %select_n.234, s32[]{:T(128)S(6)} %select_n.235) | dynamic-update-slice | bytes 110596 | tf_op jit(solution)/shard_map/while/body/eval_jaxpr/dynamic_update_slice | solution.py:126
  211.9 17.7 %dynamic_update_slice.27 = f32[48,48,152]{2,1,0:T(8,128)S(1)} dynamic-update-slice(f32[48,48,152]{2,1,0:T(8,128)S(1)} %get-tuple-element.505, f32[24,24,24]{2,1,0:T(8,128)S(1)} %dynamic-slice_add_fusion.4, s32[]{:T(128)S(6)} %select_n.230, s32[]{:T(128)S(6)} %select_n.231, s32[]{:T(128)S(6)} %select_n.232) | dynamic-update-slice | bytes 110596 | tf_op jit(solution)/shard_map/while/body/eval_jaxpr/dynamic_update_slice | solution.py:126
  236.2 16.8 %dynamic_update_slice.28 = f32[48,48,152]{2,1,0:T(8,128)S(1)} dynamic-update-slice(f32[48,48,152]{2,1,0:T(8,128)S(1)} %dynamic_update_slice.27, f32[24,24,24]{2,1,0:T(8,128)S(1)} %dynamic-slice_add_fusion.5, s32[]{:T(128)S(6)} %select_n.233, s32[]{:T(128)S(6)} %select_n.234, s32[]{:T(128)S(6)} %select_n.235) | dynamic-update-slice | bytes 110596 | tf_op jit(solution)/shard_map/while/body/eval_jaxpr/dynamic_update_slice | solution.py:126
  260.8 21.5 %dynamic_update_slice.27 = f32[48,48,152]{2,1,0:T(8,128)S(1)} dynamic-update-slice(f32[48,48,152]{2,1,0:T(8,128)S(1)} %get-tuple-element.505, f32[24,24,24]{2,1,0:T(8,128)S(1)} %dynamic-slice_add_fusion.4, s32[]{:T(128)S(6)} %select_n.230, s32[]{:T(128)S(6)} %select_n.231, s32[]{:T(128)S(6)} %select_n.232) | dynamic-update-slice | bytes 110596 | tf_op jit(solution)/shard_map/while/body/eval_jaxpr/dynamic_update_slice | solution.py:126
  288.9 16.8 %dynamic_update_slice.28 = f32[48,48,152]{2,1,0:T(8,128)S(1)} dynamic-update-slice(f32[48,48,152]{2,1,0:T(8,128)S(1)} %dynamic_update_slice.27, f32[24,24,24]{2,1,0:T(8,128)S(1)} %dynamic-slice_add_fusion.5, s32[]{:T(128)S(6)} %select_n.233, s32[]{:T(128)S(6)} %select_n.234, s32[]{:T(128)S(6)} %select_n.235) | dynamic-update-slice | bytes 110596 | tf_op jit(solution)/shard_map/while/body/eval_jaxpr/dynamic_update_slice | solution.py:126
  313.5 18.1 %dynamic_update_slice.27 = f32[48,48,152]{2,1,0:T(8,128)S(1)} dynamic-update-slice(f32[48,48,152]{2,1,0:T(8,128)S(1)} %get-tuple-element.505, f32[24,24,24]{2,1,0:T(8,128)S(1)} %dynamic-slice_add_fusion.4, s32[]{:T(128)S(6)} %select_n.230, s32[]{:T(128)S(6)} %select_n.231, s32[]{:T(128)S(6)} %select_n.232) | dynamic-update-slice | bytes 110596 | tf_op jit(solution)/shard_map/while/body/eval_jaxpr/dynamic_update_slice | solution.py:126
  338.2 18.9 %dynamic_update_slice.28 = f32[48,48,152]{2,1,0:T(8,128)S(1)} dynamic-update-slice(f32[48,48,152]{2,1,0:T(8,128)S(1)} %dynamic_update_slice.27, f32[24,24,24]{2,1,0:T(8,128)S(1)} %dynamic-slice_add_fusion.5, s32[]{:T(128)S(6)} %select_n.233, s32[]{:T(128)S(6)} %select_n.234, s32[]{:T(128)S(6)} %select_n.235) | dynamic-update-slice | bytes 110596 | tf_op jit(solution)/shard_map/while/body/eval_jaxpr/dynamic_update_slice | solution.py:126
  364.9 21.5 %dynamic_update_slice.27 = f32[48,48,152]{2,1,0:T(8,128)S(1)} dynamic-update-slice(f32[48,48,152]{2,1,0:T(8,128)S(1)} %get-tuple-element.505, f32[24,24,24]{2,1,0:T(8,128)S(1)} %dynamic-slice_add_fusion.4, s32[]{:T(128)S(6)} %select_n.230, s32[]{:T(128)S(6)} %select_n.231, s32[]{:T(128)S(6)} %select_n.232) | dynamic-update-slice | bytes 110596 | tf_op jit(solution)/shard_map/while/body/eval_jaxpr/dynamic_update_slice | solution.py:126
  393.0 16.8 %dynamic_update_slice.28 = f32[48,48,152]{2,1,0:T(8,128)S(1)} dynamic-update-slice(f32[48,48,152]{2,1,0:T(8,128)S(1)} %dynamic_update_slice.27, f32[24,24,24]{2,1,0:T(8,128)S(1)} %dynamic-slice_add_fusion.5, s32[]{:T(128)S(6)} %select_n.233, s32[]{:T(128)S(6)} %select_n.234, s32[]{:T(128)S(6)} %select_n.235) | dynamic-update-slice | bytes 110596 | tf_op jit(solution)/shard_map/while/body/eval_jaxpr/dynamic_update_slice | solution.py:126
  417.6 19.7 %dynamic_update_slice.27 = f32[48,48,152]{2,1,0:T(8,128)S(1)} dynamic-update-slice(f32[48,48,152]{2,1,0:T(8,128)S(1)} %get-tuple-element.505, f32[24,24,24]{2,1,0:T(8,128)S(1)} %dynamic-slice_add_fusion.4, s32[]{:T(128)S(6)} %select_n.230, s32[]{:T(128)S(6)} %select_n.231, s32[]{:T(128)S(6)} %select_n.232) | dynamic-update-slice | bytes 110596 | tf_op jit(solution)/shard_map/while/body/eval_jaxpr/dynamic_update_slice | solution.py:126
  443.9 19.7 %dynamic_update_slice.28 = f32[48,48,152]{2,1,0:T(8,128)S(1)} dynamic-update-slice(f32[48,48,152]{2,1,0:T(8,128)S(1)} %dynamic_update_slice.27, f32[24,24,24]{2,1,0:T(8,128)S(1)} %dynamic-slice_add_fusion.5, s32[]{:T(128)S(6)} %select_n.233, s32[]{:T(128)S(6)} %select_n.234, s32[]{:T(128)S(6)} %select_n.235) | dynamic-update-slice | bytes 110596 | tf_op jit(solution)/shard_map/while/body/eval_jaxpr/dynamic_update_slice | solution.py:126
  471.5 18.5 %dynamic_update_slice.27 = f32[48,48,152]{2,1,0:T(8,128)S(1)} dynamic-update-slice(f32[48,48,152]{2,1,0:T(8,128)S(1)} %get-tuple-element.505, f32[24,24,24]{2,1,0:T(8,128)S(1)} %dynamic-slice_add_fusion.4, s32[]{:T(128)S(6)} %select_n.230, s32[]{:T(128)S(6)} %select_n.231, s32[]{:T(128)S(6)} %select_n.232) | dynamic-update-slice | bytes 110596 | tf_op jit(solution)/shard_map/while/body/eval_jaxpr/dynamic_update_slice | solution.py:126
  496.5 21.5 %dynamic_update_slice.28 = f32[48,48,152]{2,1,0:T(8,128)S(1)} dynamic-update-slice(f32[48,48,152]{2,1,0:T(8,128)S(1)} %dynamic_update_slice.27, f32[24,24,24]{2,1,0:T(8,128)S(1)} %dynamic-slice_add_fusion.5, s32[]{:T(128)S(6)} %select_n.233, s32[]{:T(128)S(6)} %select_n.234, s32[]{:T(128)S(6)} %select_n.235) | dynamic-update-slice | bytes 110596 | tf_op jit(solution)/shard_map/while/body/eval_jaxpr/dynamic_update_slice | solution.py:126
  525.9 16.8 %dynamic_update_slice.27 = f32[48,48,152]{2,1,0:T(8,128)S(1)} dynamic-update-slice(f32[48,48,152]{2,1,0:T(8,128)S(1)} %get-tuple-element.505, f32[24,24,24]{2,1,0:T(8,128)S(1)} %dynamic-slice_add_fusion.4, s32[]{:T(128)S(6)} %select_n.230, s32[]{:T(128)S(6)} %select_n.231, s32[]{:T(128)S(6)} %select_n.232) | dynamic-update-slice | bytes 110596 | tf_op jit(solution)/shard_map/while/body/eval_jaxpr/dynamic_update_slice | solution.py:126
  549.2 16.8 %dynamic_update_slice.28 = f32[48,48,152]{2,1,0:T(8,128)S(1)} dynamic-update-slice(f32[48,48,152]{2,1,0:T(8,128)S(1)} %dynamic_update_slice.27, f32[24,24,24]{2,1,0:T(8,128)S(1)} %dynamic-slice_add_fusion.5, s32[]{:T(128)S(6)} %select_n.233, s32[]{:T(128)S(6)} %select_n.234, s32[]{:T(128)S(6)} %select_n.235) | dynamic-update-slice | bytes 110596 | tf_op jit(solution)/shard_map/while/body/eval_jaxpr/dynamic_update_slice | solution.py:126
  573.9 21.5 %dynamic_update_slice.27 = f32[48,48,152]{2,1,0:T(8,128)S(1)} dynamic-update-slice(f32[48,48,152]{2,1,0:T(8,128)S(1)} %get-tuple-element.505, f32[24,24,24]{2,1,0:T(8,128)S(1)} %dynamic-slice_add_fusion.4, s32[]{:T(128)S(6)} %select_n.230, s32[]{:T(128)S(6)} %select_n.231, s32[]{:T(128)S(6)} %select_n.232) | dynamic-update-slice | bytes 110596 | tf_op jit(solution)/shard_map/while/body/eval_jaxpr/dynamic_update_slice | solution.py:126
  601.9 16.8 %dynamic_update_slice.28 = f32[48,48,152]{2,1,0:T(8,128)S(1)} dynamic-update-slice(f32[48,48,152]{2,1,0:T(8,128)S(1)} %dynamic_update_slice.27, f32[24,24,24]{2,1,0:T(8,128)S(1)} %dynamic-slice_add_fusion.5, s32[]{:T(128)S(6)} %select_n.233, s32[]{:T(128)S(6)} %select_n.234, s32[]{:T(128)S(6)} %select_n.235) | dynamic-update-slice | bytes 110596 | tf_op jit(solution)/shard_map/while/body/eval_jaxpr/dynamic_update_slice | solution.py:126
  626.6 16.8 %dynamic_update_slice.27 = f32[48,48,152]{2,1,0:T(8,128)S(1)} dynamic-update-slice(f32[48,48,152]{2,1,0:T(8,128)S(1)} %get-tuple-element.505, f32[24,24,24]{2,1,0:T(8,128)S(1)} %dynamic-slice_add_fusion.4, s32[]{:T(128)S(6)} %select_n.230, s32[]{:T(128)S(6)} %select_n.231, s32[]{:T(128)S(6)} %select_n.232) | dynamic-update-slice | bytes 110596 | tf_op jit(solution)/shard_map/while/body/eval_jaxpr/dynamic_update_slice | solution.py:126
  649.9 16.8 %dynamic_update_slice.28 = f32[48,48,152]{2,1,0:T(8,128)S(1)} dynamic-update-slice(f32[48,48,152]{2,1,0:T(8,128)S(1)} %dynamic_update_slice.27, f32[24,24,24]{2,1,0:T(8,128)S(1)} %dynamic-slice_add_fusion.5, s32[]{:T(128)S(6)} %select_n.233, s32[]{:T(128)S(6)} %select_n.234, s32[]{:T(128)S(6)} %select_n.235) | dynamic-update-slice | bytes 110596 | tf_op jit(solution)/shard_map/while/body/eval_jaxpr/dynamic_update_slice | solution.py:126
  674.6 20.9 %dynamic_update_slice.27 = f32[48,48,152]{2,1,0:T(8,128)S(1)} dynamic-update-slice(f32[48,48,152]{2,1,0:T(8,128)S(1)} %get-tuple-element.505, f32[24,24,24]{2,1,0:T(8,128)S(1)} %dynamic-slice_add_fusion.4, s32[]{:T(128)S(6)} %select_n.230, s32[]{:T(128)S(6)} %select_n.231, s32[]{:T(128)S(6)} %select_n.232) | dynamic-update-slice | bytes 110596 | tf_op jit(solution)/shard_map/while/body/eval_jaxpr/dynamic_update_slice | solution.py:126
  702.0 16.8 %dynamic_update_slice.28 = f32[48,48,152]{2,1,0:T(8,128)S(1)} dynamic-update-slice(f32[48,48,152]{2,1,0:T(8,128)S(1)} %dynamic_update_slice.27, f32[24,24,24]{2,1,0:T(8,128)S(1)} %dynamic-slice_add_fusion.5, s32[]{:T(128)S(6)} %select_n.233, s32[]{:T(128)S(6)} %select_n.234, s32[]{:T(128)S(6)} %select_n.235) | dynamic-update-slice | bytes 110596 | tf_op jit(solution)/shard_map/while/body/eval_jaxpr/dynamic_update_slice | solution.py:126
  726.7 16.8 %dynamic_update_slice.27 = f32[48,48,152]{2,1,0:T(8,128)S(1)} dynamic-update-slice(f32[48,48,152]{2,1,0:T(8,128)S(1)} %get-tuple-element.505, f32[24,24,24]{2,1,0:T(8,128)S(1)} %dynamic-slice_add_fusion.4, s32[]{:T(128)S(6)} %select_n.230, s32[]{:T(128)S(6)} %select_n.231, s32[]{:T(128)S(6)} %select_n.232) | dynamic-update-slice | bytes 110596 | tf_op jit(solution)/shard_map/while/body/eval_jaxpr/dynamic_update_slice | solution.py:126
  750.0 16.8 %dynamic_update_slice.28 = f32[48,48,152]{2,1,0:T(8,128)S(1)} dynamic-update-slice(f32[48,48,152]{2,1,0:T(8,128)S(1)} %dynamic_update_slice.27, f32[24,24,24]{2,1,0:T(8,128)S(1)} %dynamic-slice_add_fusion.5, s32[]{:T(128)S(6)} %select_n.233, s32[]{:T(128)S(6)} %select_n.234, s32[]{:T(128)S(6)} %select_n.235) | dynamic-update-slice | bytes 110596 | tf_op jit(solution)/shard_map/while/body/eval_jaxpr/dynamic_update_slice | solution.py:126
  774.7 16.8 %dynamic_update_slice.27 = f32[48,48,152]{2,1,0:T(8,128)S(1)} dynamic-update-slice(f32[48,48,152]{2,1,0:T(8,128)S(1)} %get-tuple-element.505, f32[24,24,24]{2,1,0:T(8,128)S(1)} %dynamic-slice_add_fusion.4, s32[]{:T(128)S(6)} %select_n.230, s32[]{:T(128)S(6)} %select_n.231, s32[]{:T(128)S(6)} %select_n.232) | dynamic-update-slice | bytes 110596 | tf_op jit(solution)/shard_map/while/body/eval_jaxpr/dynamic_update_slice | solution.py:126
  798.0 16.8 %dynamic_update_slice.28 = f32[48,48,152]{2,1,0:T(8,128)S(1)} dynamic-update-slice(f32[48,48,152]{2,1,0:T(8,128)S(1)} %dynamic_update_slice.27, f32[24,24,24]{2,1,0:T(8,128)S(1)} %dynamic-slice_add_fusion.5, s32[]{:T(128)S(6)} %select_n.233, s32[]{:T(128)S(6)} %select_n.234, s32[]{:T(128)S(6)} %select_n.235) | dynamic-update-slice | bytes 110596 | tf_op jit(solution)/shard_map/while/body/eval_jaxpr/dynamic_update_slice | solution.py:126
  822.7 20.7 %dynamic_update_slice.27 = f32[48,48,152]{2,1,0:T(8,128)S(1)} dynamic-update-slice(f32[48,48,152]{2,1,0:T(8,128)S(1)} %get-tuple-element.505, f32[24,24,24]{2,1,0:T(8,128)S(1)} %dynamic-slice_add_fusion.4, s32[]{:T(128)S(6)} %select_n.230, s32[]{:T(128)S(6)} %select_n.231, s32[]{:T(128)S(6)} %select_n.232) | dynamic-update-slice | bytes 110596 | tf_op jit(solution)/shard_map/while/body/eval_jaxpr/dynamic_update_slice | solution.py:126
  849.9 16.8 %dynamic_update_slice.28 = f32[48,48,152]{2,1,0:T(8,128)S(1)} dynamic-update-slice(f32[48,48,152]{2,1,0:T(8,128)S(1)} %dynamic_update_slice.27, f32[24,24,24]{2,1,0:T(8,128)S(1)} %dynamic-slice_add_fusion.5, s32[]{:T(128)S(6)} %select_n.233, s32[]{:T(128)S(6)} %select_n.234, s32[]{:T(128)S(6)} %select_n.235) | dynamic-update-slice | bytes 110596 | tf_op jit(solution)/shard_map/while/body/eval_jaxpr/dynamic_update_slice | solution.py:126
  868.1 6.9 scatter-add.4
  876.1 6.2 collective-permute-start
  887.1 7.0 collective-permute-start.1
  894.2 6.7 collective-permute-done.1
  901.6 91.7 %all-reduce.2.cloned.1.call-done = bf16[24,24,128]{2,1,0:T(8,128)(2,1)} async-done(((bf16[24,24,128]{2,1,0:T(8,128)(2,1)}), bf16[24,24,128]{2,1,0:T(8,128)(2,1)}) %all-reduce.2.cloned.1.call-update) | async-done | bytes 147472 | tf_op jit(solution)/shard_map/psum | solution.py:137
  1011.4 4.8 fusion.23
  1022.4 77.4 %while.39 = (s32[]{:T(128)}, bf16[6,12288]{1,0:T(8,128)(2,1)S(1)}, f32[6,8,12288]{2,0,1:T(8,128)}, f32[8,64]{1,0:T(8,128)S(1)}, f32[64]{0:T(128)S(1)}, /*index=5...) while((s32[]{:T(128)}, bf16[6,12288]{1,0:T(8,128)(2,1)S(1)}, ...), condition=%wide.region_6.7_spmd, body=%wide.region_5.6_spmd.sunk | while | flops 696791040 | bytes 14027641 | solution.py:82
  1027.4 3.8 fusion.162
  1100.0 3.8 collective-permute-start.6
  1109.2 4.9 collective-permute-done.7
  1114.2 211.0 %while.40 = (s32[]{:T(128)}, bf16[16,2,13824]{2,1,0:T(2,128)(2,1)S(1)}, s32[16,2,3]{2,1,0:T(2,128)}, bf16[48,48,152]{2,1,0:T(8,128)(2,1)S(1)}, s32[]{:T(128)}, /*index=5*/s32[]{:T(128)}, s32[]{:T(128)}, s32[]{:T(128)}) while((s32[]{:T(128)}, bf16[16,2,13824]{2,1,0:T(2,128)(2,1)S(1)}, s32[16,2,3]{2,1,0:T(2,128)}, ...), condition=%wide.region_8.9_spmd, body=%wide.region_7.8_spmd.sunk | while | flops 110612 | bytes 387489 | solution.py:159
  1325.2 32.4 %all_to_all.15 = bf16[16,2,13824]{2,1,0:T(2,128)(2,1)S(1)} all-to-all(bf16[16,2,13824]{2,1,0:T(2,128)(2,1)S(1)} %get-tuple-element.204), channel_id=1, replica_groups=mesh['gz'=16,'gy'=8,'orb'=2] {'gz'}, dimensions={0} | all-to-all | bytes 1769472 | tf_op jit(solution)/shard_map/all_to_all | solution.py:162
  (343 shorter events, 206.3 us)
Async XLA Ops:
  10.4 16.9 %all-to-all-start = ((bf16[16,2,3]{2,1,0:T(2,128)(2,1)}), bf16[16,2,3]{2,1,0:T(2,128)(2,1)S(1)}, u32[]{:S(2)}, u32[]{:S(2)}) async-start(bf16[16,2,3]{2,1,0:T(2,128)(2,1)} %bitcast.41), calls=%async_computation | async-start | bytes 16384 | tf_op jit(solution)/shard_map/all_to_all | solution.py:111
  21.8 11.6 copy-start.18
  27.3 29.5 %all-to-all-start.1 = ((bf16[16,2,13824]{2,1,0:T(2,128)(2,1)}), bf16[16,2,13824]{2,1,0:T(2,128)(2,1)}, u32[]{:S(2)}, u32[]{:S(2)}) async-start(bf16[16,2,13824]{2,1,0:T(2,128)(2,1)} %reshape.511), calls=%async_computation.1 | async-start | bytes 1769472 | tf_op jit(solution)/shard_map/all_to_all | solution.py:108
  32.0 961.3 %all-reduce.2.cloned.1.call-start = ((), (), s32[]{:S(2)}) async-start(), calls=%async_computation.3 | async-start | bytes 294912 | tf_op jit(solution)/shard_map/psum | solution.py:137
  37.5 19.6 %copy-start.15 = (s32[16,2,3]{2,1,0:T(2,128)}, s32[16,2,3]{2,1,0:T(2,128)S(1)}, u32[]{:S(2)}) copy-start(s32[16,2,3]{2,1,0:T(2,128)S(1)} %convert_convert_fusion) | copy-start | bytes 1156
  868.0 140.1 %copy-start.2 = (f32[128,128]{1,0:T(8,128)S(1)}, f32[128,128]{1,0:T(8,128)}, u32[]{:S(2)}) copy-start(f32[128,128]{1,0:T(8,128)} %compare_convert_fusion.12) | copy-start | bytes 196612
  868.0 140.1 %copy-start.3 = (f32[128,128]{1,0:T(8,128)S(1)}, f32[128,128]{1,0:T(8,128)}, u32[]{:S(2)}) copy-start(f32[128,128]{1,0:T(8,128)} %get-tuple-element.335) | copy-start | bytes 196612
  868.0 140.1 %copy-start.4 = (f32[128,128]{1,0:T(8,128)S(1)}, f32[128,128]{1,0:T(8,128)}, u32[]{:S(2)}) copy-start(f32[128,128]{1,0:T(8,128)} %get-tuple-element.336) | copy-start | bytes 196612
  868.0 140.1 %copy-start.5 = (f32[128,128]{1,0:T(8,128)S(1)}, f32[128,128]{1,0:T(8,128)}, u32[]{:S(2)}) copy-start(f32[128,128]{1,0:T(8,128)} %get-tuple-element.337) | copy-start | bytes 196612
  868.0 140.1 %copy-start.6 = (f32[128,128]{1,0:T(8,128)S(1)}, f32[128,128]{1,0:T(8,128)}, u32[]{:S(2)}) copy-start(f32[128,128]{1,0:T(8,128)} %get-tuple-element.338) | copy-start | bytes 196612
  868.0 140.1 %copy-start.7 = (f32[128,128]{1,0:T(8,128)S(1)}, f32[128,128]{1,0:T(8,128)}, u32[]{:S(2)}) copy-start(f32[128,128]{1,0:T(8,128)} %get-tuple-element.339) | copy-start | bytes 196612
  868.1 140.1 %copy-start.8 = (f32[128,128]{1,0:T(8,128)S(1)}, f32[128,128]{1,0:T(8,128)}, u32[]{:S(2)}) copy-start(f32[128,128]{1,0:T(8,128)} %get-tuple-element.340) | copy-start | bytes 196612
  868.1 140.1 %copy-start.9 = (f32[128,128]{1,0:T(8,128)S(1)}, f32[128,128]{1,0:T(8,128)}, u32[]{:S(2)}) copy-start(f32[128,128]{1,0:T(8,128)} %get-tuple-element.341) | copy-start | bytes 196612
  868.1 140.1 %copy-start.10 = (f32[128,128]{1,0:T(8,128)S(1)}, f32[128,128]{1,0:T(8,128)}, u32[]{:S(2)}) copy-start(f32[128,128]{1,0:T(8,128)} %get-tuple-element.342) | copy-start | bytes 196612
  876.1 9.8 collective-permute-start
  887.1 13.8 %collective-permute-start.1 = (bf16[24,24,128]{2,1,0:T(8,128)(2,1)S(1)}, bf16[24,24,128]{2,1,0:T(8,128)(2,1)S(1)}, u32[]{:S(2)}, u32[]{:S(2)}) collective-permute-start(bf16[24,24,128]{2,1,0:T(8,128)(2,1)S(1)} %slice.271), channel_id=1, source_target_pairs={{0,2},{2,4},{4,6},{6,8},{8,10},{10,12},{12,14},{14,0},{1,3},{3,5},... | collective-permute-start | bytes 442376 | tf_op jit(solution)/shard_map/ppermute | solution.py:21
  994.1 3.3 collective-permute-start.2
  996.4 3.4 collective-permute-start.3
  999.9 6.9 collective-permute-start.4
  1002.3 5.8 collective-permute-start.5
  1008.2 3.2 copy-start.11
  1008.2 3.2 copy-start.12
  1008.2 3.2 copy-start.13
  1020.1 2.2 copy-start.14
  1020.1 2.2 copy-start.16
  1020.1 2.2 copy-start.17
  1020.1 2.2 copy-start.19
  1020.1 2.2 copy-start.20
  1100.0 14.2 %copy-start.1 = (bf16[24,24,128]{2,1,0:T(8,128)(2,1)}, bf16[24,24,128]{2,1,0:T(8,128)(2,1)S(1)}, u32[]{:S(2)}) copy-start(bf16[24,24,128]{2,1,0:T(8,128)(2,1)S(1)} %convert_element_type.308) | copy-start | bytes 442372
  1100.0 5.9 collective-permute-start.6
  1105.9 8.2 collective-permute-start.7
  1325.2 33.5 %copy-start = (bf16[16,24,576]{2,1,0:T(8,128)(2,1)S(1)}, bf16[16,24,576]{2,1,0:T(8,128)(2,1)}, u32[]{:S(2)}) copy-start(bf16[16,24,576]{2,1,0:T(8,128)(2,1)} %param.26) | copy-start | bytes 1327108
Sparse Core Ops, SparseCore 0:
  901.7 91.5 all-reduce.1
where the time goes:
time: 1370 us
  local copies, waits for them, and re-layouts  669 us (49%)
  loops' own time  365 us (27%)
  waiting for transfers between devices  136 us (10%)
  matrix products  65.3 us (5%)
  starting transfers between devices  42.5 us (3%)
  other arithmetic  42 us (3%)
  blocking collectives  32.4 us (2%)
  between operations  14.5 us (1%)
    dynamic_update_slice x32, local copies, waits for them, and re-layouts, deposit(): grid = lax.dynamic_update_slice(grid, region + piece, start)  579 us
    another operation x1, loops' own time, local(): lax.fori_loop(0, slab_count, deposit, jnp.zeros((CZ + BOX, CY + BOX, NX +...  189 us
    another operation x1, loops' own time, local(): windows = lax.map(cut, offsets)  176 us
    psum x1, waiting for transfers between devices, local(): density = lax.psum(tile.astype(jnp.bfloat16), 'orb').astype(jnp.float32)  91.7 us
    all_to_all x1, blocking collectives, local(): lax.all_to_all(for_sending(windows), 'gz', split_axis=0, concat_axis=0, t...  32.4 us
  transfers between devices with their start and end apart: 11, of which 11 were waited for; matrix products, arithmetic and copies ran while one was open for 1% of the time, Pallas kernels for 0%

commit v1 on v0

v1 whole, which is shorter than its diff:
```python
import jax
import jax.numpy as jnp
from jax import lax
from jax.experimental import pallas as pl
from jax.experimental.pallas import tpu as pltpu
from jax.sharding import PartitionSpec as P

BOX = 24
CHAN = 8
HID = 64
RAD = 6
CZ = 24
CY = 24
NX = 128
CAP = 2
SLABS = 16
HELD = 16
HALO = 8
PLANES = CZ + 2 * HALO
HALF = CY // 2
ROWS = HALF + 2 * RAD
REACH = CY + RAD
MAIN = 96
TAIL = CAP * MAIN
BLOCK_ROWS = 224
WINDOW_ROWS = TAIL + BOX

VMEM = pl.BlockSpec(memory_space=pltpu.VMEM)
SMEM = pl.BlockSpec(memory_space=pltpu.SMEM)
f32 = jnp.float32
bf16 = jnp.bfloat16


def shifted(x, axis, by):
    count = lax.axis_size(axis)
    return lax.ppermute(x, axis, [(i, (i + by) % count) for i in range(count)])


def from_next_other(x):
    tiles, owners = lax.axis_size("gy"), lax.axis_size("orb")
    pairs = [
        ((tile + 1) % tiles * owners + (orb + 1) % owners, tile * owners + orb)
        for tile in range(tiles)
        for orb in range(owners)
    ]
    return lax.ppermute(x, ("gy", "orb"), pairs)


def split(x):
    high = x.astype(bf16)
    return high, (x - high.astype(f32)).astype(bf16)


def split_table(x):
    high = lax.reduce_precision(x, 8, 7)
    return high.astype(bf16), (x - high).astype(bf16)


def lanes(rows):
    return lax.broadcasted_iota(jnp.int32, (rows, NX), 1)


def pack_body(corners, occupation, orbitals, sent, count):
    sent[...] = jnp.zeros(sent.shape, bf16)

    def clear(slab, carry):
        count[slab] = 0
        return carry

    lax.fori_loop(0, SLABS, clear, 0)
    side = lanes(32) // 64
    field = lanes(8) % 64

    def place(i, carry):
        plane = corners[i, 0]
        row = corners[i, 1]
        column = corners[i, 2]
        slab = lax.div(plane, CZ)
        rank = count[slab]
        count[slab] = rank + 1
        values = orbitals[i].astype(f32)
        density = occupation[i] * values * values
        main = jnp.concatenate([density[:, 128 * j : 128 * j + 128] for j in range(4)], axis=0)
        sent[slab, pl.ds(pl.multiple_of(rank * MAIN, 32), MAIN), :] = main.astype(bf16)
        last = density[:, 512:576]
        tail = jnp.concatenate([last, last], axis=1)
        offsets = jnp.where(
            field == 0,
            lax.rem(plane, CZ),
            jnp.where(field == 1, lax.rem(row, CY), jnp.where(field == 2, column, 0)),
        ).astype(f32)
        fresh = jnp.concatenate([tail, offsets], axis=0)
        held = sent[slab, TAIL:BLOCK_ROWS, :].astype(f32)
        sent[slab, TAIL:BLOCK_ROWS, :] = jnp.where(side == rank, fresh, held).astype(bf16)
        return carry

    lax.fori_loop(0, HELD, place, 0)


def pack(corners, occupation, orbitals):
    return pl.pallas_call(
        pack_body,
        name="pack_boxes",
        out_shape=jax.ShapeDtypeStruct((SLABS, BLOCK_ROWS, NX), bf16),
        in_specs=[SMEM, SMEM, VMEM],
        out_specs=VMEM,
        scratch_shapes=[pltpu.SMEM((SLABS,), jnp.int32)],
    )(corners, occupation, orbitals)


def read_offsets(received, rows, offsets, sem):
    for source in range(SLABS):
        rows[source : source + 1, :] = (
            received[source, 208:BLOCK_ROWS, :].astype(f32)[8:9].astype(jnp.int32)
        )
    copy = pltpu.make_async_copy(rows, offsets, sem)
    copy.start()
    return copy


def deposit_body(received, own, next_up, second_up, next_down, offsets_out, grid, rows, offsets, sem):
    copy = read_offsets(received, rows, offsets, sem)
    offsets_out[...] = rows[...]
    grid[...] = jnp.zeros(grid.shape, f32)
    copy.wait()
    lane = lanes(BOX)

    def source_step(source, carry):
        tail_both = received[source, TAIL:BLOCK_ROWS, :].astype(f32)[:BOX]
        for slot in range(CAP):
            z0 = offsets[source, 64 * slot]
            y0 = offsets[source, 64 * slot + 1]
            x0 = offsets[source, 64 * slot + 2]
            main = received[source, MAIN * slot : MAIN * slot + MAIN, :].astype(f32)
            tiles = [main[BOX * j : BOX * j + BOX] for j in range(4)]
            tiles.append(tail_both if slot == 0 else pltpu.roll(tail_both, 64, 1))
            inside = ((lane - x0) & (NX - 1)) < BOX
            for first in range(0, BOX, 8):
                olds = [
                    grid[y0 + b, pl.ds(z0, BOX), :] for b in range(first, first + 8)
                ]
                news = []
                for k in range(8):
                    b = first + k
                    tile, left = divmod(BOX * b, NX)
                    piece = tiles[tile]
                    if left + BOX > NX:
                        piece = jnp.where(lane >= left, piece, tiles[tile + 1])
                    piece = pltpu.roll(piece, (x0 - left) & (NX - 1), 1)
                    news.append(olds[k] + jnp.where(inside, piece, 0.0))
                for k in range(8):
                    grid[y0 + first + k, pl.ds(z0, BOX), :] = news[k]
        return carry

    lax.fori_loop(0, SLABS, source_step, 0)
    own[...] = grid[:, : PLANES - HALO, :]
    next_up[...] = grid[:, CZ - HALO :, :].astype(bf16)
    second_up[...] = grid[:, 2 * CZ - HALO :, :].astype(bf16)
    next_down[...] = grid[:, :HALO, :].astype(bf16)


def deposit(received):
    return pl.pallas_call(
        deposit_body,
        name="deposit_boxes",
        out_shape=(
            jax.ShapeDtypeStruct((CY + BOX, PLANES - HALO, NX), f32),
            jax.ShapeDtypeStruct((CY + BOX, PLANES - HALO, NX), bf16),
            jax.ShapeDtypeStruct((CY + BOX, HALO, NX), bf16),
            jax.ShapeDtypeStruct((CY + BOX, HALO, NX), bf16),
            jax.ShapeDtypeStruct((SLABS, NX), jnp.int32),
        ),
        in_specs=[VMEM],
        out_specs=(VMEM,) * 5,
        scratch_shapes=[
            pltpu.VMEM((CY + BOX, CZ + BOX, NX), f32),
            pltpu.VMEM((SLABS, NX), jnp.int32),
            pltpu.SMEM((SLABS, NX), jnp.int32),
            pltpu.SemaphoreType.DMA,
        ],
    )(received)


def fold_planes_body(own, below, second_below, above, kept, next_right, second_right, next_left):
    for first, last in ((0, HALO), (HALO, PLANES - HALO), (PLANES - HALO, PLANES)):
        total = None
        parts = []
        if last > HALO:
            parts.append(own[:, first - HALO : last - HALO, :])
        if last <= PLANES - HALO:
            parts.append(below[:, first:last, :].astype(f32))
        if last == HALO:
            parts.append(second_below[...].astype(f32))
        if first == PLANES - HALO:
            parts.append(above[...].astype(f32))
        total = parts[0]
        for part in parts[1:]:
            total = total + part
        kept[:, first:last, :] = total[:REACH]
        next_right[:, first:last, :] = total[CY - RAD :].astype(bf16)
        second_right[:, first:last, :] = total[2 * CY - RAD :].astype(bf16)
        next_left[:, first:last, :] = total[:RAD].astype(bf16)


def fold_planes(own, below, second_below, above):
    return pl.pallas_call(
        fold_planes_body,
        name="fold_planes",
        out_shape=(
            jax.ShapeDtypeStruct((REACH, PLANES, NX), f32),
            jax.ShapeDtypeStruct((REACH, PLANES, NX), bf16),
            jax.ShapeDtypeStruct((RAD, PLANES, NX), bf16),
            jax.ShapeDtypeStruct((RAD, PLANES, NX), bf16),
        ),
        in_specs=[VMEM] * 4,
        out_specs=(VMEM,) * 4,
    )(own, below, second_below, above)


def fold_rows_body(position, own, left, second_left, right, kept, given, total):
    for first, last in ((0, RAD), (RAD, REACH), (REACH, REACH + RAD)):
        parts = []
        if last > RAD:
            parts.append(own[first - RAD : last - RAD])
        if last <= REACH:
            parts.append(left[first:last].astype(f32))
        if last == RAD:
            parts.append(second_left[...].astype(f32))
        if first == REACH:
            parts.append(right[...].astype(f32))
        row_total = parts[0]
        for part in parts[1:]:
            row_total = row_total + part
        total[first:last] = row_total
    orb = position[0]
    kept[...] = total[pl.ds(HALF * orb, ROWS)]
    given[...] = total[pl.ds(HALF * (1 - orb), ROWS)].astype(bf16)


def fold_rows(position, own, left, second_left, right):
    return pl.pallas_call(
        fold_rows_body,
        name="fold_rows",
        out_shape=(
            jax.ShapeDtypeStruct((ROWS, PLANES, NX), f32),
            jax.ShapeDtypeStruct((ROWS, PLANES, NX), bf16),
        ),
        in_specs=[SMEM] + [VMEM] * 4,
        out_specs=(VMEM, VMEM),
        scratch_shapes=[pltpu.VMEM((REACH + RAD, PLANES, NX), f32)],
    )(position, own, left, second_left, right)


def model_body(
    taps,
    kept,
    other,
    plane_table,
    column_table,
    first_table,
    middle_table,
    middle_bias,
    last_weight,
    last_bias,
    potential,
    planes,
    features,
    result,
):
    def plane_step(pair, carry):
        density = kept[pl.ds(2 * pair, 2)] + other[pl.ds(2 * pair, 2)].astype(f32)
        density = density.astype(bf16)
        field = jnp.concatenate([density[0], density[1]], axis=1)
        both = jnp.dot(plane_table[...], field, preferred_element_type=f32)
        total = both[: CHAN * CZ] + both[CHAN * CZ :]
        planes[2 * pair] = total[:, :NX]
        planes[2 * pair + 1] = total[:, NX:]
        return carry

    lax.fori_loop(0, ROWS // 2, plane_step, 0, unroll=2)

    def channel_step(channel, carry):
        weights = [taps[channel, step] for step in range(RAD + 1)]
        lines = []
        for part in range(CZ // 8):
            start = pl.multiple_of(channel * CZ + 8 * part, 8)
            rows = [planes[y, pl.ds(start, 8), :] for y in range(ROWS)]
            for y in range(HALF):
                total = weights[RAD] * rows[y + RAD]
                for step in range(RAD):
                    total = total + weights[step] * (rows[y + step] + rows[y + 2 * RAD - step])
                lines.append(total)
        high, low = split(jnp.concatenate(lines, axis=0))
        both = jnp.dot(
            jnp.concatenate([high, low], axis=1), column_table[channel], preferred_element_type=f32
        )
        smooth = both[:, :NX] + both[:, NX:]
        features[channel] = jnp.log(1.0 + smooth)
        return carry

    lax.fori_loop(0, CHAN, channel_step, 0)

    def cell_step(step, carry):
        start = pl.multiple_of(step * 16, 16)
        inputs = [features[channel, pl.ds(start, 16), :] for channel in range(CHAN)]
        cells = jnp.concatenate(
            [
                jnp.concatenate([piece[:8] for piece in inputs], axis=0),
                jnp.concatenate([piece[8:] for piece in inputs], axis=0),
            ],
            axis=1,
        )
        high, low = split(cells)
        ones = jnp.ones((16, 2 * NX), bf16)
        stacked = jnp.concatenate([high, low, high, ones], axis=0)
        values = []
        for half in range(2):
            hidden = jnp.dot(
                first_table[256 * half : 256 * half + 256, :], stacked, preferred_element_type=f32
            )
            hidden = hidden + hidden * jnp.tanh(hidden)
            hidden_high, hidden_low = split(hidden)
            for pair in range(2):
                rows = slice(128 * pair, 128 * pair + 128)
                both = jnp.dot(
                    middle_table[...],
                    jnp.concatenate([hidden_high[rows], hidden_low[rows]], axis=0),
                    preferred_element_type=f32,
                )
                mixed = both[:128] + both[128:] + middle_bias[...]
                mixed = (mixed + mixed * jnp.tanh(mixed)) * last_weight[...]
                values.append(jnp.sum(mixed.reshape(2, HID, 2 * NX), axis=1))
        value = jnp.concatenate(values, axis=0) + last_bias[0]
        result[pl.ds(start, 8), :] = value[:, :NX]
        result[pl.ds(start + 8, 8), :] = value[:, NX:]
        return carry

    lax.fori_loop(0, CZ * HALF // 16, cell_step, 0, unroll=3)
    for part in range(CZ // 8):
        block = result[HALF * 8 * part : HALF * 8 * (part + 1), :]
        planes[:HALF, 8 * part : 8 * part + 8, :] = block.reshape(HALF, 8, NX)
    potential[...] = planes[:HALF, :CZ, :].astype(bf16)


def model(kept, other, taps, tables):
    return pl.pallas_call(
        model_body,
        name="smooth_and_network",
        out_shape=jax.ShapeDtypeStruct((HALF, CZ, NX), bf16),
        in_specs=[SMEM] + [VMEM] * 8 + [SMEM],
        out_specs=VMEM,
        scratch_shapes=[
            pltpu.VMEM((ROWS, CHAN * CZ, NX), f32),
            pltpu.VMEM((CHAN, HALF * CZ, NX), f32),
            pltpu.VMEM((HALF * CZ, NX), f32),
        ],
        compiler_params=pltpu.CompilerParams(vmem_limit_bytes=48 * 1024 * 1024),
    )(taps, kept, other, *tables)


def kernel_taps(kernel_widths):
    offsets = jnp.arange(-RAD, RAD + 1).astype(f32)
    raw = jnp.exp(-(offsets[None, :] ** 2) / (2.0 * kernel_widths[:, None] ** 2))
    return raw / jnp.sum(raw, axis=1, keepdims=True)


def tap_table(taps, distance):
    table = jnp.zeros((taps.shape[0],) + distance.shape, f32)
    for step in range(2 * RAD + 1):
        table = table + taps[:, step][:, None, None] * (distance == step).astype(f32)[None]
    return table


def model_tables(taps, w_in, b_in, w_mid, b_mid, w_out, b_out):
    out_index = jnp.arange(CZ, dtype=jnp.int32)
    in_index = jnp.arange(PLANES, dtype=jnp.int32) - (HALO - RAD)
    plane = tap_table(taps, in_index[None, :] - out_index[:, None]).reshape(CHAN * CZ, PLANES)
    plane_table = jnp.concatenate(split_table(plane), axis=0)
    source = jnp.arange(NX, dtype=jnp.int32)
    column = tap_table(taps, (source[:, None] - source[None, :] + RAD) % NX)
    column_high, column_low = split_table(column)
    column_table = jnp.concatenate(
        [
            jnp.concatenate([column_high, column_low], axis=2),
            jnp.concatenate([column_high, jnp.zeros_like(column_low)], axis=2),
        ],
        axis=1,
    )
    eight = jnp.eye(8, dtype=f32)
    first = (0.5 * w_in.T)[None, :, :, None] * eight[:, None, None, :]
    first_high, first_low = split_table(first.reshape(8 * HID, CHAN * 8))
    bias_high, bias_low = split_table(jnp.tile(0.5 * b_in, 8)[:, None])
    first_table = jnp.concatenate(
        [
            first_high,
            first_high,
            first_low,
            bias_high,
            bias_low,
            jnp.zeros((8 * HID, 14), bf16),
        ],
        axis=1,
    )
    two = jnp.eye(2, dtype=f32)
    middle = (two[:, None, :, None] * (0.5 * w_mid.T)[None, :, None, :]).reshape(2 * HID, 2 * HID)
    middle_high, middle_low = split_table(middle)
    middle_table = jnp.concatenate(
        [
            jnp.concatenate([middle_high, middle_high], axis=1),
            jnp.concatenate([middle_low, jnp.zeros_like(middle_low)], axis=1),
        ],
        axis=0,
    )
    middle_bias = jnp.broadcast_to(jnp.tile(0.5 * b_mid, 2)[:, None], (2 * HID, 2 * NX))
    last_weight = jnp.broadcast_to(jnp.tile(w_out, 2)[:, None], (2 * HID, 2 * NX))
    return (
        plane_table,
        column_table,
        first_table,
        middle_table,
        middle_bias,
        last_weight,
        b_out,
    )


def widen_body(position, own, partner, next_same, next_other, wide):
    orb = position[0]
    wide[pl.ds(HALF * orb, HALF)] = own[...]
    wide[pl.ds(HALF * (1 - orb), HALF)] = partner[...]
    wide[pl.ds(CY + HALF * orb, HALF)] = next_same[...]
    wide[pl.ds(CY + HALF * (1 - orb), HALF)] = next_other[...]


def widen(position, own, partner, next_same, next_other):
    return pl.pallas_call(
        widen_body,
        name="widen_rows",
        out_shape=jax.ShapeDtypeStruct((CY + BOX, CZ, NX), bf16),
        in_specs=[SMEM] + [VMEM] * 4,
        out_specs=VMEM,
    )(position, own, partner, next_same, next_other)


def cut_body(offsets, wide, beyond, windows, reach):
    reach[:, :CZ, :] = wide[...].astype(f32)
    reach[:, CZ:, :] = beyond[...].astype(f32)
    lane = lanes(BOX)

    def source_step(source, carry):
        mains, tails = [], []
        for slot in range(CAP):
            z0 = offsets[source, 64 * slot]
            y0 = offsets[source, 64 * slot + 1]
            x0 = offsets[source, 64 * slot + 2]
            tiles = [None] * 5
            for b in range(BOX):
                tile, left = divmod(BOX * b, NX)
                piece = reach[y0 + b, pl.ds(z0, BOX), :]
                piece = pltpu.roll(piece, (left - x0) & (NX - 1), 1)
                if tiles[tile] is None:
                    tiles[tile] = piece
                else:
                    tiles[tile] = jnp.where(lane >= left, piece, tiles[tile])
                if left + BOX > NX:
                    tiles[tile + 1] = piece
            mains += tiles[:4]
            tails.append(tiles[4])
        tail = jnp.where(lane < 64, tails[0], pltpu.roll(tails[1], 64, 1))
        windows[source] = jnp.concatenate(mains + [tail], axis=0).astype(bf16)
        return carry

    lax.fori_loop(0, SLABS, source_step, 0)


def cut(offsets, wide, beyond):
    return pl.pallas_call(
        cut_body,
        name="cut_windows",
        out_shape=jax.ShapeDtypeStruct((SLABS, WINDOW_ROWS, NX), bf16),
        in_specs=[SMEM, VMEM, VMEM],
        out_specs=VMEM,
        scratch_shapes=[pltpu.VMEM((CY + BOX, CZ + BOX, NX), f32)],
    )(offsets, wide, beyond)


def apply_body(corners, windows, orbitals, applied, count):
    def clear(slab, carry):
        count[slab] = 0
        return carry

    lax.fori_loop(0, SLABS, clear, 0)

    def place(i, carry):
        slab = lax.div(corners[i, 0], CZ)
        rank = count[slab]
        count[slab] = rank + 1
        main = windows[slab, pl.ds(pl.multiple_of(rank * MAIN, 32), MAIN), :].astype(f32)
        tail = windows[slab, TAIL:WINDOW_ROWS, :].astype(f32)
        tail = jnp.where(rank == 0, tail[:, :64], tail[:, 64:])
        whole = jnp.concatenate([main[BOX * j : BOX * j + BOX] for j in range(4)] + [tail], axis=1)
        applied[i] = (whole * orbitals[i].astype(f32)).astype(bf16)
        return carry

    lax.fori_loop(0, HELD, place, 0)


def apply(corners, windows, orbitals):
    return pl.pallas_call(
        apply_body,
        name="apply_windows",
        out_shape=jax.ShapeDtypeStruct(orbitals.shape, bf16),
        in_specs=[SMEM, VMEM, VMEM],
        out_specs=VMEM,
        scratch_shapes=[pltpu.SMEM((SLABS,), jnp.int32)],
    )(corners, windows, orbitals)


def exchange(x, axis):
    return lax.all_to_all(x, axis, split_axis=0, concat_axis=0, tiled=True)


def local(orbitals, occupation, corners, kernel_widths, w_in, b_in, w_mid, b_mid, w_out, b_out):
    taps = kernel_taps(kernel_widths)
    tables = model_tables(taps, w_in, b_in, w_mid, b_mid, w_out, b_out)
    received = exchange(pack(corners, occupation, orbitals), "gz")
    position = lax.axis_index("orb").reshape(1)
    own, next_up, second_up, next_down, offsets = deposit(received)
    below = shifted(next_up, "gz", 1)
    second_below = shifted(second_up, "gz", 2)
    above = shifted(next_down, "gz", -1)
    kept, next_right, second_right, next_left = fold_planes(own, below, second_below, above)
    left = shifted(next_right, "gy", 1)
    second_left = shifted(second_right, "gy", 2)
    right = shifted(next_left, "gy", -1)
    kept, given = fold_rows(position, kept, left, second_left, right)
    half = model(kept, shifted(given, "orb", 1), taps, tables)
    partner = shifted(half, "orb", 1)
    next_same = shifted(half, "gy", -1)
    next_other = from_next_other(half)
    wide = widen(position, half, partner, next_same, next_other)
    windows = cut(offsets, wide, shifted(wide, "gz", -1))
    applied = apply(corners, exchange(windows, "gz"), orbitals)
    return jnp.transpose(wide[:CY], (1, 0, 2)), applied


def solution(mesh):
    return jax.shard_map(
        local,
        mesh=mesh,
        in_specs=(
            P(("gz", "gy", "orb"), None, None),
            P(("gz", "gy", "orb")),
            P(("gz", "gy", "orb"), None),
            P(),
            P(),
            P(),
            P(),
            P(),
            P(),
            P(),
        ),
        out_specs=(P("gz", "gy", None), P(("gz", "gy", "orb"), None, None)),
        check_vma=False,
    )
```

time: 1370 us -> 158 us (0.12)
  local copies, waits for them, and re-layouts: 669 us -> 11 us
  loops' own time: 365 us -> 0 us
  matrix products: 65.3 us -> 0 us
  waiting for transfers between devices: 136 us -> 72.7 us
  other arithmetic: 42 us -> 2.19 us
  Pallas kernels: 0 us -> 39.3 us
  blocking collectives: 32.4 us -> 0 us
    dynamic_update_slice x38 -> x0, local copies, waits for them, and re-layouts: 586 us -> none  [the longest x32 579 us: deposit(): grid = lax.dynamic_update_slice(grid, region + piece, start)]
    another operation x3 -> x0, loops' own time: 365 us -> none  [the longest x1 189 us: local(): lax.fori_loop(0, slab_count, deposit, jnp.zeros((CZ + BOX, CY + BOX, NX +...]
    psum x1 -> x0, waiting for transfers between devices: 91.7 us -> none  [local(): density = lax.psum(tile.astype(jnp.bfloat16), 'orb').astype(jnp.float32)]
    dot_general x24 -> x0, matrix products: 65.3 us -> none  [the longest x6 22.7 us: layer_stack(): jnp.dot(w_mid.T, hidden, precision=exact_mode) + b_mid[:, None]]
    pallas_call x0 -> x8, Pallas kernels: none -> 39.3 us  [the longest x1 14.7 us: model(): pl.pallas_call(model_body, name='smooth_and_network', out_shape=jax.Shape...]
    all_to_all x1 -> x0, blocking collectives: 32.4 us -> none  [local(): lax.all_to_all(for_sending(windows), 'gz', split_axis=0, concat_axis=0, t...]
    dynamic_slice x38 -> x0, local copies, waits for them, and re-layouts: 30.3 us -> none  [the longest x6 13.8 us: network(): return lax.map(layer_stack, blocks).reshape(count)]
    convert_element_type x33 -> x17, other arithmetic: 25.9 us -> 1.56 us  [the longest x7 1.21 us: split_table(): return (high.astype(bf16), (x - high).astype(bf16))]
  transfers between devices with their start and end apart: 11 -> 13, of which waited for: 11 -> 7; matrix products, arithmetic and copies ran while one was open for 1% -> 4% of each run, Pallas kernels for 0% -> 0%
where the time goes in v1:
time: 158 us
  waiting for transfers between devices  72.7 us (46%)
  Pallas kernels  39.3 us (25%)
  starting transfers between devices  30.8 us (19%)
  local copies, waits for them, and re-layouts  11 us (7%)
  other arithmetic  2.19 us (1%)
  between operations  1.75 us (1%)
    all_to_all x2, waiting for transfers between devices, exchange(): return lax.all_to_all(x, axis, split_axis=0, concat_axis=0, tiled=True)  43.7 us
    ppermute x10, waiting for transfers between devices, shifted(): return lax.ppermute(x, axis, [(i, (i + by) % count) for i in range(count)])  26 us
    all_to_all x2, starting transfers between devices, exchange(): return lax.all_to_all(x, axis, split_axis=0, concat_axis=0, tiled=True)  15.1 us
    pallas_call x1, Pallas kernels, model(): pl.pallas_call(model_body, name='smooth_and_network', out_shape=jax.Shape...  14.7 us
    ppermute x10, starting transfers between devices, shifted(): return lax.ppermute(x, axis, [(i, (i + by) % count) for i in range(count)])  14.2 us
    unnamed x44, local copies, waits for them, and re-layouts  6.84 us
    pallas_call x1, Pallas kernels, deposit(): pl.pallas_call(deposit_body, name='deposit_boxes', out_shape=(jax.ShapeDt...  6.3 us
    pallas_call x1, Pallas kernels, cut(): pl.pallas_call(cut_body, name='cut_windows', out_shape=jax.ShapeDtypeStru...  5.19 us
  transfers between devices with their start and end apart: 13, of which 7 were waited for; matrix products, arithmetic and copies ran while one was open for 4% of the time, Pallas kernels for 0%

profile of v1, /device:TPU:1, one launch (start us, length us, event | category | flops | bytes accessed | tf_op | source)
XLA Modules:
  0.0 157.7 jit_solution(16124878763029335347)
XLA Ops:
  0.6 1.4 copy.53.corners
  2.0 3.4 %pack_boxes.1 = bf16[16,224,128]{2,1,0:T(8,128)(2,1)} custom-call(s32[16,3]{1,0:T(8,128)} %copy.53.corners, f32[16]{0:T(128)} %occupation.1, bf16[16,24,576]{2,1,0:T(8,128)(2,1)} %orbitals.3), custom_call_target="tpu_custom_call" | custom-call | tf_op jit(solution)/shard_map/pack_boxes/pallas_call | solution.py:101
  5.4 10.1 %all-to-all-start = ((bf16[16,224,128]{2,1,0:T(8,128)(2,1)}), bf16[16,224,128]{2,1,0:T(8,128)(2,1)S(1)}, u32[]{:S(2)}, u32[]{:S(2)}) async-start(bf16[16,224,128]{2,1,0:T(8,128)(2,1)} %pack_boxes.1), calls=%async_computation | async-start | bytes 1835008 | tf_op jit(solution)/shard_map/all_to_all | solution.py:520
  15.8 0.2 fusion.48
  16.1 0.4 slice_reduce_fusion.12
  16.7 0.1 mul.654
  16.8 0.1 copy.55
  16.9 0.1 copy.57
  19.1 0.2 copy.54
  19.2 0.1 copy.58
  19.5 0.4 reduce-precision_convert_fusion.1
  20.3 0.7 fusion.2
  21.0 19.8 %all-to-all-done.received = bf16[16,224,128]{2,1,0:T(8,128)(2,1)S(1)} async-done(((bf16[16,224,128]{2,1,0:T(8,128)(2,1)}), bf16[16,224,128]{2,1,0:T(8,128)(2,1)S(1)}, u32[]{:S(2)}, u32[]{:S(2)}) %all-to-all-start) | async-done | bytes 917536 | tf_op jit(solution)/shard_map/all_to_all | solution.py:520
  40.9 1.0 copy-done.2
  41.8 6.3 %deposit_boxes.1 = (f32[48,32,128]{2,1,0:T(8,128)}, bf16[48,32,128]{2,1,0:T(8,128)(2,1)}, bf16[48,8,128]{2,1,0:T(8,128)(2,1)}, bf16[48,8,128]{2,1,0:T(8,128)(2,1)}, s32[16,128]{1,0:T(8,128)}) custom-call(bf16[16,224,128]{2,1,0:T(8,128)(2,1)} %copy-done.2), custom_call_target="tpu_custom_call" | custom-call | tf_op jit(solution)/shard_map/deposit_boxes/pallas_call | solution.py:163
  48.3 0.5 collective-permute-start.2
  48.8 0.2 copy.59
  49.0 0.1 mul.662
  50.0 0.3 concatenate.28.first_table
  50.3 6.4 %collective-permute-done.1.second_below = bf16[48,8,128]{2,1,0:T(8,128)(2,1)S(1)} collective-permute-done((bf16[48,8,128]{2,1,0:T(8,128)(2,1)}, bf16[48,8,128]{2,1,0:T(8,128)(2,1)S(1)}, u32[]{:S(2)}, u32[]{:S(2)}) %collective-permute-start.1) | collective-permute-done | bytes 98336 | tf_op jit(solution)/shard_map/ppermute | solution.py:36
  56.7 0.6 copy-done.8
  57.3 0.1 copy-done.5
  57.4 2.3 %fold_planes.1 = (f32[30,40,128]{2,1,0:T(8,128)}, bf16[30,40,128]{2,1,0:T(8,128)(2,1)}, bf16[6,40,128]{2,1,0:T(8,128)(2,1)}, bf16[6,40,128]{2,1,0:T(8,128)(2,1)}) custom-call(f32[48,32,128]{2,1,0:T(8,128)} %get-tuple-element.13.own, bf16[48,32,128]{2,1,0:T(8,128)(2,1)} %copy-done.5, bf16[48,8,128]{2,1,0:T(8,128)(2,1)} %copy-done.8, bf16[48,8,128]{2,1,0:T(8,128)(2,1)} %copy-done.9), custom_call_target="tpu_custom_call" | custom-call | tf_op jit(solution)/shard_map/fold_planes/pallas_call | solution.py:206
  59.8 2.7 %collective-permute-start.3 = (bf16[30,40,128]{2,1,0:T(8,128)(2,1)}, bf16[30,40,128]{2,1,0:T(8,128)(2,1)S(1)}, u32[]{:S(2)}, u32[]{:S(2)}) collective-permute-start(bf16[30,40,128]{2,1,0:T(8,128)(2,1)} %get-tuple-element.18), channel_id=1, source_target_pairs={{0,2},{2,4},{4,6},{6,8},{8,10},{10,12},{12,14},{14,0},{1,3},{3,5},... | collective-permute-start | bytes 921608 | tf_op jit(solution)/shard_map/ppermute | solution.py:36
  62.5 1.4 collective-permute-start.4
  63.9 2.3 %collective-permute-start.5 = (bf16[6,40,128]{2,1,0:T(8,128)(2,1)}, bf16[6,40,128]{2,1,0:T(8,128)(2,1)S(1)}, u32[]{:S(2)}, u32[]{:S(2)}) collective-permute-start(bf16[6,40,128]{2,1,0:T(8,128)(2,1)} %get-tuple-element.20), channel_id=1, source_target_pairs={{0,14},{2,0},{4,2},{6,4},{8,6},{10,8},{12,10},{14,12},{1,15},{3,1}... | collective-permute-start | bytes 184328 | tf_op jit(solution)/shard_map/ppermute | solution.py:36
  66.2 8.0 %collective-permute-done.4.second_left = bf16[6,40,128]{2,1,0:T(8,128)(2,1)S(1)} collective-permute-done((bf16[6,40,128]{2,1,0:T(8,128)(2,1)}, bf16[6,40,128]{2,1,0:T(8,128)(2,1)S(1)}, u32[]{:S(2)}, u32[]{:S(2)}) %collective-permute-start.4) | collective-permute-done | bytes 61472 | tf_op jit(solution)/shard_map/ppermute | solution.py:36
  74.2 0.6 copy-done.13
  74.8 0.1 copy-done.6
  75.0 2.2 %fold_rows.1 = (f32[24,40,128]{2,1,0:T(8,128)}, bf16[24,40,128]{2,1,0:T(8,128)(2,1)}) custom-call(s32[1]{0:T(128)} %bitcast.position, f32[30,40,128]{2,1,0:T(8,128)} %get-tuple-element.17.own, bf16[30,40,128]{2,1,0:T(8,128)(2,1)} %copy-done.6, bf16[6,40,128]{2,1,0:T(8,128)(2,1)} %copy-done.13, bf16[6,40,128]{2,1,0:T(8,128)(2,1)} %copy-done.14), custom_call_target="tpu_custom_call" | custom-call | tf_op jit(solution)/shard_map/fold_rows/pallas_call | solution.py:241
  77.1 0.5 collective-permute-start.6
  77.8 6.7 %collective-permute-done.6.other = bf16[24,40,128]{2,1,0:T(8,128)(2,1)S(1)} collective-permute-done((bf16[24,40,128]{2,1,0:T(8,128)(2,1)}, bf16[24,40,128]{2,1,0:T(8,128)(2,1)S(1)}, u32[]{:S(2)}, u32[]{:S(2)}) %collective-permute-start.6) | collective-permute-done | bytes 245792 | tf_op jit(solution)/shard_map/ppermute | solution.py:36
  84.6 14.7 %smooth_and_network.1.own = bf16[12,24,128]{2,1,0:T(8,128)(2,1)S(1)} custom-call(f32[8,13]{1,0:T(8,128)S(1)} %fusion.47.taps, f32[24,40,128]{2,1,0:T(8,128)S(1)} %copy-done, bf16[24,40,128]{2,1,0:T(8,128)(2,1)S(1)} %collective-permute-done.6.other, bf16[384,40]{1,0:T(8,128)(2,1)S(1)} %pad_maximum_fusion.plane_table, ...), custom_call_target="tpu_custom_call" | custom-call | tf_op jit(solution)/shard_map/smooth_and_network/pallas_call | solution.py:346
  99.4 0.4 collective-permute-start.7
  99.8 3.3 %collective-permute-start.8 = (bf16[12,24,128]{2,1,0:T(8,128)(2,1)S(1)}, bf16[12,24,128]{2,1,0:T(8,128)(2,1)S(1)}, u32[]{:S(2)}, u32[]{:S(2)}) collective-permute-start(bf16[12,24,128]{2,1,0:T(8,128)(2,1)S(1)} %smooth_and_network.1.own), channel_id=1, source_target_pairs={{0,14},{2,0},{4,2},{6,4},{8,6},{10,8},{12,10},{14,12},{1,15},{3,1}... | collective-permute-start | bytes 221192 | tf_op jit(solution)/shard_map/ppermute | solution.py:36
  103.1 1.5 collective-permute-start.9
  104.5 3.0 %collective-permute-done.9.next_other = bf16[12,24,128]{2,1,0:T(8,128)(2,1)S(1)} collective-permute-done((bf16[12,24,128]{2,1,0:T(8,128)(2,1)S(1)}, bf16[12,24,128]{2,1,0:T(8,128)(2,1)S(1)}, u32[]{:S(2)}, u32[]{:S(2)}) %collective-permute-start.9) | collective-permute-done | bytes 73760 | tf_op jit(solution)/shard_map/ppermute | solution.py:46
  107.5 0.6 copy-done.12
  108.1 1.7 %widen_rows.1.wide = bf16[48,24,128]{2,1,0:T(8,128)(2,1)} custom-call(s32[1]{0:T(128)} %bitcast.position, bf16[12,24,128]{2,1,0:T(8,128)(2,1)} %copy-done.1, bf16[12,24,128]{2,1,0:T(8,128)(2,1)} %copy-done.10, bf16[12,24,128]{2,1,0:T(8,128)(2,1)} %copy-done.11, bf16[12,24,128]{2,1,0:T(8,128)(2,1)} %copy-done.12), custom_call_target="tpu_custom_call" | custom-call | tf_op jit(solution)/shard_map/widen_rows/pallas_call | solution.py:436
  109.9 2.9 %collective-permute-start.10 = (bf16[48,24,128]{2,1,0:T(8,128)(2,1)}, bf16[48,24,128]{2,1,0:T(8,128)(2,1)S(1)}, u32[]{:S(2)}, u32[]{:S(2)}) collective-permute-start(bf16[48,24,128]{2,1,0:T(8,128)(2,1)} %widen_rows.1.wide), channel_id=1, source_target_pairs={{0,240},{16,0},{32,16},{48,32},{64,48},{80,64},{96,80},{112,96},{1... | collective-permute-start | bytes 884744 | tf_op jit(solution)/shard_map/ppermute | solution.py:36
  112.8 5.0 %collective-permute-done.10.beyond = bf16[48,24,128]{2,1,0:T(8,128)(2,1)S(1)} collective-permute-done((bf16[48,24,128]{2,1,0:T(8,128)(2,1)}, bf16[48,24,128]{2,1,0:T(8,128)(2,1)S(1)}, u32[]{:S(2)}, u32[]{:S(2)}) %collective-permute-start.10) | collective-permute-done | bytes 294944 | tf_op jit(solution)/shard_map/ppermute | solution.py:36
  117.8 0.7 copy-done.7
  118.5 5.2 %cut_windows.1 = bf16[16,216,128]{2,1,0:T(8,128)(2,1)} custom-call(s32[16,128]{1,0:T(8,128)} %get-tuple-element.23.offsets, bf16[48,24,128]{2,1,0:T(8,128)(2,1)} %widen_rows.1.wide, bf16[48,24,128]{2,1,0:T(8,128)(2,1)} %copy-done.7), custom_call_target="tpu_custom_call" | custom-call | tf_op jit(solution)/shard_map/cut_windows/pallas_call | solution.py:477
  123.7 5.0 %all-to-all-start.1 = ((bf16[16,216,128]{2,1,0:T(8,128)(2,1)}), bf16[16,216,128]{2,1,0:T(8,128)(2,1)S(1)}, u32[]{:S(2)}, u32[]{:S(2)}) async-start(bf16[16,216,128]{2,1,0:T(8,128)(2,1)} %cut_windows.1), calls=%async_computation.1 | async-start | bytes 1769472 | tf_op jit(solution)/shard_map/all_to_all | solution.py:520
  128.7 0.7 copy.62
  129.4 23.9 %all-to-all-done.1.windows = bf16[16,216,128]{2,1,0:T(8,128)(2,1)S(1)} async-done(((bf16[16,216,128]{2,1,0:T(8,128)(2,1)}), bf16[16,216,128]{2,1,0:T(8,128)(2,1)S(1)}, u32[]{:S(2)}, u32[]{:S(2)}) %all-to-all-start.1) | async-done | bytes 884768 | tf_op jit(solution)/shard_map/all_to_all | solution.py:520
  153.3 0.9 copy-done.3
  154.2 3.4 %apply_windows.1 = bf16[16,24,576]{2,1,0:T(8,128)(2,1)} custom-call(s32[16,3]{1,0:T(8,128)} %copy.53.corners, bf16[16,216,128]{2,1,0:T(8,128)(2,1)} %copy-done.3, bf16[16,24,576]{2,1,0:T(8,128)(2,1)} %orbitals.3), custom_call_target="tpu_custom_call" | custom-call | tf_op jit(solution)/shard_map/apply_windows/pallas_call | solution.py:509
  (109 shorter events, 3.6 us)
Async XLA Ops:
  5.4 10.3 %copy-start.17 = (f32[8]{0:T(128)S(1)}, f32[8]{0:T(128)}, u32[]{:S(2)}) copy-start(f32[8]{0:T(128)} %param.13) | copy-start | bytes 100
  5.4 11.0 %copy-start.16 = (f32[8,64]{1,0:T(8,128)S(1)}, f32[8,64]{1,0:T(8,128)}, u32[]{:S(2)}) copy-start(f32[8,64]{1,0:T(8,128)} %param.14) | copy-start | bytes 6148
  5.4 11.0 %copy-start.18 = (f32[64]{0:T(128)S(1)}, f32[64]{0:T(128)}, u32[]{:S(2)}) copy-start(f32[64]{0:T(128)} %param.15) | copy-start | bytes 772
  5.4 11.1 %copy-start.15 = (f32[64,64]{1,0:T(8,128)S(1)}, f32[64,64]{1,0:T(8,128)}, u32[]{:S(2)}) copy-start(f32[64,64]{1,0:T(8,128)} %param.16) | copy-start | bytes 49156
  5.4 35.4 %all-to-all-start = ((bf16[16,224,128]{2,1,0:T(8,128)(2,1)}), bf16[16,224,128]{2,1,0:T(8,128)(2,1)S(1)}, u32[]{:S(2)}, u32[]{:S(2)}) async-start(bf16[16,224,128]{2,1,0:T(8,128)(2,1)} %pack_boxes.1), calls=%async_computation | async-start | bytes 1835008 | tf_op jit(solution)/shard_map/all_to_all | solution.py:520
  21.0 27.8 %copy-start.19 = (f32[64]{0:T(128)S(1)}, f32[64]{0:T(128)}, u32[]{:S(2)}) copy-start(f32[64]{0:T(128)} %param.17) | copy-start | bytes 772
  21.0 28.2 %copy-start.20 = (f32[64]{0:T(128)S(1)}, f32[64]{0:T(128)}, u32[]{:S(2)}) copy-start(f32[64]{0:T(128)} %param.18) | copy-start | bytes 772
  40.9 1.0 copy-start.2
  48.1 8.5 %collective-permute-start = (bf16[48,32,128]{2,1,0:T(8,128)(2,1)}, bf16[48,32,128]{2,1,0:T(8,128)(2,1)S(1)}, u32[]{:S(2)}, u32[]{:S(2)}) collective-permute-start(bf16[48,32,128]{2,1,0:T(8,128)(2,1)} %get-tuple-element.14), channel_id=1, source_target_pairs={{0,16},{16,32},{32,48},{48,64},{64,80},{80,96},{96,112},{112,128},... | collective-permute-start | bytes 1179656 | tf_op jit(solution)/shard_map/ppermute | solution.py:36
  48.2 8.4 %collective-permute-start.1 = (bf16[48,8,128]{2,1,0:T(8,128)(2,1)}, bf16[48,8,128]{2,1,0:T(8,128)(2,1)S(1)}, u32[]{:S(2)}, u32[]{:S(2)}) collective-permute-start(bf16[48,8,128]{2,1,0:T(8,128)(2,1)} %get-tuple-element.15), channel_id=1, source_target_pairs={{0,32},{16,48},{32,64},{48,80},{64,96},{80,112},{96,128},{112,144}... | collective-permute-start | bytes 294920 | tf_op jit(solution)/shard_map/ppermute | solution.py:36
  48.3 8.4 %collective-permute-start.2 = (bf16[48,8,128]{2,1,0:T(8,128)(2,1)}, bf16[48,8,128]{2,1,0:T(8,128)(2,1)S(1)}, u32[]{:S(2)}, u32[]{:S(2)}) collective-permute-start(bf16[48,8,128]{2,1,0:T(8,128)(2,1)} %get-tuple-element.16), channel_id=1, source_target_pairs={{0,240},{16,0},{32,16},{48,32},{64,48},{80,64},{96,80},{112,96},{1... | collective-permute-start | bytes 294920 | tf_op jit(solution)/shard_map/ppermute | solution.py:36
  56.6 0.6 copy-start.8
  56.6 0.7 copy-start.9
  56.6 0.8 copy-start.5
  59.8 14.5 %collective-permute-start.3 = (bf16[30,40,128]{2,1,0:T(8,128)(2,1)}, bf16[30,40,128]{2,1,0:T(8,128)(2,1)S(1)}, u32[]{:S(2)}, u32[]{:S(2)}) collective-permute-start(bf16[30,40,128]{2,1,0:T(8,128)(2,1)} %get-tuple-element.18), channel_id=1, source_target_pairs={{0,2},{2,4},{4,6},{6,8},{8,10},{10,12},{12,14},{14,0},{1,3},{3,5},... | collective-permute-start | bytes 921608 | tf_op jit(solution)/shard_map/ppermute | solution.py:36
  62.5 11.7 %collective-permute-start.4 = (bf16[6,40,128]{2,1,0:T(8,128)(2,1)}, bf16[6,40,128]{2,1,0:T(8,128)(2,1)S(1)}, u32[]{:S(2)}, u32[]{:S(2)}) collective-permute-start(bf16[6,40,128]{2,1,0:T(8,128)(2,1)} %get-tuple-element.19), channel_id=1, source_target_pairs={{0,4},{2,6},{4,8},{6,10},{8,12},{10,14},{12,0},{14,2},{1,5},{3,7},... | collective-permute-start | bytes 184328 | tf_op jit(solution)/shard_map/ppermute | solution.py:36
  63.9 10.3 %collective-permute-start.5 = (bf16[6,40,128]{2,1,0:T(8,128)(2,1)}, bf16[6,40,128]{2,1,0:T(8,128)(2,1)S(1)}, u32[]{:S(2)}, u32[]{:S(2)}) collective-permute-start(bf16[6,40,128]{2,1,0:T(8,128)(2,1)} %get-tuple-element.20), channel_id=1, source_target_pairs={{0,14},{2,0},{4,2},{6,4},{8,6},{10,8},{12,10},{14,12},{1,15},{3,1}... | collective-permute-start | bytes 184328 | tf_op jit(solution)/shard_map/ppermute | solution.py:36
  74.2 0.6 copy-start.13
  74.2 0.6 copy-start.14
  74.2 0.7 copy-start.6
  77.1 7.5 %copy-start = (f32[24,40,128]{2,1,0:T(8,128)S(1)}, f32[24,40,128]{2,1,0:T(8,128)}, u32[]{:S(2)}) copy-start(f32[24,40,128]{2,1,0:T(8,128)} %get-tuple-element.21.kept) | copy-start | bytes 1474564
  77.1 7.3 %collective-permute-start.6 = (bf16[24,40,128]{2,1,0:T(8,128)(2,1)}, bf16[24,40,128]{2,1,0:T(8,128)(2,1)S(1)}, u32[]{:S(2)}, u32[]{:S(2)}) collective-permute-start(bf16[24,40,128]{2,1,0:T(8,128)(2,1)} %get-tuple-element.22), channel_id=1, source_target_pairs={{0,1},{1,0},{2,3},{3,2},{4,5},{5,4},{6,7},{7,6},{8,9},{9,8},{10,11... | collective-permute-start | bytes 737288 | tf_op jit(solution)/shard_map/ppermute | solution.py:36
  99.4 8.1 %copy-start.1 = (bf16[12,24,128]{2,1,0:T(8,128)(2,1)}, bf16[12,24,128]{2,1,0:T(8,128)(2,1)S(1)}, u32[]{:S(2)}) copy-start(bf16[12,24,128]{2,1,0:T(8,128)(2,1)S(1)} %smooth_and_network.1.own) | copy-start | bytes 221188
  99.4 5.1 %collective-permute-start.7 = (bf16[12,24,128]{2,1,0:T(8,128)(2,1)S(1)}, bf16[12,24,128]{2,1,0:T(8,128)(2,1)S(1)}, u32[]{:S(2)}, u32[]{:S(2)}) collective-permute-start(bf16[12,24,128]{2,1,0:T(8,128)(2,1)S(1)} %smooth_and_network.1.own), channel_id=1, source_target_pairs={{0,1},{1,0},{2,3},{3,2},{4,5},{5,4},{6,7},{7,6},{8,9},{9,8},{10,11... | collective-permute-start | bytes 221192 | tf_op jit(solution)/shard_map/ppermute | solution.py:36
  99.8 4.8 %collective-permute-start.8 = (bf16[12,24,128]{2,1,0:T(8,128)(2,1)S(1)}, bf16[12,24,128]{2,1,0:T(8,128)(2,1)S(1)}, u32[]{:S(2)}, u32[]{:S(2)}) collective-permute-start(bf16[12,24,128]{2,1,0:T(8,128)(2,1)S(1)} %smooth_and_network.1.own), channel_id=1, source_target_pairs={{0,14},{2,0},{4,2},{6,4},{8,6},{10,8},{12,10},{14,12},{1,15},{3,1}... | collective-permute-start | bytes 221192 | tf_op jit(solution)/shard_map/ppermute | solution.py:36
  103.1 4.5 %collective-permute-start.9 = (bf16[12,24,128]{2,1,0:T(8,128)(2,1)S(1)}, bf16[12,24,128]{2,1,0:T(8,128)(2,1)S(1)}, u32[]{:S(2)}, u32[]{:S(2)}) collective-permute-start(bf16[12,24,128]{2,1,0:T(8,128)(2,1)S(1)} %smooth_and_network.1.own), channel_id=1, source_target_pairs={{3,0},{2,1},{5,2},{4,3},{7,4},{6,5},{9,6},{8,7},{11,8},{10,9},{13,... | collective-permute-start | bytes 221192 | tf_op jit(solution)/shard_map/ppermute | solution.py:46
  104.5 3.0 %copy-start.10 = (bf16[12,24,128]{2,1,0:T(8,128)(2,1)}, bf16[12,24,128]{2,1,0:T(8,128)(2,1)S(1)}, u32[]{:S(2)}) copy-start(bf16[12,24,128]{2,1,0:T(8,128)(2,1)S(1)} %collective-permute-done.7.partner) | copy-start | bytes 221188
  104.5 3.0 %copy-start.11 = (bf16[12,24,128]{2,1,0:T(8,128)(2,1)}, bf16[12,24,128]{2,1,0:T(8,128)(2,1)S(1)}, u32[]{:S(2)}) copy-start(bf16[12,24,128]{2,1,0:T(8,128)(2,1)S(1)} %collective-permute-done.8.next_same) | copy-start | bytes 221188
  107.5 0.6 copy-start.12
  109.9 7.9 %collective-permute-start.10 = (bf16[48,24,128]{2,1,0:T(8,128)(2,1)}, bf16[48,24,128]{2,1,0:T(8,128)(2,1)S(1)}, u32[]{:S(2)}, u32[]{:S(2)}) collective-permute-start(bf16[48,24,128]{2,1,0:T(8,128)(2,1)} %widen_rows.1.wide), channel_id=1, source_target_pairs={{0,240},{16,0},{32,16},{48,32},{64,48},{80,64},{96,80},{112,96},{1... | collective-permute-start | bytes 884744 | tf_op jit(solution)/shard_map/ppermute | solution.py:36
  117.8 0.7 copy-start.7
  123.7 5.0 %copy-start.4 = (bf16[48,24,128]{2,1,0:T(8,128)(2,1)S(1)}, bf16[48,24,128]{2,1,0:T(8,128)(2,1)}, u32[]{:S(2)}) copy-start(bf16[48,24,128]{2,1,0:T(8,128)(2,1)} %widen_rows.1.wide) | copy-start | bytes 884740
  123.7 29.6 %all-to-all-start.1 = ((bf16[16,216,128]{2,1,0:T(8,128)(2,1)}), bf16[16,216,128]{2,1,0:T(8,128)(2,1)S(1)}, u32[]{:S(2)}, u32[]{:S(2)}) async-start(bf16[16,216,128]{2,1,0:T(8,128)(2,1)} %cut_windows.1), calls=%async_computation.1 | async-start | bytes 1769472 | tf_op jit(solution)/shard_map/all_to_all | solution.py:520
  153.3 0.9 copy-start.3

commit v2 on v1

--- a/solution.py
+++ b/solution.py
@@ -27,6 +27,7 @@
 
 VMEM = pl.BlockSpec(memory_space=pltpu.VMEM)
 SMEM = pl.BlockSpec(memory_space=pltpu.SMEM)
+ROOM = pltpu.CompilerParams(vmem_limit_bytes=16 * 1024 * 1024)
 f32 = jnp.float32
 bf16 = jnp.bfloat16
 
@@ -36,10 +37,10 @@
     return lax.ppermute(x, axis, [(i, (i + by) % count) for i in range(count)])
 
 
-def from_next_other(x):
+def crossed(x, by):
     tiles, owners = lax.axis_size("gy"), lax.axis_size("orb")
     pairs = [
-        ((tile + 1) % tiles * owners + (orb + 1) % owners, tile * owners + orb)
+        (tile * owners + orb, (tile + by) % tiles * owners + (orb + 1) % owners)
         for tile in range(tiles)
         for orb in range(owners)
     ]
@@ -72,9 +73,9 @@
     field = lanes(8) % 64
 
     def place(i, carry):
-        plane = corners[i, 0]
-        row = corners[i, 1]
-        column = corners[i, 2]
+        plane = corners[0, i]
+        row = corners[1, i]
+        column = corners[2, i]
         slab = lax.div(plane, CZ)
         rank = count[slab]
         count[slab] = rank + 1
@@ -105,6 +106,7 @@
         in_specs=[SMEM, SMEM, VMEM],
         out_specs=VMEM,
         scratch_shapes=[pltpu.SMEM((SLABS,), jnp.int32)],
+        compiler_params=ROOM,
     )(corners, occupation, orbitals)
 
 
@@ -178,6 +180,7 @@
             pltpu.SMEM((SLABS, NX), jnp.int32),
             pltpu.SemaphoreType.DMA,
         ],
+        compiler_params=ROOM,
     )(received)
 
 
@@ -214,6 +217,7 @@
         ),
         in_specs=[VMEM] * 4,
         out_specs=(VMEM,) * 4,
+        compiler_params=ROOM,
     )(own, below, second_below, above)
 
 
@@ -248,6 +252,7 @@
         in_specs=[SMEM] + [VMEM] * 4,
         out_specs=(VMEM, VMEM),
         scratch_shapes=[pltpu.VMEM((REACH + RAD, PLANES, NX), f32)],
+        compiler_params=ROOM,
     )(position, own, left, second_left, right)
 
 
@@ -354,7 +359,7 @@
             pltpu.VMEM((CHAN, HALF * CZ, NX), f32),
             pltpu.VMEM((HALF * CZ, NX), f32),
         ],
-        compiler_params=pltpu.CompilerParams(vmem_limit_bytes=48 * 1024 * 1024),
+        compiler_params=ROOM,
     )(taps, kept, other, *tables)
 
 
@@ -439,6 +444,7 @@
         out_shape=jax.ShapeDtypeStruct((CY + BOX, CZ, NX), bf16),
         in_specs=[SMEM] + [VMEM] * 4,
         out_specs=VMEM,
+        compiler_params=ROOM,
     )(position, own, partner, next_same, next_other)
 
 
@@ -481,6 +487,7 @@
         in_specs=[SMEM, VMEM, VMEM],
         out_specs=VMEM,
         scratch_shapes=[pltpu.VMEM((CY + BOX, CZ + BOX, NX), f32)],
+        compiler_params=ROOM,
     )(offsets, wide, beyond)
 
 
@@ -492,7 +499,7 @@
     lax.fori_loop(0, SLABS, clear, 0)
 
     def place(i, carry):
-        slab = lax.div(corners[i, 0], CZ)
+        slab = lax.div(corners[0, i], CZ)
         rank = count[slab]
         count[slab] = rank + 1
         main = windows[slab, pl.ds(pl.multiple_of(rank * MAIN, 32), MAIN), :].astype(f32)
@@ -513,6 +520,7 @@
         in_specs=[SMEM, VMEM, VMEM],
         out_specs=VMEM,
         scratch_shapes=[pltpu.SMEM((SLABS,), jnp.int32)],
+        compiler_params=ROOM,
     )(corners, windows, orbitals)
 
 
@@ -521,6 +529,7 @@
 
 
 def local(orbitals, occupation, corners, kernel_widths, w_in, b_in, w_mid, b_mid, w_out, b_out):
+    corners = corners.T
     taps = kernel_taps(kernel_widths)
     tables = model_tables(taps, w_in, b_in, w_mid, b_mid, w_out, b_out)
     received = exchange(pack(corners, occupation, orbitals), "gz")
@@ -530,14 +539,14 @@
     second_below = shifted(second_up, "gz", 2)
     above = shifted(next_down, "gz", -1)
     kept, next_right, second_right, next_left = fold_planes(own, below, second_below, above)
-    left = shifted(next_right, "gy", 1)
+    left = crossed(next_right, 1)
     second_left = shifted(second_right, "gy", 2)
-    right = shifted(next_left, "gy", -1)
+    right = crossed(next_left, -1)
     kept, given = fold_rows(position, kept, left, second_left, right)
     half = model(kept, shifted(given, "orb", 1), taps, tables)
     partner = shifted(half, "orb", 1)
     next_same = shifted(half, "gy", -1)
-    next_other = from_next_other(half)
+    next_other = crossed(half, -1)
     wide = widen(position, half, partner, next_same, next_other)
     windows = cut(offsets, wide, shifted(wide, "gz", -1))
     applied = apply(corners, exchange(windows, "gz"), orbitals)

time: 158 us -> 144 us (0.911)
  Pallas kernels: 39.3 us -> 29.6 us
  local copies, waits for them, and re-layouts: 11 us -> 7.21 us
  waiting for transfers between devices: 72.7 us -> 71.1 us
    ppermute x10 -> x8, starting transfers between devices: 14.2 us -> 8.27 us  [shifted(): return lax.ppermute(x, axis, [(i, (i + by) % count) for i in range(count)])]
    ppermute x1 -> x3, starting transfers between devices: 1.48 us -> 6.79 us  [crossed(): return lax.ppermute(x, ('gy', 'orb'), pairs)]
    unnamed x44 -> x27, local copies, waits for them, and re-layouts: 6.84 us -> 3.09 us
    pallas_call x1, Pallas kernels: 6.3 us -> 4.09 us  [deposit(): pl.pallas_call(deposit_body, name='deposit_boxes', out_shape=(jax.ShapeDt...]
    pallas_call x1, Pallas kernels: 2.32 us -> 0.13 us  [fold_planes(): pl.pallas_call(fold_planes_body, name='fold_planes', out_shape=(jax.Shape...]
    pallas_call x1, Pallas kernels: 2.15 us -> 0.13 us  [fold_rows(): pl.pallas_call(fold_rows_body, name='fold_rows', out_shape=(jax.ShapeDtyp...]
    pallas_call x1, Pallas kernels: 1.72 us -> 0.02 us  [widen(): pl.pallas_call(widen_body, name='widen_rows', out_shape=jax.ShapeDtypeStr...]
    ppermute x10 -> x8, waiting for transfers between devices: 26 us -> 25.4 us  [shifted(): return lax.ppermute(x, axis, [(i, (i + by) % count) for i in range(count)])]
  transfers between devices with their start and end apart: 13 -> 13, of which waited for: 7 -> 7; matrix products, arithmetic and copies ran while one was open for 4% -> 6% of each run, Pallas kernels for 0% -> 0%
where the time goes in v2:
time: 144 us; the launch traced here: 143 us
  waiting for transfers between devices  71.1 us (49%)
  starting transfers between devices  30.2 us (21%)
  Pallas kernels  29.6 us (21%)
  local copies, waits for them, and re-layouts  7.21 us (5%)
  other arithmetic  3.43 us (2%)
  between operations  1.71 us (1%)
    all_to_all x2, waiting for transfers between devices, exchange(): return lax.all_to_all(x, axis, split_axis=0, concat_axis=0, tiled=True)  43.1 us
    ppermute x8, waiting for transfers between devices, shifted(): return lax.ppermute(x, axis, [(i, (i + by) % count) for i in range(count)])  25.4 us
    all_to_all x2, starting transfers between devices, exchange(): return lax.all_to_all(x, axis, split_axis=0, concat_axis=0, tiled=True)  15.1 us
    pallas_call x1, Pallas kernels, model(): pl.pallas_call(model_body, name='smooth_and_network', out_shape=jax.Shape...  14.8 us
    ppermute x8, starting transfers between devices, shifted(): return lax.ppermute(x, axis, [(i, (i + by) % count) for i in range(count)])  8.27 us
    ppermute x3, starting transfers between devices, crossed(): return lax.ppermute(x, ('gy', 'orb'), pairs)  6.79 us
    pallas_call x1, Pallas kernels, cut(): pl.pallas_call(cut_body, name='cut_windows', out_shape=jax.ShapeDtypeStru...  4.79 us
    pallas_call x1, Pallas kernels, deposit(): pl.pallas_call(deposit_body, name='deposit_boxes', out_shape=(jax.ShapeDt...  4.09 us
  transfers between devices with their start and end apart: 13, of which 7 were waited for; matrix products, arithmetic and copies ran while one was open for 6% of the time, Pallas kernels for 0%

profile of v2, /device:TPU:1, one launch (start us, length us, event | category | flops | bytes accessed | tf_op | source)
XLA Modules:
  0.0 143.2 jit_solution(9292397799062958803)
XLA Ops:
  0.6 1.0 copy-done
  1.7 0.7 copy-done.2
  2.3 0.7 copy-done.4
  3.0 3.0 %pack_boxes.1 = bf16[16,224,128]{2,1,0:T(8,128)(2,1)} custom-call(s32[3,16]{1,0:T(4,128)S(1)} %bitcast.99, f32[16]{0:T(128)S(1)} %copy-done.4, bf16[16,24,576]{2,1,0:T(8,128)(2,1)S(1)} %copy-done), custom_call_target="tpu_custom_call" | custom-call | tf_op jit(solution)/shard_map/pack_boxes/pallas_call | solution.py:102
  6.0 10.1 %all-to-all-start = ((bf16[16,224,128]{2,1,0:T(8,128)(2,1)}), bf16[16,224,128]{2,1,0:T(8,128)(2,1)S(1)}, u32[]{:S(2)}, u32[]{:S(2)}) async-start(bf16[16,224,128]{2,1,0:T(8,128)(2,1)} %pack_boxes.1), calls=%async_computation | async-start | bytes 1835008 | tf_op jit(solution)/shard_map/all_to_all | solution.py:528
  16.3 0.2 fusion.48
  16.6 0.4 slice_reduce_fusion.12
  17.1 0.1 broadcast_multiply_fusion
  17.2 0.1 mul.654
  17.3 0.1 copy.44
  17.5 0.1 copy.46
  17.7 0.1 mul.604
  19.6 0.2 copy.43
  19.8 0.1 copy.47
  20.0 1.0 reduce-precision_convert_fusion.1
  21.3 0.1 broadcast_multiply_fusion.1
  21.4 0.7 fusion.2
  22.2 19.2 %all-to-all-done.received = bf16[16,224,128]{2,1,0:T(8,128)(2,1)S(1)} async-done(((bf16[16,224,128]{2,1,0:T(8,128)(2,1)}), bf16[16,224,128]{2,1,0:T(8,128)(2,1)S(1)}, u32[]{:S(2)}, u32[]{:S(2)}) %all-to-all-start) | async-done | bytes 917536 | tf_op jit(solution)/shard_map/all_to_all | solution.py:528
  41.4 4.1 %deposit_boxes.1 = (f32[48,32,128]{2,1,0:T(8,128)S(1)}, bf16[48,32,128]{2,1,0:T(8,128)(2,1)S(1)}, bf16[48,8,128]{2,1,0:T(8,128)(2,1)S(1)}, bf16[48,8,128]{2,1,0:T(8,128)(2,1)S(1)}, s32[16,128]{1,0:T(8,128)S(1)}) custom-call(bf16[16,224,128]{2,1,0:T(8,128)(2,1)S(1)} %all-to-all-done.received), custom_call_target="tpu_custom_call" | custom-call | tf_op jit(solution)/shard_map/deposit_boxes/pallas_call | solution.py:165
  45.5 0.6 fusion.5
  46.2 0.5 collective-permute-start.2
  46.7 0.2 copy.48
  46.8 0.1 mul.662
  47.0 0.1 broadcast_in_dim.11
  47.1 0.1 broadcast_in_dim.13
  47.8 0.3 concatenate.28.first_table
  48.1 5.7 %collective-permute-done.1.second_below = bf16[48,8,128]{2,1,0:T(8,128)(2,1)S(1)} collective-permute-done((bf16[48,8,128]{2,1,0:T(8,128)(2,1)S(1)}, bf16[48,8,128]{2,1,0:T(8,128)(2,1)S(1)}, u32[]{:S(2)}, u32[]{:S(2)}) %collective-permute-start.1) | collective-permute-done | bytes 98336 | tf_op jit(solution)/shard_map/ppermute | solution.py:37
  53.8 0.1 fold_planes.1
  53.9 2.6 %collective-permute-start.3 = (bf16[30,40,128]{2,1,0:T(8,128)(2,1)S(1)}, bf16[30,40,128]{2,1,0:T(8,128)(2,1)S(1)}, u32[]{:S(2)}, u32[]{:S(2)}) collective-permute-start(bf16[30,40,128]{2,1,0:T(8,128)(2,1)S(1)} %get-tuple-element.18), channel_id=1, source_target_pairs={{0,3},{1,2},{2,5},{3,4},{4,7},{5,6},{6,9},{7,8},{8,11},{9,10},{10,... | collective-permute-start | bytes 921608 | tf_op jit(solution)/shard_map/ppermute | solution.py:47
  56.5 1.4 collective-permute-start.4
  57.9 2.3 %collective-permute-start.5 = (bf16[6,40,128]{2,1,0:T(8,128)(2,1)S(1)}, bf16[6,40,128]{2,1,0:T(8,128)(2,1)S(1)}, u32[]{:S(2)}, u32[]{:S(2)}) collective-permute-start(bf16[6,40,128]{2,1,0:T(8,128)(2,1)S(1)} %get-tuple-element.20), channel_id=1, source_target_pairs={{0,15},{1,14},{2,1},{3,0},{4,3},{5,2},{6,5},{7,4},{8,7},{9,6},{10,... | collective-permute-start | bytes 184328 | tf_op jit(solution)/shard_map/ppermute | solution.py:47
  60.2 7.8 %collective-permute-done.4.second_left = bf16[6,40,128]{2,1,0:T(8,128)(2,1)S(1)} collective-permute-done((bf16[6,40,128]{2,1,0:T(8,128)(2,1)S(1)}, bf16[6,40,128]{2,1,0:T(8,128)(2,1)S(1)}, u32[]{:S(2)}, u32[]{:S(2)}) %collective-permute-start.4) | collective-permute-done | bytes 61472 | tf_op jit(solution)/shard_map/ppermute | solution.py:37
  68.0 0.1 fold_rows.1
  68.2 0.1 collective-permute-start.6
  68.3 0.1 fusion.1.column_table
  68.4 6.9 %collective-permute-done.6.other = bf16[24,40,128]{2,1,0:T(8,128)(2,1)S(1)} collective-permute-done((bf16[24,40,128]{2,1,0:T(8,128)(2,1)S(1)}, bf16[24,40,128]{2,1,0:T(8,128)(2,1)S(1)}, u32[]{:S(2)}, u32[]{:S(2)}) %collective-permute-start.6) | collective-permute-done | bytes 245792 | tf_op jit(solution)/shard_map/ppermute | solution.py:37
  75.5 14.8 %smooth_and_network.1.own = bf16[12,24,128]{2,1,0:T(8,128)(2,1)S(1)} custom-call(f32[8,13]{1,0:T(8,128)S(1)} %fusion.47.taps, f32[24,40,128]{2,1,0:T(8,128)S(1)} %get-tuple-element.21.kept, bf16[24,40,128]{2,1,0:T(8,128)(2,1)S(1)} %collective-permute-done.6.other, bf16[384,40]{1,0:T(8,128)(2,1)S(1)} %pad_maximum_fusion.plane_table, ...), custom_call_target="tpu_custom_call" | custom-call | tf_op jit(solution)/shard_map/smooth_and_network/pallas_call | solution.py:351
  90.3 0.2 collective-permute-start.7
  90.5 2.9 %collective-permute-start.8 = (bf16[12,24,128]{2,1,0:T(8,128)(2,1)S(1)}, bf16[12,24,128]{2,1,0:T(8,128)(2,1)S(1)}, u32[]{:S(2)}, u32[]{:S(2)}) collective-permute-start(bf16[12,24,128]{2,1,0:T(8,128)(2,1)S(1)} %smooth_and_network.1.own), channel_id=1, source_target_pairs={{0,14},{2,0},{4,2},{6,4},{8,6},{10,8},{12,10},{14,12},{1,15},{3,1}... | collective-permute-start | bytes 221192 | tf_op jit(solution)/shard_map/ppermute | solution.py:37
  93.4 1.9 %collective-permute-start.9 = (bf16[12,24,128]{2,1,0:T(8,128)(2,1)S(1)}, bf16[12,24,128]{2,1,0:T(8,128)(2,1)S(1)}, u32[]{:S(2)}, u32[]{:S(2)}) collective-permute-start(bf16[12,24,128]{2,1,0:T(8,128)(2,1)S(1)} %smooth_and_network.1.own), channel_id=1, source_target_pairs={{0,15},{1,14},{2,1},{3,0},{4,3},{5,2},{6,5},{7,4},{8,7},{9,6},{10,... | collective-permute-start | bytes 221192 | tf_op jit(solution)/shard_map/ppermute | solution.py:47
  95.4 2.6 %collective-permute-done.9.next_other = bf16[12,24,128]{2,1,0:T(8,128)(2,1)S(1)} collective-permute-done((bf16[12,24,128]{2,1,0:T(8,128)(2,1)S(1)}, bf16[12,24,128]{2,1,0:T(8,128)(2,1)S(1)}, u32[]{:S(2)}, u32[]{:S(2)}) %collective-permute-start.9) | collective-permute-done | bytes 73760 | tf_op jit(solution)/shard_map/ppermute | solution.py:47
  98.0 3.2 %collective-permute-start.10 = (bf16[48,24,128]{2,1,0:T(8,128)(2,1)S(1)}, bf16[48,24,128]{2,1,0:T(8,128)(2,1)S(1)}, u32[]{:S(2)}, u32[]{:S(2)}) collective-permute-start(bf16[48,24,128]{2,1,0:T(8,128)(2,1)S(1)} %widen_rows.1.wide), channel_id=1, source_target_pairs={{0,240},{16,0},{32,16},{48,32},{64,48},{80,64},{96,80},{112,96},{1... | collective-permute-start | bytes 884744 | tf_op jit(solution)/shard_map/ppermute | solution.py:37
  101.1 5.0 %collective-permute-done.10.beyond = bf16[48,24,128]{2,1,0:T(8,128)(2,1)S(1)} collective-permute-done((bf16[48,24,128]{2,1,0:T(8,128)(2,1)S(1)}, bf16[48,24,128]{2,1,0:T(8,128)(2,1)S(1)}, u32[]{:S(2)}, u32[]{:S(2)}) %collective-permute-start.10) | collective-permute-done | bytes 294944 | tf_op jit(solution)/shard_map/ppermute | solution.py:37
  106.1 4.8 %cut_windows.1 = bf16[16,216,128]{2,1,0:T(8,128)(2,1)} custom-call(s32[16,128]{1,0:T(8,128)S(1)} %get-tuple-element.23.offsets, bf16[48,24,128]{2,1,0:T(8,128)(2,1)S(1)} %widen_rows.1.wide, bf16[48,24,128]{2,1,0:T(8,128)(2,1)S(1)} %collective-permute-done.10.beyond), custom_call_target="tpu_custom_call" | custom-call | tf_op jit(solution)/shard_map/cut_windows/pallas_call | solution.py:483
  110.9 5.0 %all-to-all-start.1 = ((bf16[16,216,128]{2,1,0:T(8,128)(2,1)}), bf16[16,216,128]{2,1,0:T(8,128)(2,1)S(1)}, u32[]{:S(2)}, u32[]{:S(2)}) async-start(bf16[16,216,128]{2,1,0:T(8,128)(2,1)} %cut_windows.1), calls=%async_computation.1 | async-start | bytes 1769472 | tf_op jit(solution)/shard_map/all_to_all | solution.py:528
  115.9 0.7 copy.50
  116.6 23.9 %all-to-all-done.1.windows = bf16[16,216,128]{2,1,0:T(8,128)(2,1)S(1)} async-done(((bf16[16,216,128]{2,1,0:T(8,128)(2,1)}), bf16[16,216,128]{2,1,0:T(8,128)(2,1)S(1)}, u32[]{:S(2)}, u32[]{:S(2)}) %all-to-all-start.1) | async-done | bytes 884768 | tf_op jit(solution)/shard_map/all_to_all | solution.py:528
  140.5 2.7 %apply_windows.1 = bf16[16,24,576]{2,1,0:T(8,128)(2,1)} custom-call(s32[3,16]{1,0:T(4,128)S(1)} %bitcast.100, bf16[16,216,128]{2,1,0:T(8,128)(2,1)S(1)} %all-to-all-done.1.windows, bf16[16,24,576]{2,1,0:T(8,128)(2,1)S(1)} %copy-done.1), custom_call_target="tpu_custom_call" | custom-call | tf_op jit(solution)/shard_map/apply_windows/pallas_call | solution.py:516
  (92 shorter events, 3.0 us)
Async XLA Ops:
  0.6 1.0 copy-start
  1.7 0.7 copy-start.2
  2.3 0.7 copy-start.4
  6.0 10.3 %copy-start.9 = (f32[8]{0:T(128)S(1)}, f32[8]{0:T(128)}, u32[]{:S(2)}) copy-start(f32[8]{0:T(128)} %param.13) | copy-start | bytes 100
  6.0 11.0 %copy-start.8 = (f32[8,64]{1,0:T(8,128)S(1)}, f32[8,64]{1,0:T(8,128)}, u32[]{:S(2)}) copy-start(f32[8,64]{1,0:T(8,128)} %param.14) | copy-start | bytes 6148
  6.0 11.0 %copy-start.10 = (f32[64]{0:T(128)S(1)}, f32[64]{0:T(128)}, u32[]{:S(2)}) copy-start(f32[64]{0:T(128)} %param.15) | copy-start | bytes 772
  6.0 11.1 %copy-start.7 = (f32[64,64]{1,0:T(8,128)S(1)}, f32[64,64]{1,0:T(8,128)}, u32[]{:S(2)}) copy-start(f32[64,64]{1,0:T(8,128)} %param.16) | copy-start | bytes 49156
  6.0 35.4 %all-to-all-start = ((bf16[16,224,128]{2,1,0:T(8,128)(2,1)}), bf16[16,224,128]{2,1,0:T(8,128)(2,1)S(1)}, u32[]{:S(2)}, u32[]{:S(2)}) async-start(bf16[16,224,128]{2,1,0:T(8,128)(2,1)} %pack_boxes.1), calls=%async_computation | async-start | bytes 1835008 | tf_op jit(solution)/shard_map/all_to_all | solution.py:528
  22.1 24.5 %copy-start.11 = (f32[64]{0:T(128)S(1)}, f32[64]{0:T(128)}, u32[]{:S(2)}) copy-start(f32[64]{0:T(128)} %param.17) | copy-start | bytes 772
  22.1 24.9 %copy-start.12 = (f32[64]{0:T(128)S(1)}, f32[64]{0:T(128)}, u32[]{:S(2)}) copy-start(f32[64]{0:T(128)} %param.18) | copy-start | bytes 772
  45.5 8.3 %collective-permute-start = (bf16[48,32,128]{2,1,0:T(8,128)(2,1)S(1)}, bf16[48,32,128]{2,1,0:T(8,128)(2,1)S(1)}, u32[]{:S(2)}, u32[]{:S(2)}) collective-permute-start(bf16[48,32,128]{2,1,0:T(8,128)(2,1)S(1)} %get-tuple-element.14), channel_id=1, source_target_pairs={{0,16},{16,32},{32,48},{48,64},{64,80},{80,96},{96,112},{112,128},... | collective-permute-start | bytes 1179656 | tf_op jit(solution)/shard_map/ppermute | solution.py:37
  46.1 7.6 %collective-permute-start.1 = (bf16[48,8,128]{2,1,0:T(8,128)(2,1)S(1)}, bf16[48,8,128]{2,1,0:T(8,128)(2,1)S(1)}, u32[]{:S(2)}, u32[]{:S(2)}) collective-permute-start(bf16[48,8,128]{2,1,0:T(8,128)(2,1)S(1)} %get-tuple-element.15), channel_id=1, source_target_pairs={{0,32},{16,48},{32,64},{48,80},{64,96},{80,112},{96,128},{112,144}... | collective-permute-start | bytes 294920 | tf_op jit(solution)/shard_map/ppermute | solution.py:37
  46.2 7.6 %collective-permute-start.2 = (bf16[48,8,128]{2,1,0:T(8,128)(2,1)S(1)}, bf16[48,8,128]{2,1,0:T(8,128)(2,1)S(1)}, u32[]{:S(2)}, u32[]{:S(2)}) collective-permute-start(bf16[48,8,128]{2,1,0:T(8,128)(2,1)S(1)} %get-tuple-element.16), channel_id=1, source_target_pairs={{0,240},{16,0},{32,16},{48,32},{64,48},{80,64},{96,80},{112,96},{1... | collective-permute-start | bytes 294920 | tf_op jit(solution)/shard_map/ppermute | solution.py:37
  53.8 14.5 %copy-start.5 = (bf16[192,40]{1,0:T(8,128)(2,1)S(1)}, bf16[192,40]{1,0:T(8,128)(2,1)}, u32[]{:S(2)}) copy-start(bf16[192,40]{1,0:T(8,128)(2,1)} %get-tuple-element.51) | copy-start | bytes 46084
  53.8 14.5 %copy-start.6 = (bf16[192,40]{1,0:T(8,128)(2,1)S(1)}, bf16[192,40]{1,0:T(8,128)(2,1)}, u32[]{:S(2)}) copy-start(bf16[192,40]{1,0:T(8,128)(2,1)} %fusion.5) | copy-start | bytes 46084
  53.9 14.1 %collective-permute-start.3 = (bf16[30,40,128]{2,1,0:T(8,128)(2,1)S(1)}, bf16[30,40,128]{2,1,0:T(8,128)(2,1)S(1)}, u32[]{:S(2)}, u32[]{:S(2)}) collective-permute-start(bf16[30,40,128]{2,1,0:T(8,128)(2,1)S(1)} %get-tuple-element.18), channel_id=1, source_target_pairs={{0,3},{1,2},{2,5},{3,4},{4,7},{5,6},{6,9},{7,8},{8,11},{9,10},{10,... | collective-permute-start | bytes 921608 | tf_op jit(solution)/shard_map/ppermute | solution.py:47
  56.5 11.5 %collective-permute-start.4 = (bf16[6,40,128]{2,1,0:T(8,128)(2,1)S(1)}, bf16[6,40,128]{2,1,0:T(8,128)(2,1)S(1)}, u32[]{:S(2)}, u32[]{:S(2)}) collective-permute-start(bf16[6,40,128]{2,1,0:T(8,128)(2,1)S(1)} %get-tuple-element.19), channel_id=1, source_target_pairs={{0,4},{2,6},{4,8},{6,10},{8,12},{10,14},{12,0},{14,2},{1,5},{3,7},... | collective-permute-start | bytes 184328 | tf_op jit(solution)/shard_map/ppermute | solution.py:37
  57.9 10.1 %collective-permute-start.5 = (bf16[6,40,128]{2,1,0:T(8,128)(2,1)S(1)}, bf16[6,40,128]{2,1,0:T(8,128)(2,1)S(1)}, u32[]{:S(2)}, u32[]{:S(2)}) collective-permute-start(bf16[6,40,128]{2,1,0:T(8,128)(2,1)S(1)} %get-tuple-element.20), channel_id=1, source_target_pairs={{0,15},{1,14},{2,1},{3,0},{4,3},{5,2},{6,5},{7,4},{8,7},{9,6},{10,... | collective-permute-start | bytes 184328 | tf_op jit(solution)/shard_map/ppermute | solution.py:47
  68.2 7.2 %collective-permute-start.6 = (bf16[24,40,128]{2,1,0:T(8,128)(2,1)S(1)}, bf16[24,40,128]{2,1,0:T(8,128)(2,1)S(1)}, u32[]{:S(2)}, u32[]{:S(2)}) collective-permute-start(bf16[24,40,128]{2,1,0:T(8,128)(2,1)S(1)} %get-tuple-element.22), channel_id=1, source_target_pairs={{0,1},{1,0},{2,3},{3,2},{4,5},{5,4},{6,7},{7,6},{8,9},{9,8},{10,11... | collective-permute-start | bytes 737288 | tf_op jit(solution)/shard_map/ppermute | solution.py:37
  90.3 5.0 %collective-permute-start.7 = (bf16[12,24,128]{2,1,0:T(8,128)(2,1)S(1)}, bf16[12,24,128]{2,1,0:T(8,128)(2,1)S(1)}, u32[]{:S(2)}, u32[]{:S(2)}) collective-permute-start(bf16[12,24,128]{2,1,0:T(8,128)(2,1)S(1)} %smooth_and_network.1.own), channel_id=1, source_target_pairs={{0,1},{1,0},{2,3},{3,2},{4,5},{5,4},{6,7},{7,6},{8,9},{9,8},{10,11... | collective-permute-start | bytes 221192 | tf_op jit(solution)/shard_map/ppermute | solution.py:37
  90.5 4.9 %collective-permute-start.8 = (bf16[12,24,128]{2,1,0:T(8,128)(2,1)S(1)}, bf16[12,24,128]{2,1,0:T(8,128)(2,1)S(1)}, u32[]{:S(2)}, u32[]{:S(2)}) collective-permute-start(bf16[12,24,128]{2,1,0:T(8,128)(2,1)S(1)} %smooth_and_network.1.own), channel_id=1, source_target_pairs={{0,14},{2,0},{4,2},{6,4},{8,6},{10,8},{12,10},{14,12},{1,15},{3,1}... | collective-permute-start | bytes 221192 | tf_op jit(solution)/shard_map/ppermute | solution.py:37
  93.4 4.5 %collective-permute-start.9 = (bf16[12,24,128]{2,1,0:T(8,128)(2,1)S(1)}, bf16[12,24,128]{2,1,0:T(8,128)(2,1)S(1)}, u32[]{:S(2)}, u32[]{:S(2)}) collective-permute-start(bf16[12,24,128]{2,1,0:T(8,128)(2,1)S(1)} %smooth_and_network.1.own), channel_id=1, source_target_pairs={{0,15},{1,14},{2,1},{3,0},{4,3},{5,2},{6,5},{7,4},{8,7},{9,6},{10,... | collective-permute-start | bytes 221192 | tf_op jit(solution)/shard_map/ppermute | solution.py:47
  98.0 8.1 %collective-permute-start.10 = (bf16[48,24,128]{2,1,0:T(8,128)(2,1)S(1)}, bf16[48,24,128]{2,1,0:T(8,128)(2,1)S(1)}, u32[]{:S(2)}, u32[]{:S(2)}) collective-permute-start(bf16[48,24,128]{2,1,0:T(8,128)(2,1)S(1)} %widen_rows.1.wide), channel_id=1, source_target_pairs={{0,240},{16,0},{32,16},{48,32},{64,48},{80,64},{96,80},{112,96},{1... | collective-permute-start | bytes 884744 | tf_op jit(solution)/shard_map/ppermute | solution.py:37
  110.9 29.6 %copy-start.1 = (bf16[16,24,576]{2,1,0:T(8,128)(2,1)S(1)}, bf16[16,24,576]{2,1,0:T(8,128)(2,1)}, u32[]{:S(2)}) copy-start(bf16[16,24,576]{2,1,0:T(8,128)(2,1)} %orbitals.3) | copy-start | bytes 1327108
  110.9 29.6 %copy-start.3 = (s32[16,3]{0,1:T(4,128)S(1)}, s32[16,3]{0,1:T(4,128)}, u32[]{:S(2)}) copy-start(s32[16,3]{0,1:T(4,128)} %param.12) | copy-start | bytes 580
  110.9 29.6 %all-to-all-start.1 = ((bf16[16,216,128]{2,1,0:T(8,128)(2,1)}), bf16[16,216,128]{2,1,0:T(8,128)(2,1)S(1)}, u32[]{:S(2)}, u32[]{:S(2)}) async-start(bf16[16,216,128]{2,1,0:T(8,128)(2,1)} %cut_windows.1), calls=%async_computation.1 | async-start | bytes 1769472 | tf_op jit(solution)/shard_map/all_to_all | solution.py:528

commit v3 on v2

--- a/solution.py
+++ b/solution.py
@@ -15,11 +15,13 @@
 CAP = 2
 SLABS = 16
 HELD = 16
-HALO = 8
-PLANES = CZ + 2 * HALO
+FIRST_PLANE = 10
+PLANES = 40
+ABOVE = PLANES - CZ
 HALF = CY // 2
 ROWS = HALF + 2 * RAD
-REACH = CY + RAD
+REACH = CY + 2 * RAD
+EDGE = REACH // 2
 MAIN = 96
 TAIL = CAP * MAIN
 BLOCK_ROWS = 224
@@ -37,10 +39,10 @@
     return lax.ppermute(x, axis, [(i, (i + by) % count) for i in range(count)])
 
 
-def crossed(x, by):
+def across_rows(x, steps, cross):
     tiles, owners = lax.axis_size("gy"), lax.axis_size("orb")
     pairs = [
-        (tile * owners + orb, (tile + by) % tiles * owners + (orb + 1) % owners)
+        (tile * owners + orb, (tile + steps[orb]) % tiles * owners + (orb + cross) % owners)
         for tile in range(tiles)
         for orb in range(owners)
     ]
@@ -120,7 +122,7 @@
     return copy
 
 
-def deposit_body(received, own, next_up, second_up, next_down, offsets_out, grid, rows, offsets, sem):
+def deposit_body(received, own, next_up, next_down, offsets_out, grid, rows, offsets, sem):
     copy = read_offsets(received, rows, offsets, sem)
     offsets_out[...] = rows[...]
     grid[...] = jnp.zeros(grid.shape, f32)
@@ -155,10 +157,9 @@
         return carry
 
     lax.fori_loop(0, SLABS, source_step, 0)
-    own[...] = grid[:, : PLANES - HALO, :]
-    next_up[...] = grid[:, CZ - HALO :, :].astype(bf16)
-    second_up[...] = grid[:, 2 * CZ - HALO :, :].astype(bf16)
-    next_down[...] = grid[:, :HALO, :].astype(bf16)
+    own[...] = grid[:, :PLANES, :]
+    next_up[...] = grid[:, CZ:, :].astype(bf16)
+    next_down[...] = grid[:, :ABOVE, :].astype(bf16)
 
 
 def deposit(received):
@@ -166,14 +167,13 @@
         deposit_body,
         name="deposit_boxes",
         out_shape=(
-            jax.ShapeDtypeStruct((CY + BOX, PLANES - HALO, NX), f32),
-            jax.ShapeDtypeStruct((CY + BOX, PLANES - HALO, NX), bf16),
-            jax.ShapeDtypeStruct((CY + BOX, HALO, NX), bf16),
-            jax.ShapeDtypeStruct((CY + BOX, HALO, NX), bf16),
+            jax.ShapeDtypeStruct((CY + BOX, PLANES, NX), f32),
+            jax.ShapeDtypeStruct((CY + BOX, BOX, NX), bf16),
+            jax.ShapeDtypeStruct((CY + BOX, ABOVE, NX), bf16),
             jax.ShapeDtypeStruct((SLABS, NX), jnp.int32),
         ),
         in_specs=[VMEM],
-        out_specs=(VMEM,) * 5,
+        out_specs=(VMEM,) * 4,
         scratch_shapes=[
             pltpu.VMEM((CY + BOX, CZ + BOX, NX), f32),
             pltpu.VMEM((SLABS, NX), jnp.int32),
@@ -184,64 +184,39 @@
     )(received)
 
 
-def fold_planes_body(own, below, second_below, above, kept, next_right, second_right, next_left):
-    for first, last in ((0, HALO), (HALO, PLANES - HALO), (PLANES - HALO, PLANES)):
-        total = None
-        parts = []
-        if last > HALO:
-            parts.append(own[:, first - HALO : last - HALO, :])
-        if last <= PLANES - HALO:
-            parts.append(below[:, first:last, :].astype(f32))
-        if last == HALO:
-            parts.append(second_below[...].astype(f32))
-        if first == PLANES - HALO:
-            parts.append(above[...].astype(f32))
-        total = parts[0]
-        for part in parts[1:]:
-            total = total + part
-        kept[:, first:last, :] = total[:REACH]
-        next_right[:, first:last, :] = total[CY - RAD :].astype(bf16)
-        second_right[:, first:last, :] = total[2 * CY - RAD :].astype(bf16)
-        next_left[:, first:last, :] = total[:RAD].astype(bf16)
-
-
-def fold_planes(own, below, second_below, above):
+def fold_planes_body(own, below, above, kept, next_right, next_left):
+    for first, last in ((0, CZ), (CZ, PLANES)):
+        other = below[...] if first == 0 else above[...]
+        total = own[:, first:last, :] + other.astype(f32)
+        kept[:, first:last, :] = total[RAD : RAD + REACH]
+        next_right[:, first:last, :] = total[2 * CY - EDGE :].astype(bf16)
+        next_left[:, first:last, :] = total[:EDGE].astype(bf16)
+
+
+def fold_planes(own, below, above):
     return pl.pallas_call(
         fold_planes_body,
         name="fold_planes",
         out_shape=(
             jax.ShapeDtypeStruct((REACH, PLANES, NX), f32),
-            jax.ShapeDtypeStruct((REACH, PLANES, NX), bf16),
-            jax.ShapeDtypeStruct((RAD, PLANES, NX), bf16),
-            jax.ShapeDtypeStruct((RAD, PLANES, NX), bf16),
+            jax.ShapeDtypeStruct((EDGE, PLANES, NX), bf16),
+            jax.ShapeDtypeStruct((EDGE, PLANES, NX), bf16),
         ),
-        in_specs=[VMEM] * 4,
-        out_specs=(VMEM,) * 4,
-        compiler_params=ROOM,
-    )(own, below, second_below, above)
-
-
-def fold_rows_body(position, own, left, second_left, right, kept, given, total):
-    for first, last in ((0, RAD), (RAD, REACH), (REACH, REACH + RAD)):
-        parts = []
-        if last > RAD:
-            parts.append(own[first - RAD : last - RAD])
-        if last <= REACH:
-            parts.append(left[first:last].astype(f32))
-        if last == RAD:
-            parts.append(second_left[...].astype(f32))
-        if first == REACH:
-            parts.append(right[...].astype(f32))
-        row_total = parts[0]
-        for part in parts[1:]:
-            row_total = row_total + part
-        total[first:last] = row_total
+        in_specs=[VMEM] * 3,
+        out_specs=(VMEM,) * 3,
+        compiler_params=ROOM,
+    )(own, below, above)
+
+
+def fold_rows_body(position, own, left, right, kept, given, total):
+    total[:EDGE] = own[:EDGE] + left[...].astype(f32)
+    total[EDGE:] = own[EDGE:] + right[...].astype(f32)
     orb = position[0]
     kept[...] = total[pl.ds(HALF * orb, ROWS)]
     given[...] = total[pl.ds(HALF * (1 - orb), ROWS)].astype(bf16)
 
 
-def fold_rows(position, own, left, second_left, right):
+def fold_rows(position, own, left, right):
     return pl.pallas_call(
         fold_rows_body,
         name="fold_rows",
@@ -249,11 +224,11 @@
             jax.ShapeDtypeStruct((ROWS, PLANES, NX), f32),
             jax.ShapeDtypeStruct((ROWS, PLANES, NX), bf16),
         ),
-        in_specs=[SMEM] + [VMEM] * 4,
+        in_specs=[SMEM] + [VMEM] * 3,
         out_specs=(VMEM, VMEM),
-        scratch_shapes=[pltpu.VMEM((REACH + RAD, PLANES, NX), f32)],
-        compiler_params=ROOM,
-    )(position, own, left, second_left, right)
+        scratch_shapes=[pltpu.VMEM((REACH, PLANES, NX), f32)],
+        compiler_params=ROOM,
+    )(position, own, left, right)
 
 
 def model_body(
@@ -282,7 +257,7 @@
         planes[2 * pair + 1] = total[:, NX:]
         return carry
 
-    lax.fori_loop(0, ROWS // 2, plane_step, 0, unroll=2)
+    lax.fori_loop(0, ROWS // 2, plane_step, 0, unroll=4)
 
     def channel_step(channel, carry):
         weights = [taps[channel, step] for step in range(RAD + 1)]
@@ -303,7 +278,7 @@
         features[channel] = jnp.log(1.0 + smooth)
         return carry
 
-    lax.fori_loop(0, CHAN, channel_step, 0)
+    lax.fori_loop(0, CHAN, channel_step, 0, unroll=2)
 
     def cell_step(step, carry):
         start = pl.multiple_of(step * 16, 16)
@@ -340,7 +315,7 @@
         result[pl.ds(start + 8, 8), :] = value[:, NX:]
         return carry
 
-    lax.fori_loop(0, CZ * HALF // 16, cell_step, 0, unroll=3)
+    lax.fori_loop(0, CZ * HALF // 16, cell_step, 0, unroll=9)
     for part in range(CZ // 8):
         block = result[HALF * 8 * part : HALF * 8 * (part + 1), :]
         planes[:HALF, 8 * part : 8 * part + 8, :] = block.reshape(HALF, 8, NX)
@@ -378,7 +353,7 @@
 
 def model_tables(taps, w_in, b_in, w_mid, b_mid, w_out, b_out):
     out_index = jnp.arange(CZ, dtype=jnp.int32)
-    in_index = jnp.arange(PLANES, dtype=jnp.int32) - (HALO - RAD)
+    in_index = jnp.arange(PLANES, dtype=jnp.int32) - (FIRST_PLANE - RAD)
     plane = tap_table(taps, in_index[None, :] - out_index[:, None]).reshape(CHAN * CZ, PLANES)
     plane_table = jnp.concatenate(split_table(plane), axis=0)
     source = jnp.arange(NX, dtype=jnp.int32)
@@ -429,28 +404,35 @@
     )
 
 
-def widen_body(position, own, partner, next_same, next_other, wide):
+def widen_body(position, own, partner, near, far, wide, first_planes, last_planes):
     orb = position[0]
-    wide[pl.ds(HALF * orb, HALF)] = own[...]
-    wide[pl.ds(HALF * (1 - orb), HALF)] = partner[...]
-    wide[pl.ds(CY + HALF * orb, HALF)] = next_same[...]
-    wide[pl.ds(CY + HALF * (1 - orb), HALF)] = next_other[...]
-
-
-def widen(position, own, partner, next_same, next_other):
+    wide[pl.ds(HALF + HALF * orb, HALF)] = own[...]
+    wide[pl.ds(2 * HALF - HALF * orb, HALF)] = partner[...]
+    wide[pl.ds(3 * HALF * orb, HALF)] = near[...]
+    wide[pl.ds(3 * HALF - 3 * HALF * orb, HALF)] = far[...]
+    first_planes[...] = wide[:, :16, :]
+    last_planes[...] = wide[...].astype(f32)[:, CZ - 16 :, :].astype(bf16)
+
+
+def widen(position, own, partner, near, far):
     return pl.pallas_call(
         widen_body,
         name="widen_rows",
-        out_shape=jax.ShapeDtypeStruct((CY + BOX, CZ, NX), bf16),
+        out_shape=(
+            jax.ShapeDtypeStruct((CY + BOX, CZ, NX), bf16),
+            jax.ShapeDtypeStruct((CY + BOX, 16, NX), bf16),
+            jax.ShapeDtypeStruct((CY + BOX, 16, NX), bf16),
+        ),
         in_specs=[SMEM] + [VMEM] * 4,
-        out_specs=VMEM,
-        compiler_params=ROOM,
-    )(position, own, partner, next_same, next_other)
-
-
-def cut_body(offsets, wide, beyond, windows, reach):
-    reach[:, :CZ, :] = wide[...].astype(f32)
-    reach[:, CZ:, :] = beyond[...].astype(f32)
+        out_specs=(VMEM,) * 3,
+        compiler_params=ROOM,
+    )(position, own, partner, near, far)
+
+
+def cut_body(offsets, wide, below, above, windows, reach):
+    reach[:, :FIRST_PLANE, :] = below[...].astype(f32)[:, 16 - FIRST_PLANE :, :]
+    reach[:, FIRST_PLANE : FIRST_PLANE + CZ, :] = wide[...].astype(f32)
+    reach[:, FIRST_PLANE + CZ :, :] = above[...].astype(f32)[:, : BOX - FIRST_PLANE, :]
     lane = lanes(BOX)
 
     def source_step(source, carry):
@@ -479,16 +461,16 @@
     lax.fori_loop(0, SLABS, source_step, 0)
 
 
-def cut(offsets, wide, beyond):
+def cut(offsets, wide, below, above):
     return pl.pallas_call(
         cut_body,
         name="cut_windows",
         out_shape=jax.ShapeDtypeStruct((SLABS, WINDOW_ROWS, NX), bf16),
-        in_specs=[SMEM, VMEM, VMEM],
+        in_specs=[SMEM, VMEM, VMEM, VMEM],
         out_specs=VMEM,
         scratch_shapes=[pltpu.VMEM((CY + BOX, CZ + BOX, NX), f32)],
         compiler_params=ROOM,
-    )(offsets, wide, beyond)
+    )(offsets, wide, below, above)
 
 
 def apply_body(corners, windows, orbitals, applied, count):
@@ -534,23 +516,24 @@
     tables = model_tables(taps, w_in, b_in, w_mid, b_mid, w_out, b_out)
     received = exchange(pack(corners, occupation, orbitals), "gz")
     position = lax.axis_index("orb").reshape(1)
-    own, next_up, second_up, next_down, offsets = deposit(received)
-    below = shifted(next_up, "gz", 1)
-    second_below = shifted(second_up, "gz", 2)
-    above = shifted(next_down, "gz", -1)
-    kept, next_right, second_right, next_left = fold_planes(own, below, second_below, above)
-    left = crossed(next_right, 1)
-    second_left = shifted(second_right, "gy", 2)
-    right = crossed(next_left, -1)
-    kept, given = fold_rows(position, kept, left, second_left, right)
+    own, next_up, next_down, offsets = deposit(received)
+    kept, next_right, next_left = fold_planes(
+        own, shifted(next_up, "gz", 1), shifted(next_down, "gz", -1)
+    )
+    left = across_rows(next_right, (1, 1), 1)
+    right = across_rows(next_left, (-1, -1), 1)
+    kept, given = fold_rows(position, kept, left, right)
     half = model(kept, shifted(given, "orb", 1), taps, tables)
     partner = shifted(half, "orb", 1)
-    next_same = shifted(half, "gy", -1)
-    next_other = crossed(half, -1)
-    wide = widen(position, half, partner, next_same, next_other)
-    windows = cut(offsets, wide, shifted(wide, "gz", -1))
+    near = across_rows(half, (-1, 1), 1)
+    far = across_rows(half, (-1, 1), 0)
+    wide, first_planes, last_planes = widen(position, half, partner, near, far)
+    below = shifted(last_planes, "gz", 1)
+    above = shifted(first_planes, "gz", -1)
+    windows = cut(offsets, wide, below, above)
     applied = apply(corners, exchange(windows, "gz"), orbitals)
-    return jnp.transpose(wide[:CY], (1, 0, 2)), applied
+    tile = jnp.concatenate([below[:CY, 16 - FIRST_PLANE :], wide[:CY, : CZ - FIRST_PLANE]], axis=1)
+    return jnp.transpose(tile, (1, 0, 2)), applied
 
 
 def solution(mesh):

time: 144 us -> 159 us (1.10)
  local copies, waits for them, and re-layouts: 7.21 us -> 22.3 us
  other arithmetic: 3.43 us -> 8.03 us
  waiting for transfers between devices: 71.1 us -> 68.3 us
  Pallas kernels: 29.6 us -> 27.9 us
    mul x26, local copies, waits for them, and re-layouts: 1.96 us -> 12.4 us  [tap_table(): taps[:, step][:, None, None] * (distance == step).astype(f32)[None]]
    ppermute x8 -> x6, waiting for transfers between devices: 25.4 us -> 15.9 us  [shifted(): return lax.ppermute(x, axis, [(i, (i + by) % count) for i in range(count)])]
    ppermute x3 -> x4, waiting for transfers between devices: 2.57 us -> 11.6 us  [across_rows(): return lax.ppermute(x, ('gy', 'orb'), pairs)]
    ppermute x8 -> x6, starting transfers between devices: 8.27 us -> 3.14 us  [shifted(): return lax.ppermute(x, axis, [(i, (i + by) % count) for i in range(count)])]
    ppermute x3 -> x4, starting transfers between devices: 6.79 us -> 9.84 us  [across_rows(): return lax.ppermute(x, ('gy', 'orb'), pairs)]
    convert_element_type x8, other arithmetic: 0.34 us -> 2.87 us  [tap_table(): (distance == step).astype(f32)[None]]
    all_to_all x2, waiting for transfers between devices: 43.1 us -> 40.8 us  [exchange(): return lax.all_to_all(x, axis, split_axis=0, concat_axis=0, tiled=True)]
    pallas_call x1, Pallas kernels: 14.8 us -> 13 us  [model(): pl.pallas_call(model_body, name='smooth_and_network', out_shape=jax.Shape...]
  transfers between devices with their start and end apart: 13 -> 12, of which waited for: 7 -> 10; matrix products, arithmetic and copies ran while one was open for 6% -> 17% of each run, Pallas kernels for 0% -> 0%
where the time goes in v3:
time: 159 us; the launch traced here: 158 us
  waiting for transfers between devices  68.3 us (43%)
  starting transfers between devices  29.8 us (19%)
  Pallas kernels  27.9 us (18%)
  local copies, waits for them, and re-layouts  22.3 us (14%)
  other arithmetic  8.03 us (5%)
  between operations  2.16 us (1%)
    all_to_all x2, waiting for transfers between devices, exchange(): return lax.all_to_all(x, axis, split_axis=0, concat_axis=0, tiled=True)  40.8 us
    all_to_all x2, starting transfers between devices, exchange(): return lax.all_to_all(x, axis, split_axis=0, concat_axis=0, tiled=True)  16.8 us
    ppermute x6, waiting for transfers between devices, shifted(): return lax.ppermute(x, axis, [(i, (i + by) % count) for i in range(count)])  15.9 us
    pallas_call x1, Pallas kernels, model(): pl.pallas_call(model_body, name='smooth_and_network', out_shape=jax.Shape...  13 us
    mul x26, local copies, waits for them, and re-layouts, tap_table(): taps[:, step][:, None, None] * (distance == step).astype(f32)[None]  12.4 us
    ppermute x4, waiting for transfers between devices, across_rows(): return lax.ppermute(x, ('gy', 'orb'), pairs)  11.6 us
    ppermute x4, starting transfers between devices, across_rows(): return lax.ppermute(x, ('gy', 'orb'), pairs)  9.84 us
    pallas_call x1, Pallas kernels, cut(): pl.pallas_call(cut_body, name='cut_windows', out_shape=jax.ShapeDtypeStru...  4.81 us
  transfers between devices with their start and end apart: 12, of which 10 were waited for; matrix products, arithmetic and copies ran while one was open for 17% of the time, Pallas kernels for 0%

profile of v3, /device:TPU:1, one launch (start us, length us, event | category | flops | bytes accessed | tf_op | source)
XLA Modules:
  0.0 158.4 jit_solution(10971951433517285824)
XLA Ops:
  0.6 1.0 copy-done
  1.7 0.7 copy-done.2
  3.0 3.0 %pack_boxes.1 = bf16[16,224,128]{2,1,0:T(8,128)(2,1)} custom-call(s32[3,16]{1,0:T(4,128)S(1)} %bitcast.99, f32[16]{0:T(128)S(1)} %copy-done.4, bf16[16,24,576]{2,1,0:T(8,128)(2,1)S(1)} %copy-done), custom_call_target="tpu_custom_call" | custom-call | tf_op jit(solution)/shard_map/pack_boxes/pallas_call | solution.py:104
  6.0 10.1 %all-to-all-start = ((bf16[16,224,128]{2,1,0:T(8,128)(2,1)}), bf16[16,224,128]{2,1,0:T(8,128)(2,1)S(1)}, u32[]{:S(2)}, u32[]{:S(2)}) async-start(bf16[16,224,128]{2,1,0:T(8,128)(2,1)} %pack_boxes.1), calls=%async_computation | async-start | bytes 1835008 | tf_op jit(solution)/shard_map/all_to_all | solution.py:510
  16.2 0.7 compare_convert_fusion.4
  16.9 0.7 compare_convert_fusion.6
  17.6 0.7 compare_convert_fusion.12
  19.2 1.0 slice_reduce_fusion.12
  22.2 0.7 fusion.33
  22.9 0.7 subtract_convert_fusion.1
  24.4 16.9 %all-to-all-done.received = bf16[16,224,128]{2,1,0:T(8,128)(2,1)S(1)} async-done(((bf16[16,224,128]{2,1,0:T(8,128)(2,1)}), bf16[16,224,128]{2,1,0:T(8,128)(2,1)S(1)}, u32[]{:S(2)}, u32[]{:S(2)}) %all-to-all-start) | async-done | bytes 917536 | tf_op jit(solution)/shard_map/all_to_all | solution.py:510
  41.4 4.1 %deposit_boxes.1 = (f32[48,40,128]{2,1,0:T(8,128)S(1)}, bf16[48,24,128]{2,1,0:T(8,128)(2,1)S(1)}, bf16[48,16,128]{2,1,0:T(8,128)(2,1)S(1)}, s32[16,128]{1,0:T(8,128)S(1)}) custom-call(bf16[16,224,128]{2,1,0:T(8,128)(2,1)S(1)} %all-to-all-done.received), custom_call_target="tpu_custom_call" | custom-call | tf_op jit(solution)/shard_map/deposit_boxes/pallas_call | solution.py:166
  45.7 0.8 fusion.4.middle_table
  46.5 0.7 mul.603
  47.3 0.7 mul.596
  48.8 0.7 mul.582
  49.7 0.7 mul.575
  50.4 0.7 mul.568
  51.2 0.7 mul.561
  52.0 0.7 mul.554
  54.0 0.7 mul.540
  54.7 0.7 mul.541
  55.4 0.7 mul.533
  56.8 0.7 mul.526
  58.2 0.7 mul.520
  62.2 0.7 broadcast_in_dim.10
  62.9 1.2 concatenate.31.first_table
  64.3 1.1 reduce-precision_convert_fusion.1
  65.9 4.6 %collective-permute-done.1.above = bf16[48,16,128]{2,1,0:T(8,128)(2,1)S(1)} collective-permute-done((bf16[48,16,128]{2,1,0:T(8,128)(2,1)S(1)}, bf16[48,16,128]{2,1,0:T(8,128)(2,1)S(1)}, u32[]{:S(2)}, u32[]{:S(2)}) %collective-permute-start.1) | collective-permute-done | bytes 196640 | tf_op jit(solution)/shard_map/ppermute | solution.py:39
  70.6 2.6 %collective-permute-start.2 = (bf16[18,40,128]{2,1,0:T(8,128)(2,1)S(1)}, bf16[18,40,128]{2,1,0:T(8,128)(2,1)S(1)}, u32[]{:S(2)}, u32[]{:S(2)}) collective-permute-start(bf16[18,40,128]{2,1,0:T(8,128)(2,1)S(1)} %get-tuple-element.18), channel_id=1, source_target_pairs={{0,3},{1,2},{2,5},{3,4},{4,7},{5,6},{6,9},{7,8},{8,11},{9,10},{10,... | collective-permute-start | bytes 552968 | tf_op jit(solution)/shard_map/ppermute | solution.py:49
  73.2 2.5 %collective-permute-start.3 = (bf16[18,40,128]{2,1,0:T(8,128)(2,1)S(1)}, bf16[18,40,128]{2,1,0:T(8,128)(2,1)S(1)}, u32[]{:S(2)}, u32[]{:S(2)}) collective-permute-start(bf16[18,40,128]{2,1,0:T(8,128)(2,1)S(1)} %get-tuple-element.19), channel_id=1, source_target_pairs={{0,15},{1,14},{2,1},{3,0},{4,3},{5,2},{6,5},{7,4},{8,7},{9,6},{10,... | collective-permute-start | bytes 552968 | tf_op jit(solution)/shard_map/ppermute | solution.py:49
  75.7 4.8 %collective-permute-done.2.left = bf16[18,40,128]{2,1,0:T(8,128)(2,1)S(1)} collective-permute-done((bf16[18,40,128]{2,1,0:T(8,128)(2,1)S(1)}, bf16[18,40,128]{2,1,0:T(8,128)(2,1)S(1)}, u32[]{:S(2)}, u32[]{:S(2)}) %collective-permute-start.2) | collective-permute-done | bytes 184352 | tf_op jit(solution)/shard_map/ppermute | solution.py:49
  80.5 2.8 %collective-permute-done.3.right = bf16[18,40,128]{2,1,0:T(8,128)(2,1)S(1)} collective-permute-done((bf16[18,40,128]{2,1,0:T(8,128)(2,1)S(1)}, bf16[18,40,128]{2,1,0:T(8,128)(2,1)S(1)}, u32[]{:S(2)}, u32[]{:S(2)}) %collective-permute-start.3) | collective-permute-done | bytes 184352 | tf_op jit(solution)/shard_map/ppermute | solution.py:49
  83.7 7.0 %collective-permute-done.4.other = bf16[24,40,128]{2,1,0:T(8,128)(2,1)S(1)} collective-permute-done((bf16[24,40,128]{2,1,0:T(8,128)(2,1)S(1)}, bf16[24,40,128]{2,1,0:T(8,128)(2,1)S(1)}, u32[]{:S(2)}, u32[]{:S(2)}) %collective-permute-start.4) | collective-permute-done | bytes 245792 | tf_op jit(solution)/shard_map/ppermute | solution.py:39
  90.9 13.0 %smooth_and_network.1.own = bf16[12,24,128]{2,1,0:T(8,128)(2,1)S(1)} custom-call(f32[8,13]{1,0:T(8,128)S(1)} %fusion.47.taps, f32[24,40,128]{2,1,0:T(8,128)S(1)} %get-tuple-element.20.kept, bf16[24,40,128]{2,1,0:T(8,128)(2,1)S(1)} %collective-permute-done.4.other, bf16[384,40]{1,0:T(8,128)(2,1)S(1)} %pad_maximum_fusion.plane_table, ...), custom_call_target="tpu_custom_call" | custom-call | tf_op jit(solution)/shard_map/smooth_and_network/pallas_call | solution.py:326
  103.9 3.9 %collective-permute-start.6 = (bf16[12,24,128]{2,1,0:T(8,128)(2,1)S(1)}, bf16[12,24,128]{2,1,0:T(8,128)(2,1)S(1)}, u32[]{:S(2)}, u32[]{:S(2)}) collective-permute-start(bf16[12,24,128]{2,1,0:T(8,128)(2,1)S(1)} %smooth_and_network.1.own), channel_id=1, source_target_pairs={{0,15},{1,2},{2,1},{3,4},{4,3},{5,6},{6,5},{7,8},{8,7},{9,10},{10,... | collective-permute-start | bytes 221192 | tf_op jit(solution)/shard_map/ppermute | solution.py:49
  107.8 0.9 collective-permute-start.7
  108.7 1.9 %collective-permute-done.6.near = bf16[12,24,128]{2,1,0:T(8,128)(2,1)S(1)} collective-permute-done((bf16[12,24,128]{2,1,0:T(8,128)(2,1)S(1)}, bf16[12,24,128]{2,1,0:T(8,128)(2,1)S(1)}, u32[]{:S(2)}, u32[]{:S(2)}) %collective-permute-start.6) | collective-permute-done | bytes 73760 | tf_op jit(solution)/shard_map/ppermute | solution.py:49
  110.5 2.2 %collective-permute-done.7.far = bf16[12,24,128]{2,1,0:T(8,128)(2,1)S(1)} collective-permute-done((bf16[12,24,128]{2,1,0:T(8,128)(2,1)S(1)}, bf16[12,24,128]{2,1,0:T(8,128)(2,1)S(1)}, u32[]{:S(2)}, u32[]{:S(2)}) %collective-permute-start.7) | collective-permute-done | bytes 73760 | tf_op jit(solution)/shard_map/ppermute | solution.py:49
  112.8 1.3 collective-permute-start.8
  114.1 1.1 collective-permute-start.9
  115.3 1.5 collective-permute-done.8.below
  116.7 2.8 %collective-permute-done.9.above = bf16[48,16,128]{2,1,0:T(8,128)(2,1)S(1)} collective-permute-done((bf16[48,16,128]{2,1,0:T(8,128)(2,1)S(1)}, bf16[48,16,128]{2,1,0:T(8,128)(2,1)S(1)}, u32[]{:S(2)}, u32[]{:S(2)}) %collective-permute-start.9) | collective-permute-done | bytes 196640 | tf_op jit(solution)/shard_map/ppermute | solution.py:39
  119.5 4.8 %cut_windows.1 = bf16[16,216,128]{2,1,0:T(8,128)(2,1)} custom-call(s32[16,128]{1,0:T(8,128)S(1)} %get-tuple-element.24.offsets, bf16[48,24,128]{2,1,0:T(8,128)(2,1)S(1)} %get-tuple-element.23.wide, bf16[48,16,128]{2,1,0:T(8,128)(2,1)S(1)} %collective-permute-done.8.below, bf16[48,16,128]{2,1,0:T(8,128)(2,1)S(1)} %collective-permute-done.9.above), custom_call_target="tpu_custom_call" | custom-call | tf_op jit(solution)/shard_map/cut_windows/pallas_call | solution.py:465
  124.3 6.7 %all-to-all-start.1 = ((bf16[16,216,128]{2,1,0:T(8,128)(2,1)}), bf16[16,216,128]{2,1,0:T(8,128)(2,1)S(1)}, u32[]{:S(2)}, u32[]{:S(2)}) async-start(bf16[16,216,128]{2,1,0:T(8,128)(2,1)} %cut_windows.1), calls=%async_computation.1 | async-start | bytes 1769472 | tf_op jit(solution)/shard_map/all_to_all | solution.py:510
  131.1 0.7 copy.50
  131.8 23.8 %all-to-all-done.1.windows = bf16[16,216,128]{2,1,0:T(8,128)(2,1)S(1)} async-done(((bf16[16,216,128]{2,1,0:T(8,128)(2,1)}), bf16[16,216,128]{2,1,0:T(8,128)(2,1)S(1)}, u32[]{:S(2)}, u32[]{:S(2)}) %all-to-all-start.1) | async-done | bytes 884768 | tf_op jit(solution)/shard_map/all_to_all | solution.py:510
  155.7 2.7 %apply_windows.1 = bf16[16,24,576]{2,1,0:T(8,128)(2,1)} custom-call(s32[3,16]{1,0:T(4,128)S(1)} %bitcast.100, bf16[16,216,128]{2,1,0:T(8,128)(2,1)S(1)} %all-to-all-done.1.windows, bf16[16,24,576]{2,1,0:T(8,128)(2,1)S(1)} %copy-done.1), custom_call_target="tpu_custom_call" | custom-call | tf_op jit(solution)/shard_map/apply_windows/pallas_call | solution.py:498
  (156 shorter events, 12.3 us)
Async XLA Ops:
  6.0 12.3 %copy-start.39 = (f32[8,64]{1,0:T(8,128)S(1)}, f32[8,64]{1,0:T(8,128)}, u32[]{:S(2)}) copy-start(f32[8,64]{1,0:T(8,128)} %param.14) | copy-start | bytes 6148
  6.0 35.4 %all-to-all-start = ((bf16[16,224,128]{2,1,0:T(8,128)(2,1)}), bf16[16,224,128]{2,1,0:T(8,128)(2,1)S(1)}, u32[]{:S(2)}, u32[]{:S(2)}) async-start(bf16[16,224,128]{2,1,0:T(8,128)(2,1)} %pack_boxes.1), calls=%async_computation | async-start | bytes 1835008 | tf_op jit(solution)/shard_map/all_to_all | solution.py:510
  20.8 2.8 %copy-start.5 = (f32[128,128]{1,0:T(8,128)S(1)}, f32[128,128]{1,0:T(8,128)}, u32[]{:S(2)}) copy-start(f32[128,128]{1,0:T(8,128)} %get-tuple-element.79) | copy-start | bytes 196612
  20.8 2.8 %copy-start.6 = (f32[128,128]{1,0:T(8,128)S(1)}, f32[128,128]{1,0:T(8,128)}, u32[]{:S(2)}) copy-start(f32[128,128]{1,0:T(8,128)} %get-tuple-element.80) | copy-start | bytes 196612
  20.8 2.8 %copy-start.7 = (f32[128,128]{1,0:T(8,128)S(1)}, f32[128,128]{1,0:T(8,128)}, u32[]{:S(2)}) copy-start(f32[128,128]{1,0:T(8,128)} %get-tuple-element.81) | copy-start | bytes 196612
  20.8 2.8 %copy-start.8 = (f32[128,128]{1,0:T(8,128)S(1)}, f32[128,128]{1,0:T(8,128)}, u32[]{:S(2)}) copy-start(f32[128,128]{1,0:T(8,128)} %compare_convert_fusion.12) | copy-start | bytes 196612
  20.8 2.8 %copy-start.23 = (f32[8]{0:T(128)S(1)}, f32[8]{0:T(128)}, u32[]{:S(2)}) copy-start(f32[8]{0:T(128)} %get-tuple-element.38) | copy-start | bytes 100
  20.8 2.8 %copy-start.25 = (f32[8]{0:T(128)S(1)}, f32[8]{0:T(128)}, u32[]{:S(2)}) copy-start(f32[8]{0:T(128)} %get-tuple-element.50) | copy-start | bytes 100
  20.8 2.8 %copy-start.26 = (f32[8]{0:T(128)S(1)}, f32[8]{0:T(128)}, u32[]{:S(2)}) copy-start(f32[8]{0:T(128)} %get-tuple-element.49) | copy-start | bytes 100
  20.9 2.8 %copy-start.27 = (f32[8]{0:T(128)S(1)}, f32[8]{0:T(128)}, u32[]{:S(2)}) copy-start(f32[8]{0:T(128)} %get-tuple-element.48) | copy-start | bytes 100
  20.9 2.8 %copy-start.28 = (f32[8]{0:T(128)S(1)}, f32[8]{0:T(128)}, u32[]{:S(2)}) copy-start(f32[8]{0:T(128)} %get-tuple-element.47) | copy-start | bytes 100
  20.9 2.8 %copy-start.29 = (f32[8]{0:T(128)S(1)}, f32[8]{0:T(128)}, u32[]{:S(2)}) copy-start(f32[8]{0:T(128)} %get-tuple-element.46) | copy-start | bytes 100
  20.9 2.8 %copy-start.30 = (f32[8]{0:T(128)S(1)}, f32[8]{0:T(128)}, u32[]{:S(2)}) copy-start(f32[8]{0:T(128)} %get-tuple-element.45) | copy-start | bytes 100
  20.9 2.8 %copy-start.31 = (f32[8]{0:T(128)S(1)}, f32[8]{0:T(128)}, u32[]{:S(2)}) copy-start(f32[8]{0:T(128)} %get-tuple-element.44) | copy-start | bytes 100
  20.9 2.8 %copy-start.32 = (f32[8]{0:T(128)S(1)}, f32[8]{0:T(128)}, u32[]{:S(2)}) copy-start(f32[8]{0:T(128)} %get-tuple-element.43) | copy-start | bytes 100
  20.9 2.8 %copy-start.33 = (f32[8]{0:T(128)S(1)}, f32[8]{0:T(128)}, u32[]{:S(2)}) copy-start(f32[8]{0:T(128)} %get-tuple-element.42) | copy-start | bytes 100
  20.9 2.8 %copy-start.34 = (f32[8]{0:T(128)S(1)}, f32[8]{0:T(128)}, u32[]{:S(2)}) copy-start(f32[8]{0:T(128)} %get-tuple-element.41) | copy-start | bytes 100
  24.4 33.7 %copy-start.24 = (f32[8]{0:T(128)S(1)}, f32[8]{0:T(128)}, u32[]{:S(2)}) copy-start(f32[8]{0:T(128)} %get-tuple-element.38) | copy-start | bytes 100
  45.5 18.7 %copy-start.9 = (f32[24,40]{1,0:T(8,128)S(1)}, f32[24,40]{1,0:T(8,128)}, u32[]{:S(2)}) copy-start(f32[24,40]{1,0:T(8,128)} %get-tuple-element.61) | copy-start | bytes 11524
  45.5 18.7 %copy-start.10 = (f32[24,40]{1,0:T(8,128)S(1)}, f32[24,40]{1,0:T(8,128)}, u32[]{:S(2)}) copy-start(f32[24,40]{1,0:T(8,128)} %get-tuple-element.62) | copy-start | bytes 11524
  45.5 18.7 %copy-start.11 = (f32[24,40]{1,0:T(8,128)S(1)}, f32[24,40]{1,0:T(8,128)}, u32[]{:S(2)}) copy-start(f32[24,40]{1,0:T(8,128)} %get-tuple-element.63) | copy-start | bytes 11524
  45.5 18.7 %copy-start.12 = (f32[24,40]{1,0:T(8,128)S(1)}, f32[24,40]{1,0:T(8,128)}, u32[]{:S(2)}) copy-start(f32[24,40]{1,0:T(8,128)} %get-tuple-element.64) | copy-start | bytes 11524
  45.5 18.7 %copy-start.13 = (f32[24,40]{1,0:T(8,128)S(1)}, f32[24,40]{1,0:T(8,128)}, u32[]{:S(2)}) copy-start(f32[24,40]{1,0:T(8,128)} %get-tuple-element.65) | copy-start | bytes 11524
  45.5 18.7 %copy-start.14 = (f32[24,40]{1,0:T(8,128)S(1)}, f32[24,40]{1,0:T(8,128)}, u32[]{:S(2)}) copy-start(f32[24,40]{1,0:T(8,128)} %get-tuple-element.66) | copy-start | bytes 11524
  45.6 18.7 %copy-start.15 = (f32[24,40]{1,0:T(8,128)S(1)}, f32[24,40]{1,0:T(8,128)}, u32[]{:S(2)}) copy-start(f32[24,40]{1,0:T(8,128)} %get-tuple-element.67) | copy-start | bytes 11524
  45.6 18.7 %copy-start.16 = (f32[24,40]{1,0:T(8,128)S(1)}, f32[24,40]{1,0:T(8,128)}, u32[]{:S(2)}) copy-start(f32[24,40]{1,0:T(8,128)} %get-tuple-element.68) | copy-start | bytes 11524
  45.6 18.7 %copy-start.17 = (f32[24,40]{1,0:T(8,128)S(1)}, f32[24,40]{1,0:T(8,128)}, u32[]{:S(2)}) copy-start(f32[24,40]{1,0:T(8,128)} %get-tuple-element.69) | copy-start | bytes 11524
  45.6 18.7 %copy-start.18 = (f32[24,40]{1,0:T(8,128)S(1)}, f32[24,40]{1,0:T(8,128)}, u32[]{:S(2)}) copy-start(f32[24,40]{1,0:T(8,128)} %get-tuple-element.70) | copy-start | bytes 11524
  45.6 18.7 %copy-start.19 = (f32[24,40]{1,0:T(8,128)S(1)}, f32[24,40]{1,0:T(8,128)}, u32[]{:S(2)}) copy-start(f32[24,40]{1,0:T(8,128)} %get-tuple-element.71) | copy-start | bytes 11524
  45.6 18.7 %copy-start.20 = (f32[24,40]{1,0:T(8,128)S(1)}, f32[24,40]{1,0:T(8,128)}, u32[]{:S(2)}) copy-start(f32[24,40]{1,0:T(8,128)} %get-tuple-element.72) | copy-start | bytes 11524
  45.6 18.7 %copy-start.21 = (f32[24,40]{1,0:T(8,128)S(1)}, f32[24,40]{1,0:T(8,128)}, u32[]{:S(2)}) copy-start(f32[24,40]{1,0:T(8,128)} %get-tuple-element.73) | copy-start | bytes 11524
  45.6 24.9 %collective-permute-start = (bf16[48,24,128]{2,1,0:T(8,128)(2,1)S(1)}, bf16[48,24,128]{2,1,0:T(8,128)(2,1)S(1)}, u32[]{:S(2)}, u32[]{:S(2)}) collective-permute-start(bf16[48,24,128]{2,1,0:T(8,128)(2,1)S(1)} %get-tuple-element.15), channel_id=1, source_target_pairs={{0,16},{16,32},{32,48},{48,64},{64,80},{80,96},{96,112},{112,128},... | collective-permute-start | bytes 884744 | tf_op jit(solution)/shard_map/ppermute | solution.py:39
  58.2 6.1 %copy-start.37 = (f32[192]{0:T(256)S(1)}, f32[192]{0:T(256)}, u32[]{:S(2)}) copy-start(f32[192]{0:T(256)} %mul.548) | copy-start | bytes 2308
  59.0 5.3 %copy-start.38 = (f32[192]{0:T(256)S(1)}, f32[192]{0:T(256)}, u32[]{:S(2)}) copy-start(f32[192]{0:T(256)} %mul.541) | copy-start | bytes 2308
  65.4 5.1 %collective-permute-start.1 = (bf16[48,16,128]{2,1,0:T(8,128)(2,1)S(1)}, bf16[48,16,128]{2,1,0:T(8,128)(2,1)S(1)}, u32[]{:S(2)}, u32[]{:S(2)}) collective-permute-start(bf16[48,16,128]{2,1,0:T(8,128)(2,1)S(1)} %get-tuple-element.16), channel_id=1, source_target_pairs={{0,240},{16,0},{32,16},{48,32},{64,48},{80,64},{96,80},{112,96},{1... | collective-permute-start | bytes 589832 | tf_op jit(solution)/shard_map/ppermute | solution.py:39
  70.6 9.9 %collective-permute-start.2 = (bf16[18,40,128]{2,1,0:T(8,128)(2,1)S(1)}, bf16[18,40,128]{2,1,0:T(8,128)(2,1)S(1)}, u32[]{:S(2)}, u32[]{:S(2)}) collective-permute-start(bf16[18,40,128]{2,1,0:T(8,128)(2,1)S(1)} %get-tuple-element.18), channel_id=1, source_target_pairs={{0,3},{1,2},{2,5},{3,4},{4,7},{5,6},{6,9},{7,8},{8,11},{9,10},{10,... | collective-permute-start | bytes 552968 | tf_op jit(solution)/shard_map/ppermute | solution.py:49
  73.2 10.1 %collective-permute-start.3 = (bf16[18,40,128]{2,1,0:T(8,128)(2,1)S(1)}, bf16[18,40,128]{2,1,0:T(8,128)(2,1)S(1)}, u32[]{:S(2)}, u32[]{:S(2)}) collective-permute-start(bf16[18,40,128]{2,1,0:T(8,128)(2,1)S(1)} %get-tuple-element.19), channel_id=1, source_target_pairs={{0,15},{1,14},{2,1},{3,0},{4,3},{5,2},{6,5},{7,4},{8,7},{9,6},{10,... | collective-permute-start | bytes 552968 | tf_op jit(solution)/shard_map/ppermute | solution.py:49
  83.4 7.3 %copy-start.40 = (f32[128]{0:T(128)S(1)}, f32[128]{0:T(128)}, u32[]{:S(2)}) copy-start(f32[128]{0:T(128)} %broadcast_in_dim.11) | copy-start | bytes 1540
  83.4 7.3 %copy-start.41 = (f32[128]{0:T(128)S(1)}, f32[128]{0:T(128)}, u32[]{:S(2)}) copy-start(f32[128]{0:T(128)} %broadcast_in_dim.13) | copy-start | bytes 1540
  83.4 7.2 %collective-permute-start.4 = (bf16[24,40,128]{2,1,0:T(8,128)(2,1)S(1)}, bf16[24,40,128]{2,1,0:T(8,128)(2,1)S(1)}, u32[]{:S(2)}, u32[]{:S(2)}) collective-permute-start(bf16[24,40,128]{2,1,0:T(8,128)(2,1)S(1)} %get-tuple-element.21), channel_id=1, source_target_pairs={{0,1},{1,0},{2,3},{3,2},{4,5},{5,4},{6,7},{7,6},{8,9},{9,8},{10,11... | collective-permute-start | bytes 737288 | tf_op jit(solution)/shard_map/ppermute | solution.py:39
  103.8 4.9 %collective-permute-start.5 = (bf16[12,24,128]{2,1,0:T(8,128)(2,1)S(1)}, bf16[12,24,128]{2,1,0:T(8,128)(2,1)S(1)}, u32[]{:S(2)}, u32[]{:S(2)}) collective-permute-start(bf16[12,24,128]{2,1,0:T(8,128)(2,1)S(1)} %smooth_and_network.1.own), channel_id=1, source_target_pairs={{0,1},{1,0},{2,3},{3,2},{4,5},{5,4},{6,7},{7,6},{8,9},{9,8},{10,11... | collective-permute-start | bytes 221192 | tf_op jit(solution)/shard_map/ppermute | solution.py:39
  103.9 6.6 %collective-permute-start.6 = (bf16[12,24,128]{2,1,0:T(8,128)(2,1)S(1)}, bf16[12,24,128]{2,1,0:T(8,128)(2,1)S(1)}, u32[]{:S(2)}, u32[]{:S(2)}) collective-permute-start(bf16[12,24,128]{2,1,0:T(8,128)(2,1)S(1)} %smooth_and_network.1.own), channel_id=1, source_target_pairs={{0,15},{1,2},{2,1},{3,4},{4,3},{5,6},{6,5},{7,8},{8,7},{9,10},{10,... | collective-permute-start | bytes 221192 | tf_op jit(solution)/shard_map/ppermute | solution.py:49
  107.8 4.9 %collective-permute-start.7 = (bf16[12,24,128]{2,1,0:T(8,128)(2,1)S(1)}, bf16[12,24,128]{2,1,0:T(8,128)(2,1)S(1)}, u32[]{:S(2)}, u32[]{:S(2)}) collective-permute-start(bf16[12,24,128]{2,1,0:T(8,128)(2,1)S(1)} %smooth_and_network.1.own), channel_id=1, source_target_pairs={{0,14},{1,3},{2,0},{3,5},{4,2},{5,7},{6,4},{7,9},{8,6},{9,11},{10,... | collective-permute-start | bytes 221192 | tf_op jit(solution)/shard_map/ppermute | solution.py:49
  112.8 4.0 %collective-permute-start.8 = (bf16[48,16,128]{2,1,0:T(8,128)(2,1)S(1)}, bf16[48,16,128]{2,1,0:T(8,128)(2,1)S(1)}, u32[]{:S(2)}, u32[]{:S(2)}) collective-permute-start(bf16[48,16,128]{2,1,0:T(8,128)(2,1)S(1)} %get-tuple-element.22), channel_id=1, source_target_pairs={{0,16},{16,32},{32,48},{48,64},{64,80},{80,96},{96,112},{112,128},... | collective-permute-start | bytes 589832 | tf_op jit(solution)/shard_map/ppermute | solution.py:39
  114.1 5.4 %collective-permute-start.9 = (bf16[48,16,128]{2,1,0:T(8,128)(2,1)S(1)}, bf16[48,16,128]{2,1,0:T(8,128)(2,1)S(1)}, u32[]{:S(2)}, u32[]{:S(2)}) collective-permute-start(bf16[48,16,128]{2,1,0:T(8,128)(2,1)S(1)} %get-tuple-element.25), channel_id=1, source_target_pairs={{0,240},{16,0},{32,16},{48,32},{64,48},{80,64},{96,80},{112,96},{1... | collective-permute-start | bytes 589832 | tf_op jit(solution)/shard_map/ppermute | solution.py:39
  124.3 31.3 %copy-start.1 = (bf16[16,24,576]{2,1,0:T(8,128)(2,1)S(1)}, bf16[16,24,576]{2,1,0:T(8,128)(2,1)}, u32[]{:S(2)}) copy-start(bf16[16,24,576]{2,1,0:T(8,128)(2,1)} %orbitals.3) | copy-start | bytes 1327108
  124.3 31.3 %copy-start.3 = (s32[16,3]{0,1:T(4,128)S(1)}, s32[16,3]{0,1:T(4,128)}, u32[]{:S(2)}) copy-start(s32[16,3]{0,1:T(4,128)} %param.12) | copy-start | bytes 580
  124.3 31.3 %all-to-all-start.1 = ((bf16[16,216,128]{2,1,0:T(8,128)(2,1)}), bf16[16,216,128]{2,1,0:T(8,128)(2,1)S(1)}, u32[]{:S(2)}, u32[]{:S(2)}) async-start(bf16[16,216,128]{2,1,0:T(8,128)(2,1)} %cut_windows.1), calls=%async_computation.1 | async-start | bytes 1769472 | tf_op jit(solution)/shard_map/all_to_all | solution.py:510
  (9 other events, 17.9 us)

commit v4 on v3

--- a/solution.py
+++ b/solution.py
@@ -25,6 +25,7 @@
 MAIN = 96
 TAIL = CAP * MAIN
 BLOCK_ROWS = 224
+GROUP = 4
 WINDOW_ROWS = TAIL + BOX
 
 VMEM = pl.BlockSpec(memory_space=pltpu.VMEM)
@@ -63,7 +64,10 @@
     return lax.broadcasted_iota(jnp.int32, (rows, NX), 1)
 
 
-def pack_body(corners, occupation, orbitals, sent, count):
+def pack_body(corners, occupation, orbitals, sent, boxes, count, sems):
+    copies = [pltpu.make_async_copy(orbitals.at[i], boxes.at[i], sems.at[i]) for i in range(HELD)]
+    for copy in copies:
+        copy.start()
     sent[...] = jnp.zeros(sent.shape, bf16)
 
     def clear(slab, carry):
@@ -74,14 +78,14 @@
     side = lanes(32) // 64
     field = lanes(8) % 64
 
-    def place(i, carry):
+    def place(i):
         plane = corners[0, i]
         row = corners[1, i]
         column = corners[2, i]
         slab = lax.div(plane, CZ)
         rank = count[slab]
         count[slab] = rank + 1
-        values = orbitals[i].astype(f32)
+        values = boxes[i].astype(f32)
         density = occupation[i] * values * values
         main = jnp.concatenate([density[:, 128 * j : 128 * j + 128] for j in range(4)], axis=0)
         sent[slab, pl.ds(pl.multiple_of(rank * MAIN, 32), MAIN), :] = main.astype(bf16)
@@ -95,9 +99,10 @@
         fresh = jnp.concatenate([tail, offsets], axis=0)
         held = sent[slab, TAIL:BLOCK_ROWS, :].astype(f32)
         sent[slab, TAIL:BLOCK_ROWS, :] = jnp.where(side == rank, fresh, held).astype(bf16)
-        return carry
-
-    lax.fori_loop(0, HELD, place, 0)
+
+    for i in range(HELD):
+        copies[i].wait()
+        place(i)
 
 
 def pack(corners, occupation, orbitals):
@@ -105,10 +110,14 @@
         pack_body,
         name="pack_boxes",
         out_shape=jax.ShapeDtypeStruct((SLABS, BLOCK_ROWS, NX), bf16),
-        in_specs=[SMEM, SMEM, VMEM],
+        in_specs=[SMEM, SMEM, pl.BlockSpec(memory_space=pl.ANY)],
         out_specs=VMEM,
-        scratch_shapes=[pltpu.SMEM((SLABS,), jnp.int32)],
-        compiler_params=ROOM,
+        scratch_shapes=[
+            pltpu.VMEM((HELD, BOX, BOX * BOX), bf16),
+            pltpu.SMEM((SLABS,), jnp.int32),
+            pltpu.SemaphoreType.DMA((HELD,)),
+        ],
+        compiler_params=pltpu.CompilerParams(vmem_limit_bytes=60 * 1024 * 1024),
     )(corners, occupation, orbitals)
 
 
@@ -122,44 +131,44 @@
     return copy
 
 
-def deposit_body(received, own, next_up, next_down, offsets_out, grid, rows, offsets, sem):
+def deposit_body(received, own, next_up, next_down, offsets_out, grids, rows, offsets, sem):
     copy = read_offsets(received, rows, offsets, sem)
     offsets_out[...] = rows[...]
-    grid[...] = jnp.zeros(grid.shape, f32)
+    for grid in grids:
+        grid[...] = jnp.zeros(grid.shape, f32)
     copy.wait()
     lane = lanes(BOX)
 
     def source_step(source, carry):
         tail_both = received[source, TAIL:BLOCK_ROWS, :].astype(f32)[:BOX]
+        boxes = []
         for slot in range(CAP):
-            z0 = offsets[source, 64 * slot]
-            y0 = offsets[source, 64 * slot + 1]
-            x0 = offsets[source, 64 * slot + 2]
+            start = [offsets[source, 64 * slot + field] for field in range(3)]
             main = received[source, MAIN * slot : MAIN * slot + MAIN, :].astype(f32)
             tiles = [main[BOX * j : BOX * j + BOX] for j in range(4)]
             tiles.append(tail_both if slot == 0 else pltpu.roll(tail_both, 64, 1))
-            inside = ((lane - x0) & (NX - 1)) < BOX
-            for first in range(0, BOX, 8):
-                olds = [
-                    grid[y0 + b, pl.ds(z0, BOX), :] for b in range(first, first + 8)
-                ]
+            boxes.append((start, tiles, ((lane - start[2]) & (NX - 1)) < BOX))
+        for first in range(0, BOX, GROUP):
+            for slot in range(CAP):
+                (z0, y0, x0), tiles, inside = boxes[slot]
+                grid = grids[slot]
+                olds = [grid[y0 + first + k, pl.ds(z0, BOX), :] for k in range(GROUP)]
                 news = []
-                for k in range(8):
-                    b = first + k
-                    tile, left = divmod(BOX * b, NX)
+                for k in range(GROUP):
+                    tile, left = divmod(BOX * (first + k), NX)
                     piece = tiles[tile]
                     if left + BOX > NX:
                         piece = jnp.where(lane >= left, piece, tiles[tile + 1])
                     piece = pltpu.roll(piece, (x0 - left) & (NX - 1), 1)
                     news.append(olds[k] + jnp.where(inside, piece, 0.0))
-                for k in range(8):
+                for k in range(GROUP):
                     grid[y0 + first + k, pl.ds(z0, BOX), :] = news[k]
         return carry
 
     lax.fori_loop(0, SLABS, source_step, 0)
-    own[...] = grid[:, :PLANES, :]
-    next_up[...] = grid[:, CZ:, :].astype(bf16)
-    next_down[...] = grid[:, :ABOVE, :].astype(bf16)
+    own[...] = grids[0][:, :PLANES, :] + grids[1][:, :PLANES, :]
+    next_up[...] = (grids[0][:, CZ:, :] + grids[1][:, CZ:, :]).astype(bf16)
+    next_down[...] = (grids[0][:, :ABOVE, :] + grids[1][:, :ABOVE, :]).astype(bf16)
 
 
 def deposit(received):
@@ -175,7 +184,7 @@
         in_specs=[VMEM],
         out_specs=(VMEM,) * 4,
         scratch_shapes=[
-            pltpu.VMEM((CY + BOX, CZ + BOX, NX), f32),
+            [pltpu.VMEM((CY + BOX, CZ + BOX, NX), f32)] * CAP,
             pltpu.VMEM((SLABS, NX), jnp.int32),
             pltpu.SMEM((SLABS, NX), jnp.int32),
             pltpu.SemaphoreType.DMA,
@@ -338,26 +347,24 @@
     )(taps, kept, other, *tables)
 
 
-def kernel_taps(kernel_widths):
-    offsets = jnp.arange(-RAD, RAD + 1).astype(f32)
-    raw = jnp.exp(-(offsets[None, :] ** 2) / (2.0 * kernel_widths[:, None] ** 2))
-    return raw / jnp.sum(raw, axis=1, keepdims=True)
-
-
-def tap_table(taps, distance):
-    table = jnp.zeros((taps.shape[0],) + distance.shape, f32)
-    for step in range(2 * RAD + 1):
-        table = table + taps[:, step][:, None, None] * (distance == step).astype(f32)[None]
-    return table
-
-
-def model_tables(taps, w_in, b_in, w_mid, b_mid, w_out, b_out):
+def tap_weights(kernel_widths, distance):
+    width = kernel_widths.reshape((CHAN,) + (1,) * distance.ndim)
+    reach = jnp.arange(-RAD, RAD + 1).astype(f32).reshape((2 * RAD + 1,) + (1,) * distance.ndim)
+    whole = jnp.sum(jnp.exp(-(reach**2)[None] / (2.0 * width[:, None] ** 2)), axis=1)
+    far = distance.astype(f32)[None]
+    raw = jnp.where(jnp.abs(far) <= RAD, jnp.exp(-(far**2) / (2.0 * width**2)), 0.0)
+    return raw / whole
+
+
+def model_tables(kernel_widths, w_in, b_in, w_mid, b_mid, w_out, b_out):
     out_index = jnp.arange(CZ, dtype=jnp.int32)
-    in_index = jnp.arange(PLANES, dtype=jnp.int32) - (FIRST_PLANE - RAD)
-    plane = tap_table(taps, in_index[None, :] - out_index[:, None]).reshape(CHAN * CZ, PLANES)
+    in_index = jnp.arange(PLANES, dtype=jnp.int32) - FIRST_PLANE
+    plane = tap_weights(kernel_widths, in_index[None, :] - out_index[:, None])
+    plane = plane.reshape(CHAN * CZ, PLANES)
     plane_table = jnp.concatenate(split_table(plane), axis=0)
     source = jnp.arange(NX, dtype=jnp.int32)
-    column = tap_table(taps, (source[:, None] - source[None, :] + RAD) % NX)
+    around = (source[:, None] - source[None, :] + NX // 2) % NX - NX // 2
+    column = tap_weights(kernel_widths, around)
     column_high, column_low = split_table(column)
     column_table = jnp.concatenate(
         [
@@ -458,7 +465,7 @@
         windows[source] = jnp.concatenate(mains + [tail], axis=0).astype(bf16)
         return carry
 
-    lax.fori_loop(0, SLABS, source_step, 0)
+    lax.fori_loop(0, SLABS, source_step, 0, unroll=2)
 
 
 def cut(offsets, wide, below, above):
@@ -491,7 +498,7 @@
         applied[i] = (whole * orbitals[i].astype(f32)).astype(bf16)
         return carry
 
-    lax.fori_loop(0, HELD, place, 0)
+    lax.fori_loop(0, HELD, place, 0, unroll=4)
 
 
 def apply(corners, windows, orbitals):
@@ -512,9 +519,10 @@
 
 def local(orbitals, occupation, corners, kernel_widths, w_in, b_in, w_mid, b_mid, w_out, b_out):
     corners = corners.T
-    taps = kernel_taps(kernel_widths)
-    tables = model_tables(taps, w_in, b_in, w_mid, b_mid, w_out, b_out)
+    taps = tap_weights(kernel_widths, jnp.arange(-RAD, RAD + 1))
+    tables = model_tables(kernel_widths, w_in, b_in, w_mid, b_mid, w_out, b_out)
     received = exchange(pack(corners, occupation, orbitals), "gz")
+    received, taps, tables = lax.optimization_barrier((received, taps, tables))
     position = lax.axis_index("orb").reshape(1)
     own, next_up, next_down, offsets = deposit(received)
     kept, next_right, next_left = fold_planes(

time: 159 us -> 136 us (0.86)
  local copies, waits for them, and re-layouts: 22.3 us -> 3.24 us
  other arithmetic: 8.03 us -> 1.43 us
  waiting for transfers between devices: 68.3 us -> 71.3 us
    mul x26 -> x0, local copies, waits for them, and re-layouts: 12.4 us -> none  [tap_table(): taps[:, step][:, None, None] * (distance == step).astype(f32)[None]]
    all_to_all x2, waiting for transfers between devices: 40.8 us -> 45.2 us  [exchange(): return lax.all_to_all(x, axis, split_axis=0, concat_axis=0, tiled=True)]
    convert_element_type x8 -> x0, other arithmetic: 2.87 us -> none  [tap_table(): (distance == step).astype(f32)[None]]
    convert_element_type x7 -> x6, other arithmetic: 3.15 us -> 0.36 us  [split_table(): return (high.astype(bf16), (x - high).astype(bf16))]
    unnamed x91 -> x17, local copies, waits for them, and re-layouts: 3.22 us -> 0.83 us
  transfers between devices with their start and end apart: 12 -> 12, of which waited for: 10 -> 10; matrix products, arithmetic and copies ran while one was open for 17% -> 3% of each run, Pallas kernels for 0% -> 0%
where the time goes in v4:
time: 136 us; the launch traced here: 135 us
  waiting for transfers between devices  71.3 us (52%)
  starting transfers between devices  30.1 us (22%)
  Pallas kernels  27.7 us (20%)
  local copies, waits for them, and re-layouts  3.24 us (2%)
  between operations  1.67 us (1%)
  other arithmetic  1.43 us (1%)
    all_to_all x2, waiting for transfers between devices, exchange(): return lax.all_to_all(x, axis, split_axis=0, concat_axis=0, tiled=True)  45.2 us
    all_to_all x2, starting transfers between devices, exchange(): return lax.all_to_all(x, axis, split_axis=0, concat_axis=0, tiled=True)  16.4 us
    ppermute x6, waiting for transfers between devices, shifted(): return lax.ppermute(x, axis, [(i, (i + by) % count) for i in range(count)])  14.8 us
    pallas_call x1, Pallas kernels, model(): pl.pallas_call(model_body, name='smooth_and_network', out_shape=jax.Shape...  12.9 us
    ppermute x4, waiting for transfers between devices, across_rows(): return lax.ppermute(x, ('gy', 'orb'), pairs)  11.2 us
    ppermute x4, starting transfers between devices, across_rows(): return lax.ppermute(x, ('gy', 'orb'), pairs)  9.95 us
    pallas_call x1, Pallas kernels, cut(): pl.pallas_call(cut_body, name='cut_windows', out_shape=jax.ShapeDtypeStru...  4.49 us
    pallas_call x1, Pallas kernels, pack(): pl.pallas_call(pack_body, name='pack_boxes', out_shape=jax.ShapeDtypeStru...  3.81 us
  transfers between devices with their start and end apart: 12, of which 10 were waited for; matrix products, arithmetic and copies ran while one was open for 3% of the time, Pallas kernels for 0%

profile of v4, /device:TPU:1, one launch (start us, length us, event | category | flops | bytes accessed | tf_op | source)
XLA Modules:
  0.0 135.4 jit_solution(17015388463944078745)
XLA Ops:
  0.6 3.8 %pack_boxes.1 = bf16[16,224,128]{2,1,0:T(8,128)(2,1)} custom-call(s32[3,16]{1,0:T(4,128)} %bitcast.14, f32[16]{0:T(128)} %occupation.1, bf16[16,24,576]{2,1,0:T(8,128)(2,1)} %orbitals.3), custom_call_target="tpu_custom_call" | custom-call | tf_op jit(solution)/shard_map/pack_boxes/pallas_call | solution.py:109
  4.5 10.0 %all-to-all-start = ((bf16[16,224,128]{2,1,0:T(8,128)(2,1)}), bf16[16,224,128]{2,1,0:T(8,128)(2,1)S(1)}, u32[]{:S(2)}, u32[]{:S(2)}) async-start(bf16[16,224,128]{2,1,0:T(8,128)(2,1)} %pack_boxes.1), calls=%async_computation | async-start | bytes 1835008 | tf_op jit(solution)/shard_map/all_to_all | solution.py:517
  14.6 0.1 broadcast_multiply_fusion
  14.7 0.1 mul.76
  14.9 0.1 copy.49
  15.0 0.1 copy-done.4
  15.2 0.1 copy.51
  15.4 0.2 fusion.15
  15.7 0.1 div.142
  15.8 0.1 div.135
  16.0 0.1 copy.47
  16.1 0.1 copy.48
  16.2 0.1 copy.52
  16.4 0.2 copy.53
  16.7 0.1 broadcast_multiply_fusion.1
  16.8 0.1 mul.84
  17.0 0.1 broadcast_in_dim.81
  17.2 0.3 concatenate.31.first_table
  17.6 0.2 fusion.14
  17.9 0.2 fusion.4
  18.2 0.1 fusion.1.column_table
  18.4 21.4 %all-to-all-done.received = bf16[16,224,128]{2,1,0:T(8,128)(2,1)S(1)} async-done(((bf16[16,224,128]{2,1,0:T(8,128)(2,1)}), bf16[16,224,128]{2,1,0:T(8,128)(2,1)S(1)}, u32[]{:S(2)}, u32[]{:S(2)}) %all-to-all-start) | async-done | bytes 917536 | tf_op jit(solution)/shard_map/all_to_all | solution.py:517
  39.9 3.6 %deposit_boxes.1 = (f32[48,40,128]{2,1,0:T(8,128)S(1)}, bf16[48,24,128]{2,1,0:T(8,128)(2,1)S(1)}, bf16[48,16,128]{2,1,0:T(8,128)(2,1)S(1)}, s32[16,128]{1,0:T(8,128)S(1)}) custom-call(bf16[16,224,128]{2,1,0:T(8,128)(2,1)S(1)} %all-to-all-done.received), custom_call_target="tpu_custom_call" | custom-call | tf_op jit(solution)/shard_map/deposit_boxes/pallas_call | solution.py:175
  43.6 0.5 collective-permute-start.1
  44.1 4.9 %collective-permute-done.1.above = bf16[48,16,128]{2,1,0:T(8,128)(2,1)S(1)} collective-permute-done((bf16[48,16,128]{2,1,0:T(8,128)(2,1)S(1)}, bf16[48,16,128]{2,1,0:T(8,128)(2,1)S(1)}, u32[]{:S(2)}, u32[]{:S(2)}) %collective-permute-start.1) | collective-permute-done | bytes 196640 | tf_op jit(solution)/shard_map/ppermute | solution.py:40
  49.0 0.1 fold_planes.1
  49.1 2.5 %collective-permute-start.2 = (bf16[18,40,128]{2,1,0:T(8,128)(2,1)S(1)}, bf16[18,40,128]{2,1,0:T(8,128)(2,1)S(1)}, u32[]{:S(2)}, u32[]{:S(2)}) collective-permute-start(bf16[18,40,128]{2,1,0:T(8,128)(2,1)S(1)} %get-tuple-element.29), channel_id=1, source_target_pairs={{0,3},{1,2},{2,5},{3,4},{4,7},{5,6},{6,9},{7,8},{8,11},{9,10},{10,... | collective-permute-start | bytes 552968 | tf_op jit(solution)/shard_map/ppermute | solution.py:50
  51.6 2.6 %collective-permute-start.3 = (bf16[18,40,128]{2,1,0:T(8,128)(2,1)S(1)}, bf16[18,40,128]{2,1,0:T(8,128)(2,1)S(1)}, u32[]{:S(2)}, u32[]{:S(2)}) collective-permute-start(bf16[18,40,128]{2,1,0:T(8,128)(2,1)S(1)} %get-tuple-element.30), channel_id=1, source_target_pairs={{0,15},{1,14},{2,1},{3,0},{4,3},{5,2},{6,5},{7,4},{8,7},{9,6},{10,... | collective-permute-start | bytes 552968 | tf_op jit(solution)/shard_map/ppermute | solution.py:50
  54.2 4.4 %collective-permute-done.2.left = bf16[18,40,128]{2,1,0:T(8,128)(2,1)S(1)} collective-permute-done((bf16[18,40,128]{2,1,0:T(8,128)(2,1)S(1)}, bf16[18,40,128]{2,1,0:T(8,128)(2,1)S(1)}, u32[]{:S(2)}, u32[]{:S(2)}) %collective-permute-start.2) | collective-permute-done | bytes 184352 | tf_op jit(solution)/shard_map/ppermute | solution.py:50
  58.6 2.5 %collective-permute-done.3.right = bf16[18,40,128]{2,1,0:T(8,128)(2,1)S(1)} collective-permute-done((bf16[18,40,128]{2,1,0:T(8,128)(2,1)S(1)}, bf16[18,40,128]{2,1,0:T(8,128)(2,1)S(1)}, u32[]{:S(2)}, u32[]{:S(2)}) %collective-permute-start.3) | collective-permute-done | bytes 184352 | tf_op jit(solution)/shard_map/ppermute | solution.py:50
  61.1 0.8 fold_rows.1
  62.6 0.1 copy.55.plane_table
  62.8 5.6 %collective-permute-done.4.other = bf16[24,40,128]{2,1,0:T(8,128)(2,1)S(1)} collective-permute-done((bf16[24,40,128]{2,1,0:T(8,128)(2,1)}, bf16[24,40,128]{2,1,0:T(8,128)(2,1)S(1)}, u32[]{:S(2)}, u32[]{:S(2)}) %collective-permute-start.4) | collective-permute-done | bytes 245792 | tf_op jit(solution)/shard_map/ppermute | solution.py:40
  68.4 12.9 %smooth_and_network.1.own = bf16[12,24,128]{2,1,0:T(8,128)(2,1)S(1)} custom-call(f32[8,13]{1,0:T(8,128)S(1)} %fusion.13.taps, f32[24,40,128]{2,1,0:T(8,128)S(1)} %get-tuple-element.31.kept, bf16[24,40,128]{2,1,0:T(8,128)(2,1)S(1)} %collective-permute-done.4.other, bf16[384,40]{1,0:T(8,128)(2,1)S(1)} %copy.55.plane_table, ...), custom_call_target="tpu_custom_call" | custom-call | tf_op jit(solution)/shard_map/smooth_and_network/pallas_call | solution.py:335
  81.3 0.1 collective-permute-start.5
  81.5 3.8 %collective-permute-start.6 = (bf16[12,24,128]{2,1,0:T(8,128)(2,1)S(1)}, bf16[12,24,128]{2,1,0:T(8,128)(2,1)S(1)}, u32[]{:S(2)}, u32[]{:S(2)}) collective-permute-start(bf16[12,24,128]{2,1,0:T(8,128)(2,1)S(1)} %smooth_and_network.1.own), channel_id=1, source_target_pairs={{0,15},{1,2},{2,1},{3,4},{4,3},{5,6},{6,5},{7,8},{8,7},{9,10},{10,... | collective-permute-start | bytes 221192 | tf_op jit(solution)/shard_map/ppermute | solution.py:50
  85.3 1.0 collective-permute-start.7
  86.3 1.7 %collective-permute-done.6.near = bf16[12,24,128]{2,1,0:T(8,128)(2,1)S(1)} collective-permute-done((bf16[12,24,128]{2,1,0:T(8,128)(2,1)S(1)}, bf16[12,24,128]{2,1,0:T(8,128)(2,1)S(1)}, u32[]{:S(2)}, u32[]{:S(2)}) %collective-permute-start.6) | collective-permute-done | bytes 73760 | tf_op jit(solution)/shard_map/ppermute | solution.py:50
  88.1 2.5 %collective-permute-done.7.far = bf16[12,24,128]{2,1,0:T(8,128)(2,1)S(1)} collective-permute-done((bf16[12,24,128]{2,1,0:T(8,128)(2,1)S(1)}, bf16[12,24,128]{2,1,0:T(8,128)(2,1)S(1)}, u32[]{:S(2)}, u32[]{:S(2)}) %collective-permute-start.7) | collective-permute-done | bytes 73760 | tf_op jit(solution)/shard_map/ppermute | solution.py:50
  90.6 2.0 %collective-permute-start.8 = (bf16[48,16,128]{2,1,0:T(8,128)(2,1)S(1)}, bf16[48,16,128]{2,1,0:T(8,128)(2,1)S(1)}, u32[]{:S(2)}, u32[]{:S(2)}) collective-permute-start(bf16[48,16,128]{2,1,0:T(8,128)(2,1)S(1)} %get-tuple-element.40), channel_id=1, source_target_pairs={{0,16},{16,32},{32,48},{48,64},{64,80},{80,96},{96,112},{112,128},... | collective-permute-start | bytes 589832 | tf_op jit(solution)/shard_map/ppermute | solution.py:40
  92.6 1.1 collective-permute-start.9
  93.7 1.5 %collective-permute-done.8.below = bf16[48,16,128]{2,1,0:T(8,128)(2,1)S(1)} collective-permute-done((bf16[48,16,128]{2,1,0:T(8,128)(2,1)S(1)}, bf16[48,16,128]{2,1,0:T(8,128)(2,1)S(1)}, u32[]{:S(2)}, u32[]{:S(2)}) %collective-permute-start.8) | collective-permute-done | bytes 196640 | tf_op jit(solution)/shard_map/ppermute | solution.py:40
  95.2 2.8 %collective-permute-done.9.above = bf16[48,16,128]{2,1,0:T(8,128)(2,1)S(1)} collective-permute-done((bf16[48,16,128]{2,1,0:T(8,128)(2,1)S(1)}, bf16[48,16,128]{2,1,0:T(8,128)(2,1)S(1)}, u32[]{:S(2)}, u32[]{:S(2)}) %collective-permute-start.9) | collective-permute-done | bytes 196640 | tf_op jit(solution)/shard_map/ppermute | solution.py:40
  98.0 4.5 %cut_windows.1 = bf16[16,216,128]{2,1,0:T(8,128)(2,1)} custom-call(s32[16,128]{1,0:T(8,128)S(1)} %get-tuple-element.42.offsets, bf16[48,24,128]{2,1,0:T(8,128)(2,1)S(1)} %get-tuple-element.41.wide, bf16[48,16,128]{2,1,0:T(8,128)(2,1)S(1)} %collective-permute-done.8.below, bf16[48,16,128]{2,1,0:T(8,128)(2,1)S(1)} %collective-permute-done.9.above), custom_call_target="tpu_custom_call" | custom-call | tf_op jit(solution)/shard_map/cut_windows/pallas_call | solution.py:472
  102.5 6.4 %all-to-all-start.1 = ((bf16[16,216,128]{2,1,0:T(8,128)(2,1)}), bf16[16,216,128]{2,1,0:T(8,128)(2,1)S(1)}, u32[]{:S(2)}, u32[]{:S(2)}) async-start(bf16[16,216,128]{2,1,0:T(8,128)(2,1)} %cut_windows.1), calls=%async_computation.1 | async-start | bytes 1769472 | tf_op jit(solution)/shard_map/all_to_all | solution.py:517
  109.0 0.7 copy.56
  109.7 23.8 %all-to-all-done.1.windows = bf16[16,216,128]{2,1,0:T(8,128)(2,1)S(1)} async-done(((bf16[16,216,128]{2,1,0:T(8,128)(2,1)}), bf16[16,216,128]{2,1,0:T(8,128)(2,1)S(1)}, u32[]{:S(2)}, u32[]{:S(2)}) %all-to-all-start.1) | async-done | bytes 884768 | tf_op jit(solution)/shard_map/all_to_all | solution.py:517
  133.6 1.8 %apply_windows.1 = bf16[16,24,576]{2,1,0:T(8,128)(2,1)} custom-call(s32[3,16]{1,0:T(4,128)S(1)} %bitcast.15, bf16[16,216,128]{2,1,0:T(8,128)(2,1)S(1)} %all-to-all-done.1.windows, bf16[16,24,576]{2,1,0:T(8,128)(2,1)S(1)} %copy-done), custom_call_target="tpu_custom_call" | custom-call | tf_op jit(solution)/shard_map/apply_windows/pallas_call | solution.py:505
  (61 shorter events, 1.4 us)
Async XLA Ops:
  4.4 10.2 %copy-start.3 = (f32[8,64]{1,0:T(8,128)S(1)}, f32[8,64]{1,0:T(8,128)}, u32[]{:S(2)}) copy-start(f32[8,64]{1,0:T(8,128)} %param.14) | copy-start | bytes 6148
  4.5 35.3 %all-to-all-start = ((bf16[16,224,128]{2,1,0:T(8,128)(2,1)}), bf16[16,224,128]{2,1,0:T(8,128)(2,1)S(1)}, u32[]{:S(2)}, u32[]{:S(2)}) async-start(bf16[16,224,128]{2,1,0:T(8,128)(2,1)} %pack_boxes.1), calls=%async_computation | async-start | bytes 1835008 | tf_op jit(solution)/shard_map/all_to_all | solution.py:517
  14.5 0.7 copy-start.4
  14.5 0.9 copy-start.5
  14.8 1.7 %copy-start.2 = (f32[64,64]{1,0:T(8,128)S(1)}, f32[64,64]{1,0:T(8,128)}, u32[]{:S(2)}) copy-start(f32[64,64]{1,0:T(8,128)} %param.16) | copy-start | bytes 49156
  15.1 1.8 %copy-start.6 = (f32[64]{0:T(128)S(1)}, f32[64]{0:T(128)}, u32[]{:S(2)}) copy-start(f32[64]{0:T(128)} %param.17) | copy-start | bytes 772
  15.1 1.9 %copy-start.7 = (f32[64]{0:T(128)S(1)}, f32[64]{0:T(128)}, u32[]{:S(2)}) copy-start(f32[64]{0:T(128)} %param.18) | copy-start | bytes 772
  43.5 5.4 %collective-permute-start = (bf16[48,24,128]{2,1,0:T(8,128)(2,1)S(1)}, bf16[48,24,128]{2,1,0:T(8,128)(2,1)S(1)}, u32[]{:S(2)}, u32[]{:S(2)}) collective-permute-start(bf16[48,24,128]{2,1,0:T(8,128)(2,1)S(1)} %get-tuple-element.26), channel_id=1, source_target_pairs={{0,16},{16,32},{32,48},{48,64},{64,80},{80,96},{96,112},{112,128},... | collective-permute-start | bytes 884744 | tf_op jit(solution)/shard_map/ppermute | solution.py:40
  43.6 5.4 %collective-permute-start.1 = (bf16[48,16,128]{2,1,0:T(8,128)(2,1)S(1)}, bf16[48,16,128]{2,1,0:T(8,128)(2,1)S(1)}, u32[]{:S(2)}, u32[]{:S(2)}) collective-permute-start(bf16[48,16,128]{2,1,0:T(8,128)(2,1)S(1)} %get-tuple-element.27), channel_id=1, source_target_pairs={{0,240},{16,0},{32,16},{48,32},{64,48},{80,64},{96,80},{112,96},{1... | collective-permute-start | bytes 589832 | tf_op jit(solution)/shard_map/ppermute | solution.py:40
  49.1 9.6 %collective-permute-start.2 = (bf16[18,40,128]{2,1,0:T(8,128)(2,1)S(1)}, bf16[18,40,128]{2,1,0:T(8,128)(2,1)S(1)}, u32[]{:S(2)}, u32[]{:S(2)}) collective-permute-start(bf16[18,40,128]{2,1,0:T(8,128)(2,1)S(1)} %get-tuple-element.29), channel_id=1, source_target_pairs={{0,3},{1,2},{2,5},{3,4},{4,7},{5,6},{6,9},{7,8},{8,11},{9,10},{10,... | collective-permute-start | bytes 552968 | tf_op jit(solution)/shard_map/ppermute | solution.py:50
  51.6 9.5 %collective-permute-start.3 = (bf16[18,40,128]{2,1,0:T(8,128)(2,1)S(1)}, bf16[18,40,128]{2,1,0:T(8,128)(2,1)S(1)}, u32[]{:S(2)}, u32[]{:S(2)}) collective-permute-start(bf16[18,40,128]{2,1,0:T(8,128)(2,1)S(1)} %get-tuple-element.30), channel_id=1, source_target_pairs={{0,15},{1,14},{2,1},{3,0},{4,3},{5,2},{6,5},{7,4},{8,7},{9,6},{10,... | collective-permute-start | bytes 552968 | tf_op jit(solution)/shard_map/ppermute | solution.py:50
  62.0 6.4 %collective-permute-start.4 = (bf16[24,40,128]{2,1,0:T(8,128)(2,1)}, bf16[24,40,128]{2,1,0:T(8,128)(2,1)S(1)}, u32[]{:S(2)}, u32[]{:S(2)}) collective-permute-start(bf16[24,40,128]{2,1,0:T(8,128)(2,1)} %get-tuple-element.32), channel_id=1, source_target_pairs={{0,1},{1,0},{2,3},{3,2},{4,5},{5,4},{6,7},{7,6},{8,9},{9,8},{10,11... | collective-permute-start | bytes 737288 | tf_op jit(solution)/shard_map/ppermute | solution.py:40
  81.3 5.0 %collective-permute-start.5 = (bf16[12,24,128]{2,1,0:T(8,128)(2,1)S(1)}, bf16[12,24,128]{2,1,0:T(8,128)(2,1)S(1)}, u32[]{:S(2)}, u32[]{:S(2)}) collective-permute-start(bf16[12,24,128]{2,1,0:T(8,128)(2,1)S(1)} %smooth_and_network.1.own), channel_id=1, source_target_pairs={{0,1},{1,0},{2,3},{3,2},{4,5},{5,4},{6,7},{7,6},{8,9},{9,8},{10,11... | collective-permute-start | bytes 221192 | tf_op jit(solution)/shard_map/ppermute | solution.py:40
  81.5 6.6 %collective-permute-start.6 = (bf16[12,24,128]{2,1,0:T(8,128)(2,1)S(1)}, bf16[12,24,128]{2,1,0:T(8,128)(2,1)S(1)}, u32[]{:S(2)}, u32[]{:S(2)}) collective-permute-start(bf16[12,24,128]{2,1,0:T(8,128)(2,1)S(1)} %smooth_and_network.1.own), channel_id=1, source_target_pairs={{0,15},{1,2},{2,1},{3,4},{4,3},{5,6},{6,5},{7,8},{8,7},{9,10},{10,... | collective-permute-start | bytes 221192 | tf_op jit(solution)/shard_map/ppermute | solution.py:50
  85.3 5.2 %collective-permute-start.7 = (bf16[12,24,128]{2,1,0:T(8,128)(2,1)S(1)}, bf16[12,24,128]{2,1,0:T(8,128)(2,1)S(1)}, u32[]{:S(2)}, u32[]{:S(2)}) collective-permute-start(bf16[12,24,128]{2,1,0:T(8,128)(2,1)S(1)} %smooth_and_network.1.own), channel_id=1, source_target_pairs={{0,14},{1,3},{2,0},{3,5},{4,2},{5,7},{6,4},{7,9},{8,6},{9,11},{10,... | collective-permute-start | bytes 221192 | tf_op jit(solution)/shard_map/ppermute | solution.py:50
  90.6 4.6 %collective-permute-start.8 = (bf16[48,16,128]{2,1,0:T(8,128)(2,1)S(1)}, bf16[48,16,128]{2,1,0:T(8,128)(2,1)S(1)}, u32[]{:S(2)}, u32[]{:S(2)}) collective-permute-start(bf16[48,16,128]{2,1,0:T(8,128)(2,1)S(1)} %get-tuple-element.40), channel_id=1, source_target_pairs={{0,16},{16,32},{32,48},{48,64},{64,80},{80,96},{96,112},{112,128},... | collective-permute-start | bytes 589832 | tf_op jit(solution)/shard_map/ppermute | solution.py:40
  92.6 5.4 %collective-permute-start.9 = (bf16[48,16,128]{2,1,0:T(8,128)(2,1)S(1)}, bf16[48,16,128]{2,1,0:T(8,128)(2,1)S(1)}, u32[]{:S(2)}, u32[]{:S(2)}) collective-permute-start(bf16[48,16,128]{2,1,0:T(8,128)(2,1)S(1)} %get-tuple-element.43), channel_id=1, source_target_pairs={{0,240},{16,0},{32,16},{48,32},{64,48},{80,64},{96,80},{112,96},{1... | collective-permute-start | bytes 589832 | tf_op jit(solution)/shard_map/ppermute | solution.py:40
  102.5 31.1 %copy-start = (bf16[16,24,576]{2,1,0:T(8,128)(2,1)S(1)}, bf16[16,24,576]{2,1,0:T(8,128)(2,1)}, u32[]{:S(2)}) copy-start(bf16[16,24,576]{2,1,0:T(8,128)(2,1)} %orbitals.3) | copy-start | bytes 1327108
  102.5 31.1 %copy-start.1 = (s32[16,3]{0,1:T(4,128)S(1)}, s32[16,3]{0,1:T(4,128)}, u32[]{:S(2)}) copy-start(s32[16,3]{0,1:T(4,128)} %param.12) | copy-start | bytes 580
  102.5 31.1 %all-to-all-start.1 = ((bf16[16,216,128]{2,1,0:T(8,128)(2,1)}), bf16[16,216,128]{2,1,0:T(8,128)(2,1)S(1)}, u32[]{:S(2)}, u32[]{:S(2)}) async-start(bf16[16,216,128]{2,1,0:T(8,128)(2,1)} %cut_windows.1), calls=%async_computation.1 | async-start | bytes 1769472 | tf_op jit(solution)/shard_map/all_to_all | solution.py:517

commit v5 on v4

--- a/solution.py
+++ b/solution.py
@@ -26,6 +26,7 @@
 TAIL = CAP * MAIN
 BLOCK_ROWS = 224
 GROUP = 4
+PART = 4
 WINDOW_ROWS = TAIL + BOX
 
 VMEM = pl.BlockSpec(memory_space=pltpu.VMEM)
@@ -65,7 +66,12 @@
 
 
 def pack_body(corners, occupation, orbitals, sent, boxes, count, sems):
-    copies = [pltpu.make_async_copy(orbitals.at[i], boxes.at[i], sems.at[i]) for i in range(HELD)]
+    copies = [
+        pltpu.make_async_copy(
+            orbitals.at[pl.ds(PART * i, PART)], boxes.at[pl.ds(PART * i, PART)], sems.at[i]
+        )
+        for i in range(HELD // PART)
+    ]
     for copy in copies:
         copy.start()
     sent[...] = jnp.zeros(sent.shape, bf16)
@@ -101,7 +107,8 @@
         sent[slab, TAIL:BLOCK_ROWS, :] = jnp.where(side == rank, fresh, held).astype(bf16)
 
     for i in range(HELD):
-        copies[i].wait()
+        if i % PART == 0:
+            copies[i // PART].wait()
         place(i)
 
 
@@ -115,7 +122,7 @@
         scratch_shapes=[
             pltpu.VMEM((HELD, BOX, BOX * BOX), bf16),
             pltpu.SMEM((SLABS,), jnp.int32),
-            pltpu.SemaphoreType.DMA((HELD,)),
+            pltpu.SemaphoreType.DMA((HELD // PART,)),
         ],
         compiler_params=pltpu.CompilerParams(vmem_limit_bytes=60 * 1024 * 1024),
     )(corners, occupation, orbitals)
@@ -266,7 +273,7 @@
         planes[2 * pair + 1] = total[:, NX:]
         return carry
 
-    lax.fori_loop(0, ROWS // 2, plane_step, 0, unroll=4)
+    lax.fori_loop(0, ROWS // 2, plane_step, 0, unroll=12)
 
     def channel_step(channel, carry):
         weights = [taps[channel, step] for step in range(RAD + 1)]
@@ -287,7 +294,7 @@
         features[channel] = jnp.log(1.0 + smooth)
         return carry
 
-    lax.fori_loop(0, CHAN, channel_step, 0, unroll=2)
+    lax.fori_loop(0, CHAN, channel_step, 0, unroll=8)
 
     def cell_step(step, carry):
         start = pl.multiple_of(step * 16, 16)
@@ -411,7 +418,7 @@
     )
 
 
-def widen_body(position, own, partner, near, far, wide, first_planes, last_planes):
+def widen_body(position, far, near, partner, own, wide, first_planes, last_planes):
     orb = position[0]
     wide[pl.ds(HALF + HALF * orb, HALF)] = own[...]
     wide[pl.ds(2 * HALF - HALF * orb, HALF)] = partner[...]
@@ -421,7 +428,7 @@
     last_planes[...] = wide[...].astype(f32)[:, CZ - 16 :, :].astype(bf16)
 
 
-def widen(position, own, partner, near, far):
+def widen(position, far, near, partner, own):
     return pl.pallas_call(
         widen_body,
         name="widen_rows",
@@ -433,19 +440,22 @@
         in_specs=[SMEM] + [VMEM] * 4,
         out_specs=(VMEM,) * 3,
         compiler_params=ROOM,
-    )(position, own, partner, near, far)
-
-
-def cut_body(offsets, wide, below, above, windows, reach):
-    reach[:, :FIRST_PLANE, :] = below[...].astype(f32)[:, 16 - FIRST_PLANE :, :]
-    reach[:, FIRST_PLANE : FIRST_PLANE + CZ, :] = wide[...].astype(f32)
-    reach[:, FIRST_PLANE + CZ :, :] = above[...].astype(f32)[:, : BOX - FIRST_PLANE, :]
+    )(position, far, near, partner, own)
+
+
+def cut_body(rows, wide, below, above, windows, reach, cuts, offsets, offsets_sem, sems):
+    fetch = pltpu.make_async_copy(rows, offsets, offsets_sem)
+    fetch.start()
+    reach[:, :16, :] = below[...].astype(f32)
+    reach[:, 16 : 16 + CZ, :] = wide[...].astype(f32)
+    reach[:, 16 + CZ :, :] = above[...].astype(f32)
+    fetch.wait()
     lane = lanes(BOX)
 
     def source_step(source, carry):
         mains, tails = [], []
         for slot in range(CAP):
-            z0 = offsets[source, 64 * slot]
+            z0 = offsets[source, 64 * slot] + 16 - FIRST_PLANE
             y0 = offsets[source, 64 * slot + 1]
             x0 = offsets[source, 64 * slot + 2]
             tiles = [None] * 5
@@ -462,10 +472,19 @@
             mains += tiles[:4]
             tails.append(tiles[4])
         tail = jnp.where(lane < 64, tails[0], pltpu.roll(tails[1], 64, 1))
-        windows[source] = jnp.concatenate(mains + [tail], axis=0).astype(bf16)
-        return carry
-
-    lax.fori_loop(0, SLABS, source_step, 0, unroll=2)
+        cuts[source] = jnp.concatenate(mains + [tail], axis=0).astype(bf16)
+        return carry
+
+    copies = []
+    for first in range(0, SLABS, PART):
+        lax.fori_loop(first, first + PART, source_step, 0, unroll=2)
+        copy = pltpu.make_async_copy(
+            cuts.at[pl.ds(first, PART)], windows.at[pl.ds(first, PART)], sems.at[first // PART]
+        )
+        copy.start()
+        copies.append(copy)
+    for copy in copies:
+        copy.wait()
 
 
 def cut(offsets, wide, below, above):
@@ -473,9 +492,15 @@
         cut_body,
         name="cut_windows",
         out_shape=jax.ShapeDtypeStruct((SLABS, WINDOW_ROWS, NX), bf16),
-        in_specs=[SMEM, VMEM, VMEM, VMEM],
-        out_specs=VMEM,
-        scratch_shapes=[pltpu.VMEM((CY + BOX, CZ + BOX, NX), f32)],
+        in_specs=[VMEM] * 4,
+        out_specs=pl.BlockSpec(memory_space=pl.ANY),
+        scratch_shapes=[
+            pltpu.VMEM((CY + BOX, CZ + 32, NX), f32),
+            pltpu.VMEM((SLABS, WINDOW_ROWS, NX), bf16),
+            pltpu.SMEM((SLABS, NX), jnp.int32),
+            pltpu.SemaphoreType.DMA,
+            pltpu.SemaphoreType.DMA((SLABS // PART,)),
+        ],
         compiler_params=ROOM,
     )(offsets, wide, below, above)
 
@@ -532,10 +557,10 @@
     right = across_rows(next_left, (-1, -1), 1)
     kept, given = fold_rows(position, kept, left, right)
     half = model(kept, shifted(given, "orb", 1), taps, tables)
+    far = across_rows(half, (-1, 1), 0)
+    near = across_rows(half, (-1, 1), 1)
     partner = shifted(half, "orb", 1)
-    near = across_rows(half, (-1, 1), 1)
-    far = across_rows(half, (-1, 1), 0)
-    wide, first_planes, last_planes = widen(position, half, partner, near, far)
+    wide, first_planes, last_planes = widen(position, far, near, partner, half)
     below = shifted(last_planes, "gz", 1)
     above = shifted(first_planes, "gz", -1)
     windows = cut(offsets, wide, below, above)

time: 136 us -> 135 us (level)
  Pallas kernels: 27.7 us -> 25.9 us
    ppermute x4, waiting for transfers between devices: 11.2 us -> 12.6 us  [across_rows(): return lax.ppermute(x, ('gy', 'orb'), pairs)]
where the time goes in v5:
time: 135 us
  waiting for transfers between devices  72.6 us (54%)
  starting transfers between devices  30 us (22%)
  Pallas kernels  25.9 us (19%)
  local copies, waits for them, and re-layouts  3.25 us (2%)
  between operations  1.69 us (1%)
  other arithmetic  1.43 us (1%)
    all_to_all x2, waiting for transfers between devices, exchange(): return lax.all_to_all(x, axis, split_axis=0, concat_axis=0, tiled=True)  45.2 us
    all_to_all x2, starting transfers between devices, exchange(): return lax.all_to_all(x, axis, split_axis=0, concat_axis=0, tiled=True)  16.4 us
    ppermute x6, waiting for transfers between devices, shifted(): return lax.ppermute(x, axis, [(i, (i + by) % count) for i in range(count)])  14.8 us
    ppermute x4, waiting for transfers between devices, across_rows(): return lax.ppermute(x, ('gy', 'orb'), pairs)  12.6 us
    pallas_call x1, Pallas kernels, model(): pl.pallas_call(model_body, name='smooth_and_network', out_shape=jax.Shape...  12.3 us
    ppermute x4, starting transfers between devices, across_rows(): return lax.ppermute(x, ('gy', 'orb'), pairs)  9.69 us
    pallas_call x1, Pallas kernels, cut(): pl.pallas_call(cut_body, name='cut_windows', out_shape=jax.ShapeDtypeStru...  4.19 us
    ppermute x6, starting transfers between devices, shifted(): return lax.ppermute(x, axis, [(i, (i + by) % count) for i in range(count)])  3.86 us
  transfers between devices with their start and end apart: 12, of which 10 were waited for; matrix products, arithmetic and copies ran while one was open for 3% of the time, Pallas kernels for 0%

profile of v5, /device:TPU:1, one launch (start us, length us, event | category | flops | bytes accessed | tf_op | source)
XLA Modules:
  0.0 134.9 jit_solution(3256875761929627036)
XLA Ops:
  0.6 3.0 %pack_boxes.1 = bf16[16,224,128]{2,1,0:T(8,128)(2,1)} custom-call(s32[3,16]{1,0:T(4,128)} %bitcast.14, f32[16]{0:T(128)} %occupation.1, bf16[16,24,576]{2,1,0:T(8,128)(2,1)} %orbitals.3), custom_call_target="tpu_custom_call" | custom-call | tf_op jit(solution)/shard_map/pack_boxes/pallas_call | solution.py:116
  3.6 10.0 %all-to-all-start = ((bf16[16,224,128]{2,1,0:T(8,128)(2,1)}), bf16[16,224,128]{2,1,0:T(8,128)(2,1)S(1)}, u32[]{:S(2)}, u32[]{:S(2)}) async-start(bf16[16,224,128]{2,1,0:T(8,128)(2,1)} %pack_boxes.1), calls=%async_computation | async-start | bytes 1835008 | tf_op jit(solution)/shard_map/all_to_all | solution.py:542
  13.8 0.1 broadcast_multiply_fusion
  13.9 0.1 mul.76
  14.0 0.1 copy.49
  14.2 0.1 copy-done.4
  14.4 0.1 copy.51
  14.6 0.2 fusion.15
  15.0 0.1 div.135
  15.2 0.1 copy.47
  15.3 0.1 copy.48
  15.4 0.1 copy.52
  15.6 0.2 copy.53
  15.9 0.1 broadcast_multiply_fusion.1
  16.0 0.1 mul.84
  16.1 0.1 broadcast_in_dim.79
  16.2 0.1 broadcast_in_dim.81
  16.4 0.3 concatenate.31.first_table
  16.8 0.2 fusion.14
  17.1 0.2 fusion.4
  17.3 0.1 fusion.1.column_table
  17.5 21.4 %all-to-all-done.received = bf16[16,224,128]{2,1,0:T(8,128)(2,1)S(1)} async-done(((bf16[16,224,128]{2,1,0:T(8,128)(2,1)}), bf16[16,224,128]{2,1,0:T(8,128)(2,1)S(1)}, u32[]{:S(2)}, u32[]{:S(2)}) %all-to-all-start) | async-done | bytes 917536 | tf_op jit(solution)/shard_map/all_to_all | solution.py:542
  39.1 3.6 %deposit_boxes.1 = (f32[48,40,128]{2,1,0:T(8,128)S(1)}, bf16[48,24,128]{2,1,0:T(8,128)(2,1)S(1)}, bf16[48,16,128]{2,1,0:T(8,128)(2,1)S(1)}, s32[16,128]{1,0:T(8,128)S(1)}) custom-call(bf16[16,224,128]{2,1,0:T(8,128)(2,1)S(1)} %all-to-all-done.received), custom_call_target="tpu_custom_call" | custom-call | tf_op jit(solution)/shard_map/deposit_boxes/pallas_call | solution.py:182
  42.7 0.5 collective-permute-start.1
  43.2 4.9 %collective-permute-done.1.above = bf16[48,16,128]{2,1,0:T(8,128)(2,1)S(1)} collective-permute-done((bf16[48,16,128]{2,1,0:T(8,128)(2,1)S(1)}, bf16[48,16,128]{2,1,0:T(8,128)(2,1)S(1)}, u32[]{:S(2)}, u32[]{:S(2)}) %collective-permute-start.1) | collective-permute-done | bytes 196640 | tf_op jit(solution)/shard_map/ppermute | solution.py:41
  48.1 0.1 fold_planes.1
  48.2 2.5 %collective-permute-start.2 = (bf16[18,40,128]{2,1,0:T(8,128)(2,1)S(1)}, bf16[18,40,128]{2,1,0:T(8,128)(2,1)S(1)}, u32[]{:S(2)}, u32[]{:S(2)}) collective-permute-start(bf16[18,40,128]{2,1,0:T(8,128)(2,1)S(1)} %get-tuple-element.29), channel_id=1, source_target_pairs={{0,3},{1,2},{2,5},{3,4},{4,7},{5,6},{6,9},{7,8},{8,11},{9,10},{10,... | collective-permute-start | bytes 552968 | tf_op jit(solution)/shard_map/ppermute | solution.py:51
  50.8 2.5 %collective-permute-start.3 = (bf16[18,40,128]{2,1,0:T(8,128)(2,1)S(1)}, bf16[18,40,128]{2,1,0:T(8,128)(2,1)S(1)}, u32[]{:S(2)}, u32[]{:S(2)}) collective-permute-start(bf16[18,40,128]{2,1,0:T(8,128)(2,1)S(1)} %get-tuple-element.30), channel_id=1, source_target_pairs={{0,15},{1,14},{2,1},{3,0},{4,3},{5,2},{6,5},{7,4},{8,7},{9,6},{10,... | collective-permute-start | bytes 552968 | tf_op jit(solution)/shard_map/ppermute | solution.py:51
  53.3 4.4 %collective-permute-done.2.left = bf16[18,40,128]{2,1,0:T(8,128)(2,1)S(1)} collective-permute-done((bf16[18,40,128]{2,1,0:T(8,128)(2,1)S(1)}, bf16[18,40,128]{2,1,0:T(8,128)(2,1)S(1)}, u32[]{:S(2)}, u32[]{:S(2)}) %collective-permute-start.2) | collective-permute-done | bytes 184352 | tf_op jit(solution)/shard_map/ppermute | solution.py:51
  57.8 2.5 %collective-permute-done.3.right = bf16[18,40,128]{2,1,0:T(8,128)(2,1)S(1)} collective-permute-done((bf16[18,40,128]{2,1,0:T(8,128)(2,1)S(1)}, bf16[18,40,128]{2,1,0:T(8,128)(2,1)S(1)}, u32[]{:S(2)}, u32[]{:S(2)}) %collective-permute-start.3) | collective-permute-done | bytes 184352 | tf_op jit(solution)/shard_map/ppermute | solution.py:51
  60.3 0.8 fold_rows.1
  61.8 0.1 copy.55.plane_table
  61.9 5.6 %collective-permute-done.4.other = bf16[24,40,128]{2,1,0:T(8,128)(2,1)S(1)} collective-permute-done((bf16[24,40,128]{2,1,0:T(8,128)(2,1)}, bf16[24,40,128]{2,1,0:T(8,128)(2,1)S(1)}, u32[]{:S(2)}, u32[]{:S(2)}) %collective-permute-start.4) | collective-permute-done | bytes 245792 | tf_op jit(solution)/shard_map/ppermute | solution.py:41
  67.6 12.3 %smooth_and_network.1.own = bf16[12,24,128]{2,1,0:T(8,128)(2,1)S(1)} custom-call(f32[8,13]{1,0:T(8,128)S(1)} %fusion.13.taps, f32[24,40,128]{2,1,0:T(8,128)S(1)} %get-tuple-element.31.kept, bf16[24,40,128]{2,1,0:T(8,128)(2,1)S(1)} %collective-permute-done.4.other, bf16[384,40]{1,0:T(8,128)(2,1)S(1)} %copy.55.plane_table, ...), custom_call_target="tpu_custom_call" | custom-call | tf_op jit(solution)/shard_map/smooth_and_network/pallas_call | solution.py:342
  79.8 3.7 %collective-permute-start.5 = (bf16[12,24,128]{2,1,0:T(8,128)(2,1)S(1)}, bf16[12,24,128]{2,1,0:T(8,128)(2,1)S(1)}, u32[]{:S(2)}, u32[]{:S(2)}) collective-permute-start(bf16[12,24,128]{2,1,0:T(8,128)(2,1)S(1)} %smooth_and_network.1.own), channel_id=1, source_target_pairs={{0,14},{1,3},{2,0},{3,5},{4,2},{5,7},{6,4},{7,9},{8,6},{9,11},{10,... | collective-permute-start | bytes 221192 | tf_op jit(solution)/shard_map/ppermute | solution.py:51
  83.5 0.9 collective-permute-start.6
  84.4 0.5 collective-permute-done.5.far
  84.9 5.1 %collective-permute-done.6.near = bf16[12,24,128]{2,1,0:T(8,128)(2,1)S(1)} collective-permute-done((bf16[12,24,128]{2,1,0:T(8,128)(2,1)S(1)}, bf16[12,24,128]{2,1,0:T(8,128)(2,1)S(1)}, u32[]{:S(2)}, u32[]{:S(2)}) %collective-permute-start.6) | collective-permute-done | bytes 73760 | tf_op jit(solution)/shard_map/ppermute | solution.py:51
  90.1 0.1 widen_rows.1
  90.1 2.2 %collective-permute-start.8 = (bf16[48,16,128]{2,1,0:T(8,128)(2,1)S(1)}, bf16[48,16,128]{2,1,0:T(8,128)(2,1)S(1)}, u32[]{:S(2)}, u32[]{:S(2)}) collective-permute-start(bf16[48,16,128]{2,1,0:T(8,128)(2,1)S(1)} %get-tuple-element.40), channel_id=1, source_target_pairs={{0,16},{16,32},{32,48},{48,64},{64,80},{80,96},{96,112},{112,128},... | collective-permute-start | bytes 589832 | tf_op jit(solution)/shard_map/ppermute | solution.py:41
  92.4 1.1 collective-permute-start.9
  93.5 1.5 %collective-permute-done.8.below = bf16[48,16,128]{2,1,0:T(8,128)(2,1)S(1)} collective-permute-done((bf16[48,16,128]{2,1,0:T(8,128)(2,1)S(1)}, bf16[48,16,128]{2,1,0:T(8,128)(2,1)S(1)}, u32[]{:S(2)}, u32[]{:S(2)}) %collective-permute-start.8) | collective-permute-done | bytes 196640 | tf_op jit(solution)/shard_map/ppermute | solution.py:41
  95.0 2.8 %collective-permute-done.9.above = bf16[48,16,128]{2,1,0:T(8,128)(2,1)S(1)} collective-permute-done((bf16[48,16,128]{2,1,0:T(8,128)(2,1)S(1)}, bf16[48,16,128]{2,1,0:T(8,128)(2,1)S(1)}, u32[]{:S(2)}, u32[]{:S(2)}) %collective-permute-start.9) | collective-permute-done | bytes 196640 | tf_op jit(solution)/shard_map/ppermute | solution.py:41
  97.7 4.2 %cut_windows.1 = bf16[16,216,128]{2,1,0:T(8,128)(2,1)} custom-call(s32[16,128]{1,0:T(8,128)S(1)} %get-tuple-element.42.rows, bf16[48,24,128]{2,1,0:T(8,128)(2,1)S(1)} %get-tuple-element.41.wide, bf16[48,16,128]{2,1,0:T(8,128)(2,1)S(1)} %collective-permute-done.8.below, bf16[48,16,128]{2,1,0:T(8,128)(2,1)S(1)} %collective-permute-done.9.above), custom_call_target="tpu_custom_call" | custom-call | tf_op jit(solution)/shard_map/cut_windows/pallas_call | solution.py:491
  102.0 6.4 %all-to-all-start.1 = ((bf16[16,216,128]{2,1,0:T(8,128)(2,1)}), bf16[16,216,128]{2,1,0:T(8,128)(2,1)S(1)}, u32[]{:S(2)}, u32[]{:S(2)}) async-start(bf16[16,216,128]{2,1,0:T(8,128)(2,1)} %cut_windows.1), calls=%async_computation.1 | async-start | bytes 1769472 | tf_op jit(solution)/shard_map/all_to_all | solution.py:542
  108.5 0.7 copy.56
  109.2 23.8 %all-to-all-done.1.windows = bf16[16,216,128]{2,1,0:T(8,128)(2,1)S(1)} async-done(((bf16[16,216,128]{2,1,0:T(8,128)(2,1)}), bf16[16,216,128]{2,1,0:T(8,128)(2,1)S(1)}, u32[]{:S(2)}, u32[]{:S(2)}) %all-to-all-start.1) | async-done | bytes 884768 | tf_op jit(solution)/shard_map/all_to_all | solution.py:542
  133.0 1.8 %apply_windows.1 = bf16[16,24,576]{2,1,0:T(8,128)(2,1)} custom-call(s32[3,16]{1,0:T(4,128)S(1)} %bitcast.15, bf16[16,216,128]{2,1,0:T(8,128)(2,1)S(1)} %all-to-all-done.1.windows, bf16[16,24,576]{2,1,0:T(8,128)(2,1)S(1)} %copy-done), custom_call_target="tpu_custom_call" | custom-call | tf_op jit(solution)/shard_map/apply_windows/pallas_call | solution.py:530
  (61 shorter events, 1.3 us)
Async XLA Ops:
  3.6 10.2 %copy-start.3 = (f32[8,64]{1,0:T(8,128)S(1)}, f32[8,64]{1,0:T(8,128)}, u32[]{:S(2)}) copy-start(f32[8,64]{1,0:T(8,128)} %param.14) | copy-start | bytes 6148
  3.6 35.3 %all-to-all-start = ((bf16[16,224,128]{2,1,0:T(8,128)(2,1)}), bf16[16,224,128]{2,1,0:T(8,128)(2,1)S(1)}, u32[]{:S(2)}, u32[]{:S(2)}) async-start(bf16[16,224,128]{2,1,0:T(8,128)(2,1)} %pack_boxes.1), calls=%async_computation | async-start | bytes 1835008 | tf_op jit(solution)/shard_map/all_to_all | solution.py:542
  13.6 0.7 copy-start.4
  13.6 0.9 copy-start.5
  14.0 1.7 %copy-start.2 = (f32[64,64]{1,0:T(8,128)S(1)}, f32[64,64]{1,0:T(8,128)}, u32[]{:S(2)}) copy-start(f32[64,64]{1,0:T(8,128)} %param.16) | copy-start | bytes 49156
  14.3 1.8 %copy-start.6 = (f32[64]{0:T(128)S(1)}, f32[64]{0:T(128)}, u32[]{:S(2)}) copy-start(f32[64]{0:T(128)} %param.17) | copy-start | bytes 772
  14.3 1.9 %copy-start.7 = (f32[64]{0:T(128)S(1)}, f32[64]{0:T(128)}, u32[]{:S(2)}) copy-start(f32[64]{0:T(128)} %param.18) | copy-start | bytes 772
  42.7 5.4 %collective-permute-start = (bf16[48,24,128]{2,1,0:T(8,128)(2,1)S(1)}, bf16[48,24,128]{2,1,0:T(8,128)(2,1)S(1)}, u32[]{:S(2)}, u32[]{:S(2)}) collective-permute-start(bf16[48,24,128]{2,1,0:T(8,128)(2,1)S(1)} %get-tuple-element.26), channel_id=1, source_target_pairs={{0,16},{16,32},{32,48},{48,64},{64,80},{80,96},{96,112},{112,128},... | collective-permute-start | bytes 884744 | tf_op jit(solution)/shard_map/ppermute | solution.py:41
  42.7 5.4 %collective-permute-start.1 = (bf16[48,16,128]{2,1,0:T(8,128)(2,1)S(1)}, bf16[48,16,128]{2,1,0:T(8,128)(2,1)S(1)}, u32[]{:S(2)}, u32[]{:S(2)}) collective-permute-start(bf16[48,16,128]{2,1,0:T(8,128)(2,1)S(1)} %get-tuple-element.27), channel_id=1, source_target_pairs={{0,240},{16,0},{32,16},{48,32},{64,48},{80,64},{96,80},{112,96},{1... | collective-permute-start | bytes 589832 | tf_op jit(solution)/shard_map/ppermute | solution.py:41
  48.2 9.5 %collective-permute-start.2 = (bf16[18,40,128]{2,1,0:T(8,128)(2,1)S(1)}, bf16[18,40,128]{2,1,0:T(8,128)(2,1)S(1)}, u32[]{:S(2)}, u32[]{:S(2)}) collective-permute-start(bf16[18,40,128]{2,1,0:T(8,128)(2,1)S(1)} %get-tuple-element.29), channel_id=1, source_target_pairs={{0,3},{1,2},{2,5},{3,4},{4,7},{5,6},{6,9},{7,8},{8,11},{9,10},{10,... | collective-permute-start | bytes 552968 | tf_op jit(solution)/shard_map/ppermute | solution.py:51
  50.8 9.5 %collective-permute-start.3 = (bf16[18,40,128]{2,1,0:T(8,128)(2,1)S(1)}, bf16[18,40,128]{2,1,0:T(8,128)(2,1)S(1)}, u32[]{:S(2)}, u32[]{:S(2)}) collective-permute-start(bf16[18,40,128]{2,1,0:T(8,128)(2,1)S(1)} %get-tuple-element.30), channel_id=1, source_target_pairs={{0,15},{1,14},{2,1},{3,0},{4,3},{5,2},{6,5},{7,4},{8,7},{9,6},{10,... | collective-permute-start | bytes 552968 | tf_op jit(solution)/shard_map/ppermute | solution.py:51
  61.1 6.4 %collective-permute-start.4 = (bf16[24,40,128]{2,1,0:T(8,128)(2,1)}, bf16[24,40,128]{2,1,0:T(8,128)(2,1)S(1)}, u32[]{:S(2)}, u32[]{:S(2)}) collective-permute-start(bf16[24,40,128]{2,1,0:T(8,128)(2,1)} %get-tuple-element.32), channel_id=1, source_target_pairs={{0,1},{1,0},{2,3},{3,2},{4,5},{5,4},{6,7},{7,6},{8,9},{9,8},{10,11... | collective-permute-start | bytes 737288 | tf_op jit(solution)/shard_map/ppermute | solution.py:41
  79.8 5.1 %collective-permute-start.5 = (bf16[12,24,128]{2,1,0:T(8,128)(2,1)S(1)}, bf16[12,24,128]{2,1,0:T(8,128)(2,1)S(1)}, u32[]{:S(2)}, u32[]{:S(2)}) collective-permute-start(bf16[12,24,128]{2,1,0:T(8,128)(2,1)S(1)} %smooth_and_network.1.own), channel_id=1, source_target_pairs={{0,14},{1,3},{2,0},{3,5},{4,2},{5,7},{6,4},{7,9},{8,6},{9,11},{10,... | collective-permute-start | bytes 221192 | tf_op jit(solution)/shard_map/ppermute | solution.py:51
  83.5 6.5 %collective-permute-start.6 = (bf16[12,24,128]{2,1,0:T(8,128)(2,1)S(1)}, bf16[12,24,128]{2,1,0:T(8,128)(2,1)S(1)}, u32[]{:S(2)}, u32[]{:S(2)}) collective-permute-start(bf16[12,24,128]{2,1,0:T(8,128)(2,1)S(1)} %smooth_and_network.1.own), channel_id=1, source_target_pairs={{0,15},{1,2},{2,1},{3,4},{4,3},{5,6},{6,5},{7,8},{8,7},{9,10},{10,... | collective-permute-start | bytes 221192 | tf_op jit(solution)/shard_map/ppermute | solution.py:51
  84.4 5.6 %collective-permute-start.7 = (bf16[12,24,128]{2,1,0:T(8,128)(2,1)S(1)}, bf16[12,24,128]{2,1,0:T(8,128)(2,1)S(1)}, u32[]{:S(2)}, u32[]{:S(2)}) collective-permute-start(bf16[12,24,128]{2,1,0:T(8,128)(2,1)S(1)} %smooth_and_network.1.own), channel_id=1, source_target_pairs={{0,1},{1,0},{2,3},{3,2},{4,5},{5,4},{6,7},{7,6},{8,9},{9,8},{10,11... | collective-permute-start | bytes 221192 | tf_op jit(solution)/shard_map/ppermute | solution.py:41
  90.1 4.8 %collective-permute-start.8 = (bf16[48,16,128]{2,1,0:T(8,128)(2,1)S(1)}, bf16[48,16,128]{2,1,0:T(8,128)(2,1)S(1)}, u32[]{:S(2)}, u32[]{:S(2)}) collective-permute-start(bf16[48,16,128]{2,1,0:T(8,128)(2,1)S(1)} %get-tuple-element.40), channel_id=1, source_target_pairs={{0,16},{16,32},{32,48},{48,64},{64,80},{80,96},{96,112},{112,128},... | collective-permute-start | bytes 589832 | tf_op jit(solution)/shard_map/ppermute | solution.py:41
  92.4 5.4 %collective-permute-start.9 = (bf16[48,16,128]{2,1,0:T(8,128)(2,1)S(1)}, bf16[48,16,128]{2,1,0:T(8,128)(2,1)S(1)}, u32[]{:S(2)}, u32[]{:S(2)}) collective-permute-start(bf16[48,16,128]{2,1,0:T(8,128)(2,1)S(1)} %get-tuple-element.43), channel_id=1, source_target_pairs={{0,240},{16,0},{32,16},{48,32},{64,48},{80,64},{96,80},{112,96},{1... | collective-permute-start | bytes 589832 | tf_op jit(solution)/shard_map/ppermute | solution.py:41
  101.9 31.1 %copy-start = (bf16[16,24,576]{2,1,0:T(8,128)(2,1)S(1)}, bf16[16,24,576]{2,1,0:T(8,128)(2,1)}, u32[]{:S(2)}) copy-start(bf16[16,24,576]{2,1,0:T(8,128)(2,1)} %orbitals.3) | copy-start | bytes 1327108
  102.0 31.1 %copy-start.1 = (s32[16,3]{0,1:T(4,128)S(1)}, s32[16,3]{0,1:T(4,128)}, u32[]{:S(2)}) copy-start(s32[16,3]{0,1:T(4,128)} %param.12) | copy-start | bytes 580
  102.0 31.1 %all-to-all-start.1 = ((bf16[16,216,128]{2,1,0:T(8,128)(2,1)}), bf16[16,216,128]{2,1,0:T(8,128)(2,1)S(1)}, u32[]{:S(2)}, u32[]{:S(2)}) async-start(bf16[16,216,128]{2,1,0:T(8,128)(2,1)} %cut_windows.1), calls=%async_computation.1 | async-start | bytes 1769472 | tf_op jit(solution)/shard_map/all_to_all | solution.py:542

commit v6 on v5

--- a/solution.py
+++ b/solution.py
@@ -65,7 +65,13 @@
     return lax.broadcasted_iota(jnp.int32, (rows, NX), 1)
 
 
-def pack_body(corners, occupation, orbitals, sent, boxes, count, sems):
+def pack_body(corners_in, occupation_in, orbitals, sent, boxes, corners, occupation, count, scalar_sems, sems):
+    scalars = [
+        pltpu.make_async_copy(corners_in, corners, scalar_sems.at[0]),
+        pltpu.make_async_copy(occupation_in, occupation, scalar_sems.at[1]),
+    ]
+    for copy in scalars:
+        copy.start()
     copies = [
         pltpu.make_async_copy(
             orbitals.at[pl.ds(PART * i, PART)], boxes.at[pl.ds(PART * i, PART)], sems.at[i]
@@ -106,6 +112,8 @@
         held = sent[slab, TAIL:BLOCK_ROWS, :].astype(f32)
         sent[slab, TAIL:BLOCK_ROWS, :] = jnp.where(side == rank, fresh, held).astype(bf16)
 
+    for copy in scalars:
+        copy.wait()
     for i in range(HELD):
         if i % PART == 0:
             copies[i // PART].wait()
@@ -117,11 +125,14 @@
         pack_body,
         name="pack_boxes",
         out_shape=jax.ShapeDtypeStruct((SLABS, BLOCK_ROWS, NX), bf16),
-        in_specs=[SMEM, SMEM, pl.BlockSpec(memory_space=pl.ANY)],
+        in_specs=[pl.BlockSpec(memory_space=pl.ANY)] * 3,
         out_specs=VMEM,
         scratch_shapes=[
             pltpu.VMEM((HELD, BOX, BOX * BOX), bf16),
+            pltpu.SMEM((3, HELD), jnp.int32),
+            pltpu.SMEM((HELD,), f32),
             pltpu.SMEM((SLABS,), jnp.int32),
+            pltpu.SemaphoreType.DMA((2,)),
             pltpu.SemaphoreType.DMA((HELD // PART,)),
         ],
         compiler_params=pltpu.CompilerParams(vmem_limit_bytes=60 * 1024 * 1024),
@@ -172,7 +183,7 @@
                     grid[y0 + first + k, pl.ds(z0, BOX), :] = news[k]
         return carry
 
-    lax.fori_loop(0, SLABS, source_step, 0)
+    lax.fori_loop(0, SLABS, source_step, 0, unroll=2)
     own[...] = grids[0][:, :PLANES, :] + grids[1][:, :PLANES, :]
     next_up[...] = (grids[0][:, CZ:, :] + grids[1][:, CZ:, :]).astype(bf16)
     next_down[...] = (grids[0][:, :ABOVE, :] + grids[1][:, :ABOVE, :]).astype(bf16)
@@ -477,7 +488,7 @@
 
     copies = []
     for first in range(0, SLABS, PART):
-        lax.fori_loop(first, first + PART, source_step, 0, unroll=2)
+        lax.fori_loop(first, first + PART, source_step, 0, unroll=4)
         copy = pltpu.make_async_copy(
             cuts.at[pl.ds(first, PART)], windows.at[pl.ds(first, PART)], sems.at[first // PART]
         )
@@ -505,7 +516,7 @@
     )(offsets, wide, below, above)
 
 
-def apply_body(corners, windows, orbitals, applied, count):
+def apply_body(corners, windows, orbitals, applied, products, count, sems):
     def clear(slab, carry):
         count[slab] = 0
         return carry
@@ -520,10 +531,19 @@
         tail = windows[slab, TAIL:WINDOW_ROWS, :].astype(f32)
         tail = jnp.where(rank == 0, tail[:, :64], tail[:, 64:])
         whole = jnp.concatenate([main[BOX * j : BOX * j + BOX] for j in range(4)] + [tail], axis=1)
-        applied[i] = (whole * orbitals[i].astype(f32)).astype(bf16)
-        return carry
-
-    lax.fori_loop(0, HELD, place, 0, unroll=4)
+        products[i] = (whole * orbitals[i].astype(f32)).astype(bf16)
+        return carry
+
+    copies = []
+    for first in range(0, HELD, PART):
+        lax.fori_loop(first, first + PART, place, 0, unroll=4)
+        copy = pltpu.make_async_copy(
+            products.at[pl.ds(first, PART)], applied.at[pl.ds(first, PART)], sems.at[first // PART]
+        )
+        copy.start()
+        copies.append(copy)
+    for copy in copies:
+        copy.wait()
 
 
 def apply(corners, windows, orbitals):
@@ -532,8 +552,12 @@
         name="apply_windows",
         out_shape=jax.ShapeDtypeStruct(orbitals.shape, bf16),
         in_specs=[SMEM, VMEM, VMEM],
-        out_specs=VMEM,
-        scratch_shapes=[pltpu.SMEM((SLABS,), jnp.int32)],
+        out_specs=pl.BlockSpec(memory_space=pl.ANY),
+        scratch_shapes=[
+            pltpu.VMEM((HELD, BOX, BOX * BOX), bf16),
+            pltpu.SMEM((SLABS,), jnp.int32),
+            pltpu.SemaphoreType.DMA((HELD // PART,)),
+        ],
         compiler_params=ROOM,
     )(corners, windows, orbitals)
 

time: 135 us -> 134 us (level)
  Pallas kernels: 25.9 us -> 24.1 us
where the time goes in v6:
time: 134 us; the launch traced here: 133 us
  waiting for transfers between devices  72.6 us (54%)
  starting transfers between devices  30 us (22%)
  Pallas kernels  24.1 us (18%)
  local copies, waits for them, and re-layouts  3.25 us (2%)
  between operations  1.86 us (1%)
  other arithmetic  1.43 us (1%)
    all_to_all x2, waiting for transfers between devices, exchange(): return lax.all_to_all(x, axis, split_axis=0, concat_axis=0, tiled=True)  45.2 us
    all_to_all x2, starting transfers between devices, exchange(): return lax.all_to_all(x, axis, split_axis=0, concat_axis=0, tiled=True)  16.4 us
    ppermute x6, waiting for transfers between devices, shifted(): return lax.ppermute(x, axis, [(i, (i + by) % count) for i in range(count)])  14.8 us
    ppermute x4, waiting for transfers between devices, across_rows(): return lax.ppermute(x, ('gy', 'orb'), pairs)  12.6 us
    pallas_call x1, Pallas kernels, model(): pl.pallas_call(model_body, name='smooth_and_network', out_shape=jax.Shape...  12.3 us
    ppermute x4, starting transfers between devices, across_rows(): return lax.ppermute(x, ('gy', 'orb'), pairs)  9.69 us
    pallas_call x1, Pallas kernels, cut(): pl.pallas_call(cut_body, name='cut_windows', out_shape=jax.ShapeDtypeStru...  3.92 us
    ppermute x6, starting transfers between devices, shifted(): return lax.ppermute(x, axis, [(i, (i + by) % count) for i in range(count)])  3.86 us
  transfers between devices with their start and end apart: 12, of which 10 were waited for; matrix products, arithmetic and copies ran while one was open for 3% of the time, Pallas kernels for 0%

profile of v6, /device:TPU:1, one launch (start us, length us, event | category | flops | bytes accessed | tf_op | source)
XLA Modules:
  0.0 133.2 jit_solution(18347044242345232416)
XLA Ops:
  0.6 2.3 %pack_boxes.1 = bf16[16,224,128]{2,1,0:T(8,128)(2,1)} custom-call(s32[3,16]{1,0:T(4,128)} %bitcast.14, f32[16]{0:T(128)} %occupation_in.1, bf16[16,24,576]{2,1,0:T(8,128)(2,1)} %orbitals.3), custom_call_target="tpu_custom_call" | custom-call | tf_op jit(solution)/shard_map/pack_boxes/pallas_call | solution.py:124
  3.0 10.0 %all-to-all-start = ((bf16[16,224,128]{2,1,0:T(8,128)(2,1)}), bf16[16,224,128]{2,1,0:T(8,128)(2,1)S(1)}, u32[]{:S(2)}, u32[]{:S(2)}) async-start(bf16[16,224,128]{2,1,0:T(8,128)(2,1)} %pack_boxes.1), calls=%async_computation | async-start | bytes 1835008 | tf_op jit(solution)/shard_map/all_to_all | solution.py:566
  13.1 0.1 broadcast_multiply_fusion
  13.2 0.1 mul.76
  13.4 0.1 copy.49
  13.5 0.1 copy-done.4
  13.7 0.1 copy.51
  13.9 0.2 fusion.15
  14.1 0.1 div.142
  14.3 0.1 div.135
  14.5 0.1 copy.47
  14.6 0.1 copy.48
  14.7 0.1 copy.52
  14.9 0.2 copy.53
  15.2 0.1 broadcast_multiply_fusion.1
  15.3 0.1 mul.84
  15.4 0.1 broadcast_in_dim.79
  15.5 0.1 broadcast_in_dim.81
  15.7 0.3 concatenate.31.first_table
  16.1 0.2 fusion.14
  16.4 0.2 fusion.4
  16.7 0.1 fusion.1.column_table
  16.8 21.4 %all-to-all-done.received = bf16[16,224,128]{2,1,0:T(8,128)(2,1)S(1)} async-done(((bf16[16,224,128]{2,1,0:T(8,128)(2,1)}), bf16[16,224,128]{2,1,0:T(8,128)(2,1)S(1)}, u32[]{:S(2)}, u32[]{:S(2)}) %all-to-all-start) | async-done | bytes 917536 | tf_op jit(solution)/shard_map/all_to_all | solution.py:566
  38.4 3.0 %deposit_boxes.1 = (f32[48,40,128]{2,1,0:T(8,128)S(1)}, bf16[48,24,128]{2,1,0:T(8,128)(2,1)S(1)}, bf16[48,16,128]{2,1,0:T(8,128)(2,1)S(1)}, s32[16,128]{1,0:T(8,128)S(1)}) custom-call(bf16[16,224,128]{2,1,0:T(8,128)(2,1)S(1)} %all-to-all-done.received), custom_call_target="tpu_custom_call" | custom-call | tf_op jit(solution)/shard_map/deposit_boxes/pallas_call | solution.py:193
  41.4 0.5 collective-permute-start.1
  41.9 4.9 %collective-permute-done.1.above = bf16[48,16,128]{2,1,0:T(8,128)(2,1)S(1)} collective-permute-done((bf16[48,16,128]{2,1,0:T(8,128)(2,1)S(1)}, bf16[48,16,128]{2,1,0:T(8,128)(2,1)S(1)}, u32[]{:S(2)}, u32[]{:S(2)}) %collective-permute-start.1) | collective-permute-done | bytes 196640 | tf_op jit(solution)/shard_map/ppermute | solution.py:41
  46.8 0.1 fold_planes.1
  46.9 2.6 %collective-permute-start.2 = (bf16[18,40,128]{2,1,0:T(8,128)(2,1)S(1)}, bf16[18,40,128]{2,1,0:T(8,128)(2,1)S(1)}, u32[]{:S(2)}, u32[]{:S(2)}) collective-permute-start(bf16[18,40,128]{2,1,0:T(8,128)(2,1)S(1)} %get-tuple-element.29), channel_id=1, source_target_pairs={{0,3},{1,2},{2,5},{3,4},{4,7},{5,6},{6,9},{7,8},{8,11},{9,10},{10,... | collective-permute-start | bytes 552968 | tf_op jit(solution)/shard_map/ppermute | solution.py:51
  49.5 2.5 %collective-permute-start.3 = (bf16[18,40,128]{2,1,0:T(8,128)(2,1)S(1)}, bf16[18,40,128]{2,1,0:T(8,128)(2,1)S(1)}, u32[]{:S(2)}, u32[]{:S(2)}) collective-permute-start(bf16[18,40,128]{2,1,0:T(8,128)(2,1)S(1)} %get-tuple-element.30), channel_id=1, source_target_pairs={{0,15},{1,14},{2,1},{3,0},{4,3},{5,2},{6,5},{7,4},{8,7},{9,6},{10,... | collective-permute-start | bytes 552968 | tf_op jit(solution)/shard_map/ppermute | solution.py:51
  52.0 4.5 %collective-permute-done.2.left = bf16[18,40,128]{2,1,0:T(8,128)(2,1)S(1)} collective-permute-done((bf16[18,40,128]{2,1,0:T(8,128)(2,1)S(1)}, bf16[18,40,128]{2,1,0:T(8,128)(2,1)S(1)}, u32[]{:S(2)}, u32[]{:S(2)}) %collective-permute-start.2) | collective-permute-done | bytes 184352 | tf_op jit(solution)/shard_map/ppermute | solution.py:51
  56.5 2.5 %collective-permute-done.3.right = bf16[18,40,128]{2,1,0:T(8,128)(2,1)S(1)} collective-permute-done((bf16[18,40,128]{2,1,0:T(8,128)(2,1)S(1)}, bf16[18,40,128]{2,1,0:T(8,128)(2,1)S(1)}, u32[]{:S(2)}, u32[]{:S(2)}) %collective-permute-start.3) | collective-permute-done | bytes 184352 | tf_op jit(solution)/shard_map/ppermute | solution.py:51
  59.0 0.8 fold_rows.1
  60.5 0.1 copy.55.plane_table
  60.6 5.6 %collective-permute-done.4.other = bf16[24,40,128]{2,1,0:T(8,128)(2,1)S(1)} collective-permute-done((bf16[24,40,128]{2,1,0:T(8,128)(2,1)}, bf16[24,40,128]{2,1,0:T(8,128)(2,1)S(1)}, u32[]{:S(2)}, u32[]{:S(2)}) %collective-permute-start.4) | collective-permute-done | bytes 245792 | tf_op jit(solution)/shard_map/ppermute | solution.py:41
  66.3 12.3 %smooth_and_network.1.own = bf16[12,24,128]{2,1,0:T(8,128)(2,1)S(1)} custom-call(f32[8,13]{1,0:T(8,128)S(1)} %fusion.13.taps, f32[24,40,128]{2,1,0:T(8,128)S(1)} %get-tuple-element.31.kept, bf16[24,40,128]{2,1,0:T(8,128)(2,1)S(1)} %collective-permute-done.4.other, bf16[384,40]{1,0:T(8,128)(2,1)S(1)} %copy.55.plane_table, ...), custom_call_target="tpu_custom_call" | custom-call | tf_op jit(solution)/shard_map/smooth_and_network/pallas_call | solution.py:353
  78.6 3.6 %collective-permute-start.5 = (bf16[12,24,128]{2,1,0:T(8,128)(2,1)S(1)}, bf16[12,24,128]{2,1,0:T(8,128)(2,1)S(1)}, u32[]{:S(2)}, u32[]{:S(2)}) collective-permute-start(bf16[12,24,128]{2,1,0:T(8,128)(2,1)S(1)} %smooth_and_network.1.own), channel_id=1, source_target_pairs={{0,14},{1,3},{2,0},{3,5},{4,2},{5,7},{6,4},{7,9},{8,6},{9,11},{10,... | collective-permute-start | bytes 221192 | tf_op jit(solution)/shard_map/ppermute | solution.py:51
  82.2 0.9 collective-permute-start.6
  83.2 0.5 collective-permute-done.5.far
  83.6 5.1 %collective-permute-done.6.near = bf16[12,24,128]{2,1,0:T(8,128)(2,1)S(1)} collective-permute-done((bf16[12,24,128]{2,1,0:T(8,128)(2,1)S(1)}, bf16[12,24,128]{2,1,0:T(8,128)(2,1)S(1)}, u32[]{:S(2)}, u32[]{:S(2)}) %collective-permute-start.6) | collective-permute-done | bytes 73760 | tf_op jit(solution)/shard_map/ppermute | solution.py:51
  88.8 2.2 %collective-permute-start.8 = (bf16[48,16,128]{2,1,0:T(8,128)(2,1)S(1)}, bf16[48,16,128]{2,1,0:T(8,128)(2,1)S(1)}, u32[]{:S(2)}, u32[]{:S(2)}) collective-permute-start(bf16[48,16,128]{2,1,0:T(8,128)(2,1)S(1)} %get-tuple-element.40), channel_id=1, source_target_pairs={{0,16},{16,32},{32,48},{48,64},{64,80},{80,96},{96,112},{112,128},... | collective-permute-start | bytes 589832 | tf_op jit(solution)/shard_map/ppermute | solution.py:41
  91.1 1.1 collective-permute-start.9
  92.2 1.5 %collective-permute-done.8.below = bf16[48,16,128]{2,1,0:T(8,128)(2,1)S(1)} collective-permute-done((bf16[48,16,128]{2,1,0:T(8,128)(2,1)S(1)}, bf16[48,16,128]{2,1,0:T(8,128)(2,1)S(1)}, u32[]{:S(2)}, u32[]{:S(2)}) %collective-permute-start.8) | collective-permute-done | bytes 196640 | tf_op jit(solution)/shard_map/ppermute | solution.py:41
  93.7 2.8 %collective-permute-done.9.above = bf16[48,16,128]{2,1,0:T(8,128)(2,1)S(1)} collective-permute-done((bf16[48,16,128]{2,1,0:T(8,128)(2,1)S(1)}, bf16[48,16,128]{2,1,0:T(8,128)(2,1)S(1)}, u32[]{:S(2)}, u32[]{:S(2)}) %collective-permute-start.9) | collective-permute-done | bytes 196640 | tf_op jit(solution)/shard_map/ppermute | solution.py:41
  96.5 3.9 %cut_windows.1 = bf16[16,216,128]{2,1,0:T(8,128)(2,1)} custom-call(s32[16,128]{1,0:T(8,128)S(1)} %get-tuple-element.42.rows, bf16[48,24,128]{2,1,0:T(8,128)(2,1)S(1)} %get-tuple-element.41.wide, bf16[48,16,128]{2,1,0:T(8,128)(2,1)S(1)} %collective-permute-done.8.below, bf16[48,16,128]{2,1,0:T(8,128)(2,1)S(1)} %collective-permute-done.9.above), custom_call_target="tpu_custom_call" | custom-call | tf_op jit(solution)/shard_map/cut_windows/pallas_call | solution.py:502
  100.4 6.4 %all-to-all-start.1 = ((bf16[16,216,128]{2,1,0:T(8,128)(2,1)}), bf16[16,216,128]{2,1,0:T(8,128)(2,1)S(1)}, u32[]{:S(2)}, u32[]{:S(2)}) async-start(bf16[16,216,128]{2,1,0:T(8,128)(2,1)} %cut_windows.1), calls=%async_computation.1 | async-start | bytes 1769472 | tf_op jit(solution)/shard_map/all_to_all | solution.py:566
  106.9 0.7 copy.56
  107.6 23.8 %all-to-all-done.1.windows = bf16[16,216,128]{2,1,0:T(8,128)(2,1)S(1)} async-done(((bf16[16,216,128]{2,1,0:T(8,128)(2,1)}), bf16[16,216,128]{2,1,0:T(8,128)(2,1)S(1)}, u32[]{:S(2)}, u32[]{:S(2)}) %all-to-all-start.1) | async-done | bytes 884768 | tf_op jit(solution)/shard_map/all_to_all | solution.py:566
  131.5 1.6 %apply_windows.1 = bf16[16,24,576]{2,1,0:T(8,128)(2,1)} custom-call(s32[3,16]{1,0:T(4,128)S(1)} %bitcast.15, bf16[16,216,128]{2,1,0:T(8,128)(2,1)S(1)} %all-to-all-done.1.windows, bf16[16,24,576]{2,1,0:T(8,128)(2,1)S(1)} %copy-done), custom_call_target="tpu_custom_call" | custom-call | tf_op jit(solution)/shard_map/apply_windows/pallas_call | solution.py:550
  (61 shorter events, 1.3 us)
Async XLA Ops:
  2.9 10.2 %copy-start.3 = (f32[8,64]{1,0:T(8,128)S(1)}, f32[8,64]{1,0:T(8,128)}, u32[]{:S(2)}) copy-start(f32[8,64]{1,0:T(8,128)} %param.14) | copy-start | bytes 6148
  3.0 35.3 %all-to-all-start = ((bf16[16,224,128]{2,1,0:T(8,128)(2,1)}), bf16[16,224,128]{2,1,0:T(8,128)(2,1)S(1)}, u32[]{:S(2)}, u32[]{:S(2)}) async-start(bf16[16,224,128]{2,1,0:T(8,128)(2,1)} %pack_boxes.1), calls=%async_computation | async-start | bytes 1835008 | tf_op jit(solution)/shard_map/all_to_all | solution.py:566
  12.9 0.7 copy-start.4
  13.0 0.9 copy-start.5
  13.3 1.7 %copy-start.2 = (f32[64,64]{1,0:T(8,128)S(1)}, f32[64,64]{1,0:T(8,128)}, u32[]{:S(2)}) copy-start(f32[64,64]{1,0:T(8,128)} %param.16) | copy-start | bytes 49156
  13.6 1.8 %copy-start.6 = (f32[64]{0:T(128)S(1)}, f32[64]{0:T(128)}, u32[]{:S(2)}) copy-start(f32[64]{0:T(128)} %param.17) | copy-start | bytes 772
  13.6 1.9 %copy-start.7 = (f32[64]{0:T(128)S(1)}, f32[64]{0:T(128)}, u32[]{:S(2)}) copy-start(f32[64]{0:T(128)} %param.18) | copy-start | bytes 772
  41.4 5.4 %collective-permute-start = (bf16[48,24,128]{2,1,0:T(8,128)(2,1)S(1)}, bf16[48,24,128]{2,1,0:T(8,128)(2,1)S(1)}, u32[]{:S(2)}, u32[]{:S(2)}) collective-permute-start(bf16[48,24,128]{2,1,0:T(8,128)(2,1)S(1)} %get-tuple-element.26), channel_id=1, source_target_pairs={{0,16},{16,32},{32,48},{48,64},{64,80},{80,96},{96,112},{112,128},... | collective-permute-start | bytes 884744 | tf_op jit(solution)/shard_map/ppermute | solution.py:41
  41.4 5.4 %collective-permute-start.1 = (bf16[48,16,128]{2,1,0:T(8,128)(2,1)S(1)}, bf16[48,16,128]{2,1,0:T(8,128)(2,1)S(1)}, u32[]{:S(2)}, u32[]{:S(2)}) collective-permute-start(bf16[48,16,128]{2,1,0:T(8,128)(2,1)S(1)} %get-tuple-element.27), channel_id=1, source_target_pairs={{0,240},{16,0},{32,16},{48,32},{64,48},{80,64},{96,80},{112,96},{1... | collective-permute-start | bytes 589832 | tf_op jit(solution)/shard_map/ppermute | solution.py:41
  46.9 9.6 %collective-permute-start.2 = (bf16[18,40,128]{2,1,0:T(8,128)(2,1)S(1)}, bf16[18,40,128]{2,1,0:T(8,128)(2,1)S(1)}, u32[]{:S(2)}, u32[]{:S(2)}) collective-permute-start(bf16[18,40,128]{2,1,0:T(8,128)(2,1)S(1)} %get-tuple-element.29), channel_id=1, source_target_pairs={{0,3},{1,2},{2,5},{3,4},{4,7},{5,6},{6,9},{7,8},{8,11},{9,10},{10,... | collective-permute-start | bytes 552968 | tf_op jit(solution)/shard_map/ppermute | solution.py:51
  49.5 9.5 %collective-permute-start.3 = (bf16[18,40,128]{2,1,0:T(8,128)(2,1)S(1)}, bf16[18,40,128]{2,1,0:T(8,128)(2,1)S(1)}, u32[]{:S(2)}, u32[]{:S(2)}) collective-permute-start(bf16[18,40,128]{2,1,0:T(8,128)(2,1)S(1)} %get-tuple-element.30), channel_id=1, source_target_pairs={{0,15},{1,14},{2,1},{3,0},{4,3},{5,2},{6,5},{7,4},{8,7},{9,6},{10,... | collective-permute-start | bytes 552968 | tf_op jit(solution)/shard_map/ppermute | solution.py:51
  59.8 6.4 %collective-permute-start.4 = (bf16[24,40,128]{2,1,0:T(8,128)(2,1)}, bf16[24,40,128]{2,1,0:T(8,128)(2,1)S(1)}, u32[]{:S(2)}, u32[]{:S(2)}) collective-permute-start(bf16[24,40,128]{2,1,0:T(8,128)(2,1)} %get-tuple-element.32), channel_id=1, source_target_pairs={{0,1},{1,0},{2,3},{3,2},{4,5},{5,4},{6,7},{7,6},{8,9},{9,8},{10,11... | collective-permute-start | bytes 737288 | tf_op jit(solution)/shard_map/ppermute | solution.py:41
  78.6 5.1 %collective-permute-start.5 = (bf16[12,24,128]{2,1,0:T(8,128)(2,1)S(1)}, bf16[12,24,128]{2,1,0:T(8,128)(2,1)S(1)}, u32[]{:S(2)}, u32[]{:S(2)}) collective-permute-start(bf16[12,24,128]{2,1,0:T(8,128)(2,1)S(1)} %smooth_and_network.1.own), channel_id=1, source_target_pairs={{0,14},{1,3},{2,0},{3,5},{4,2},{5,7},{6,4},{7,9},{8,6},{9,11},{10,... | collective-permute-start | bytes 221192 | tf_op jit(solution)/shard_map/ppermute | solution.py:51
  82.2 6.5 %collective-permute-start.6 = (bf16[12,24,128]{2,1,0:T(8,128)(2,1)S(1)}, bf16[12,24,128]{2,1,0:T(8,128)(2,1)S(1)}, u32[]{:S(2)}, u32[]{:S(2)}) collective-permute-start(bf16[12,24,128]{2,1,0:T(8,128)(2,1)S(1)} %smooth_and_network.1.own), channel_id=1, source_target_pairs={{0,15},{1,2},{2,1},{3,4},{4,3},{5,6},{6,5},{7,8},{8,7},{9,10},{10,... | collective-permute-start | bytes 221192 | tf_op jit(solution)/shard_map/ppermute | solution.py:51
  83.2 5.6 %collective-permute-start.7 = (bf16[12,24,128]{2,1,0:T(8,128)(2,1)S(1)}, bf16[12,24,128]{2,1,0:T(8,128)(2,1)S(1)}, u32[]{:S(2)}, u32[]{:S(2)}) collective-permute-start(bf16[12,24,128]{2,1,0:T(8,128)(2,1)S(1)} %smooth_and_network.1.own), channel_id=1, source_target_pairs={{0,1},{1,0},{2,3},{3,2},{4,5},{5,4},{6,7},{7,6},{8,9},{9,8},{10,11... | collective-permute-start | bytes 221192 | tf_op jit(solution)/shard_map/ppermute | solution.py:41
  88.8 4.8 %collective-permute-start.8 = (bf16[48,16,128]{2,1,0:T(8,128)(2,1)S(1)}, bf16[48,16,128]{2,1,0:T(8,128)(2,1)S(1)}, u32[]{:S(2)}, u32[]{:S(2)}) collective-permute-start(bf16[48,16,128]{2,1,0:T(8,128)(2,1)S(1)} %get-tuple-element.40), channel_id=1, source_target_pairs={{0,16},{16,32},{32,48},{48,64},{64,80},{80,96},{96,112},{112,128},... | collective-permute-start | bytes 589832 | tf_op jit(solution)/shard_map/ppermute | solution.py:41
  91.1 5.4 %collective-permute-start.9 = (bf16[48,16,128]{2,1,0:T(8,128)(2,1)S(1)}, bf16[48,16,128]{2,1,0:T(8,128)(2,1)S(1)}, u32[]{:S(2)}, u32[]{:S(2)}) collective-permute-start(bf16[48,16,128]{2,1,0:T(8,128)(2,1)S(1)} %get-tuple-element.43), channel_id=1, source_target_pairs={{0,240},{16,0},{32,16},{48,32},{64,48},{80,64},{96,80},{112,96},{1... | collective-permute-start | bytes 589832 | tf_op jit(solution)/shard_map/ppermute | solution.py:41
  100.4 31.1 %copy-start = (bf16[16,24,576]{2,1,0:T(8,128)(2,1)S(1)}, bf16[16,24,576]{2,1,0:T(8,128)(2,1)}, u32[]{:S(2)}) copy-start(bf16[16,24,576]{2,1,0:T(8,128)(2,1)} %orbitals.3) | copy-start | bytes 1327108
  100.4 31.1 %copy-start.1 = (s32[16,3]{0,1:T(4,128)S(1)}, s32[16,3]{0,1:T(4,128)}, u32[]{:S(2)}) copy-start(s32[16,3]{0,1:T(4,128)} %param.12) | copy-start | bytes 580
  100.4 31.1 %all-to-all-start.1 = ((bf16[16,216,128]{2,1,0:T(8,128)(2,1)}), bf16[16,216,128]{2,1,0:T(8,128)(2,1)S(1)}, u32[]{:S(2)}, u32[]{:S(2)}) async-start(bf16[16,216,128]{2,1,0:T(8,128)(2,1)} %cut_windows.1), calls=%async_computation.1 | async-start | bytes 1769472 | tf_op jit(solution)/shard_map/all_to_all | solution.py:566

commit v7 on v6

--- a/solution.py
+++ b/solution.py
@@ -17,6 +17,8 @@
 HELD = 16
 FIRST_PLANE = 10
 PLANES = 40
+SKIP = FIRST_PLANE - RAD
+DEPTH = PLANES - SKIP
 ABOVE = PLANES - CZ
 HALF = CY // 2
 ROWS = HALF + 2 * RAD
@@ -211,13 +213,14 @@
     )(received)
 
 
-def fold_planes_body(own, below, above, kept, next_right, next_left):
-    for first, last in ((0, CZ), (CZ, PLANES)):
-        other = below[...] if first == 0 else above[...]
-        total = own[:, first:last, :] + other.astype(f32)
-        kept[:, first:last, :] = total[RAD : RAD + REACH]
-        next_right[:, first:last, :] = total[2 * CY - EDGE :].astype(bf16)
-        next_left[:, first:last, :] = total[:EDGE].astype(bf16)
+def fold_planes_body(own, below, above, kept, next_right, next_left, total, flat):
+    total[:, :CZ, :] = own[:, :CZ, :] + below[...].astype(f32)
+    total[:, CZ:, :] = own[:, CZ:, :] + above[...].astype(f32)
+    kept[...] = total[RAD : RAD + REACH, SKIP:, :]
+    for side, first, sent in ((0, 2 * CY - EDGE, next_right), (1, 0, next_left)):
+        for row in range(EDGE):
+            flat[side, DEPTH * row : DEPTH * (row + 1), :] = total[first + row, SKIP:, :]
+        sent[...] = flat[side].astype(bf16)
 
 
 def fold_planes(own, below, above):
@@ -225,22 +228,32 @@
         fold_planes_body,
         name="fold_planes",
         out_shape=(
-            jax.ShapeDtypeStruct((REACH, PLANES, NX), f32),
-            jax.ShapeDtypeStruct((EDGE, PLANES, NX), bf16),
-            jax.ShapeDtypeStruct((EDGE, PLANES, NX), bf16),
+            jax.ShapeDtypeStruct((REACH, DEPTH, NX), f32),
+            jax.ShapeDtypeStruct((EDGE * DEPTH, NX), bf16),
+            jax.ShapeDtypeStruct((EDGE * DEPTH, NX), bf16),
         ),
         in_specs=[VMEM] * 3,
         out_specs=(VMEM,) * 3,
+        scratch_shapes=[
+            pltpu.VMEM((CY + BOX, PLANES, NX), f32),
+            pltpu.VMEM((2, EDGE * DEPTH, NX), f32),
+        ],
         compiler_params=ROOM,
     )(own, below, above)
 
 
-def fold_rows_body(position, own, left, right, kept, given, total):
-    total[:EDGE] = own[:EDGE] + left[...].astype(f32)
-    total[EDGE:] = own[EDGE:] + right[...].astype(f32)
+def fold_rows_body(position, own, left, right, kept, given, total, sides, flat):
+    for side, received in enumerate((left, right)):
+        sides[side] = received[...].astype(f32)
+        for row in range(EDGE):
+            total[EDGE * side + row] = (
+                own[EDGE * side + row] + sides[side, DEPTH * row : DEPTH * (row + 1), :]
+            )
     orb = position[0]
     kept[...] = total[pl.ds(HALF * orb, ROWS)]
-    given[...] = total[pl.ds(HALF * (1 - orb), ROWS)].astype(bf16)
+    for row in range(ROWS):
+        flat[DEPTH * row : DEPTH * (row + 1), :] = total[HALF * (1 - orb) + row]
+    given[...] = flat[...].astype(bf16)
 
 
 def fold_rows(position, own, left, right):
@@ -248,12 +261,16 @@
         fold_rows_body,
         name="fold_rows",
         out_shape=(
-            jax.ShapeDtypeStruct((ROWS, PLANES, NX), f32),
-            jax.ShapeDtypeStruct((ROWS, PLANES, NX), bf16),
+            jax.ShapeDtypeStruct((ROWS, DEPTH, NX), f32),
+            jax.ShapeDtypeStruct((ROWS * DEPTH, NX), bf16),
         ),
         in_specs=[SMEM] + [VMEM] * 3,
         out_specs=(VMEM, VMEM),
-        scratch_shapes=[pltpu.VMEM((REACH, PLANES, NX), f32)],
+        scratch_shapes=[
+            pltpu.VMEM((REACH, DEPTH, NX), f32),
+            pltpu.VMEM((2, EDGE * DEPTH, NX), f32),
+            pltpu.VMEM((ROWS * DEPTH, NX), f32),
+        ],
         compiler_params=ROOM,
     )(position, own, left, right)
 
@@ -273,11 +290,15 @@
     planes,
     features,
     result,
+    flat,
 ):
+    flat[...] = other[...].astype(f32)
+
     def plane_step(pair, carry):
-        density = kept[pl.ds(2 * pair, 2)] + other[pl.ds(2 * pair, 2)].astype(f32)
-        density = density.astype(bf16)
-        field = jnp.concatenate([density[0], density[1]], axis=1)
+        density = [
+            kept[row] + flat[pl.ds(DEPTH * row, DEPTH), :] for row in (2 * pair, 2 * pair + 1)
+        ]
+        field = jnp.concatenate(density, axis=1).astype(bf16)
         both = jnp.dot(plane_table[...], field, preferred_element_type=f32)
         total = both[: CHAN * CZ] + both[CHAN * CZ :]
         planes[2 * pair] = total[:, :NX]
@@ -360,6 +381,7 @@
             pltpu.VMEM((ROWS, CHAN * CZ, NX), f32),
             pltpu.VMEM((CHAN, HALF * CZ, NX), f32),
             pltpu.VMEM((HALF * CZ, NX), f32),
+            pltpu.VMEM((ROWS * DEPTH, NX), f32),
         ],
         compiler_params=ROOM,
     )(taps, kept, other, *tables)
@@ -376,9 +398,9 @@
 
 def model_tables(kernel_widths, w_in, b_in, w_mid, b_mid, w_out, b_out):
     out_index = jnp.arange(CZ, dtype=jnp.int32)
-    in_index = jnp.arange(PLANES, dtype=jnp.int32) - FIRST_PLANE
+    in_index = jnp.arange(DEPTH, dtype=jnp.int32) - RAD
     plane = tap_weights(kernel_widths, in_index[None, :] - out_index[:, None])
-    plane = plane.reshape(CHAN * CZ, PLANES)
+    plane = plane.reshape(CHAN * CZ, DEPTH)
     plane_table = jnp.concatenate(split_table(plane), axis=0)
     source = jnp.arange(NX, dtype=jnp.int32)
     around = (source[:, None] - source[None, :] + NX // 2) % NX - NX // 2

time: 134 us -> 132 us (0.985)
  no operation moved by 1% of the time
where the time goes in v7:
time: 132 us; the launch traced here: 131 us
  waiting for transfers between devices  71.3 us (54%)
  starting transfers between devices  29.9 us (23%)
  Pallas kernels  23.5 us (18%)
  local copies, waits for them, and re-layouts  3.22 us (2%)
  between operations  1.91 us (1%)
  other arithmetic  1.56 us (1%)
    all_to_all x2, waiting for transfers between devices, exchange(): return lax.all_to_all(x, axis, split_axis=0, concat_axis=0, tiled=True)  45.1 us
    all_to_all x2, starting transfers between devices, exchange(): return lax.all_to_all(x, axis, split_axis=0, concat_axis=0, tiled=True)  16.3 us
    ppermute x6, waiting for transfers between devices, shifted(): return lax.ppermute(x, axis, [(i, (i + by) % count) for i in range(count)])  14.4 us
    pallas_call x1, Pallas kernels, model(): pl.pallas_call(model_body, name='smooth_and_network', out_shape=jax.Shape...  12.3 us
    ppermute x4, waiting for transfers between devices, across_rows(): return lax.ppermute(x, ('gy', 'orb'), pairs)  11.8 us
    ppermute x4, starting transfers between devices, across_rows(): return lax.ppermute(x, ('gy', 'orb'), pairs)  9.68 us
    ppermute x6, starting transfers between devices, shifted(): return lax.ppermute(x, axis, [(i, (i + by) % count) for i in range(count)])  3.95 us
    pallas_call x1, Pallas kernels, cut(): pl.pallas_call(cut_body, name='cut_windows', out_shape=jax.ShapeDtypeStru...  3.92 us
  transfers between devices with their start and end apart: 12, of which 10 were waited for; matrix products, arithmetic and copies ran while one was open for 3% of the time, Pallas kernels for 0%

profile of v7, /device:TPU:1, one launch (start us, length us, event | category | flops | bytes accessed | tf_op | source)
XLA Modules:
  0.0 131.5 jit_solution(14783046760752062554)
XLA Ops:
  0.6 2.3 %pack_boxes.1 = bf16[16,224,128]{2,1,0:T(8,128)(2,1)} custom-call(s32[3,16]{1,0:T(4,128)} %bitcast.16, f32[16]{0:T(128)} %occupation_in.1, bf16[16,24,576]{2,1,0:T(8,128)(2,1)} %orbitals.3), custom_call_target="tpu_custom_call" | custom-call | tf_op jit(solution)/shard_map/pack_boxes/pallas_call | solution.py:126
  3.0 10.0 %all-to-all-start = ((bf16[16,224,128]{2,1,0:T(8,128)(2,1)}), bf16[16,224,128]{2,1,0:T(8,128)(2,1)S(1)}, u32[]{:S(2)}, u32[]{:S(2)}) async-start(bf16[16,224,128]{2,1,0:T(8,128)(2,1)} %pack_boxes.1), calls=%async_computation | async-start | bytes 1835008 | tf_op jit(solution)/shard_map/all_to_all | solution.py:588
  13.3 0.1 broadcast_multiply_fusion
  13.3 0.1 mul.76
  13.5 0.1 copy.43
  13.8 0.1 copy.45
  13.9 0.2 fusion.15
  14.2 0.1 div.142
  14.4 0.1 div.135
  14.5 0.1 div.133
  14.6 0.1 broadcast_in_dim.74
  14.7 0.1 copy.42
  14.9 0.1 copy.46
  15.0 0.2 copy.47
  15.3 0.1 broadcast_multiply_fusion.1
  15.4 0.1 mul.84
  15.7 0.1 broadcast_in_dim.81
  15.9 0.3 concatenate.31.first_table
  16.3 0.2 fusion.14
  16.6 0.2 fusion.4
  16.8 0.1 fusion.1.column_table
  17.0 21.3 %all-to-all-done.received = bf16[16,224,128]{2,1,0:T(8,128)(2,1)S(1)} async-done(((bf16[16,224,128]{2,1,0:T(8,128)(2,1)}), bf16[16,224,128]{2,1,0:T(8,128)(2,1)S(1)}, u32[]{:S(2)}, u32[]{:S(2)}) %all-to-all-start) | async-done | bytes 917536 | tf_op jit(solution)/shard_map/all_to_all | solution.py:588
  38.4 3.0 %deposit_boxes.1 = (f32[48,40,128]{2,1,0:T(8,128)S(1)}, bf16[48,24,128]{2,1,0:T(8,128)(2,1)S(1)}, bf16[48,16,128]{2,1,0:T(8,128)(2,1)S(1)}, s32[16,128]{1,0:T(8,128)S(1)}) custom-call(bf16[16,224,128]{2,1,0:T(8,128)(2,1)S(1)} %all-to-all-done.received), custom_call_target="tpu_custom_call" | custom-call | tf_op jit(solution)/shard_map/deposit_boxes/pallas_call | solution.py:195
  41.4 0.5 collective-permute-start.1
  41.9 4.9 %collective-permute-done.1.above = bf16[48,16,128]{2,1,0:T(8,128)(2,1)S(1)} collective-permute-done((bf16[48,16,128]{2,1,0:T(8,128)(2,1)S(1)}, bf16[48,16,128]{2,1,0:T(8,128)(2,1)S(1)}, u32[]{:S(2)}, u32[]{:S(2)}) %collective-permute-start.1) | collective-permute-done | bytes 196640 | tf_op jit(solution)/shard_map/ppermute | solution.py:43
  46.8 0.2 fold_planes.1
  47.1 2.6 %collective-permute-start.2 = (bf16[648,128]{1,0:T(8,128)(2,1)S(1)}, bf16[648,128]{1,0:T(8,128)(2,1)S(1)}, u32[]{:S(2)}, u32[]{:S(2)}) collective-permute-start(bf16[648,128]{1,0:T(8,128)(2,1)S(1)} %get-tuple-element.29), channel_id=1, source_target_pairs={{0,3},{1,2},{2,5},{3,4},{4,7},{5,6},{6,9},{7,8},{8,11},{9,10},{10,... | collective-permute-start | bytes 497672 | tf_op jit(solution)/shard_map/ppermute | solution.py:53
  49.6 2.5 %collective-permute-start.3 = (bf16[648,128]{1,0:T(8,128)(2,1)S(1)}, bf16[648,128]{1,0:T(8,128)(2,1)S(1)}, u32[]{:S(2)}, u32[]{:S(2)}) collective-permute-start(bf16[648,128]{1,0:T(8,128)(2,1)S(1)} %get-tuple-element.30), channel_id=1, source_target_pairs={{0,15},{1,14},{2,1},{3,0},{4,3},{5,2},{6,5},{7,4},{8,7},{9,6},{10,... | collective-permute-start | bytes 497672 | tf_op jit(solution)/shard_map/ppermute | solution.py:53
  52.1 4.0 %collective-permute-done.2.left = bf16[648,128]{1,0:T(8,128)(2,1)S(1)} collective-permute-done((bf16[648,128]{1,0:T(8,128)(2,1)S(1)}, bf16[648,128]{1,0:T(8,128)(2,1)S(1)}, u32[]{:S(2)}, u32[]{:S(2)}) %collective-permute-start.2) | collective-permute-done | bytes 165920 | tf_op jit(solution)/shard_map/ppermute | solution.py:53
  56.2 2.1 %collective-permute-done.3.right = bf16[648,128]{1,0:T(8,128)(2,1)S(1)} collective-permute-done((bf16[648,128]{1,0:T(8,128)(2,1)S(1)}, bf16[648,128]{1,0:T(8,128)(2,1)S(1)}, u32[]{:S(2)}, u32[]{:S(2)}) %collective-permute-start.3) | collective-permute-done | bytes 165920 | tf_op jit(solution)/shard_map/ppermute | solution.py:53
  58.3 0.2 fold_rows.1
  58.5 0.1 collective-permute-start.4
  59.3 0.1 copy.49.plane_table
  59.4 4.9 %collective-permute-done.4.other = bf16[864,128]{1,0:T(8,128)(2,1)S(1)} collective-permute-done((bf16[864,128]{1,0:T(8,128)(2,1)S(1)}, bf16[864,128]{1,0:T(8,128)(2,1)S(1)}, u32[]{:S(2)}, u32[]{:S(2)}) %collective-permute-start.4) | collective-permute-done | bytes 221216 | tf_op jit(solution)/shard_map/ppermute | solution.py:43
  64.3 12.3 %smooth_and_network.1.own = bf16[12,24,128]{2,1,0:T(8,128)(2,1)S(1)} custom-call(f32[8,13]{1,0:T(8,128)S(1)} %fusion.13.taps, f32[24,36,128]{2,1,0:T(8,128)S(1)} %get-tuple-element.31.kept, bf16[864,128]{1,0:T(8,128)(2,1)S(1)} %collective-permute-done.4.other, bf16[384,36]{1,0:T(8,128)(2,1)S(1)} %copy.49.plane_table, ...), custom_call_target="tpu_custom_call" | custom-call | tf_op jit(solution)/shard_map/smooth_and_network/pallas_call | solution.py:374
  76.6 3.7 %collective-permute-start.5 = (bf16[12,24,128]{2,1,0:T(8,128)(2,1)S(1)}, bf16[12,24,128]{2,1,0:T(8,128)(2,1)S(1)}, u32[]{:S(2)}, u32[]{:S(2)}) collective-permute-start(bf16[12,24,128]{2,1,0:T(8,128)(2,1)S(1)} %smooth_and_network.1.own), channel_id=1, source_target_pairs={{0,14},{1,3},{2,0},{3,5},{4,2},{5,7},{6,4},{7,9},{8,6},{9,11},{10,... | collective-permute-start | bytes 221192 | tf_op jit(solution)/shard_map/ppermute | solution.py:53
  80.2 0.9 collective-permute-start.6
  81.2 0.5 collective-permute-done.5.far
  81.6 5.1 %collective-permute-done.6.near = bf16[12,24,128]{2,1,0:T(8,128)(2,1)S(1)} collective-permute-done((bf16[12,24,128]{2,1,0:T(8,128)(2,1)S(1)}, bf16[12,24,128]{2,1,0:T(8,128)(2,1)S(1)}, u32[]{:S(2)}, u32[]{:S(2)}) %collective-permute-start.6) | collective-permute-done | bytes 73760 | tf_op jit(solution)/shard_map/ppermute | solution.py:53
  86.9 2.6 %collective-permute-start.8 = (bf16[48,16,128]{2,1,0:T(8,128)(2,1)S(1)}, bf16[48,16,128]{2,1,0:T(8,128)(2,1)S(1)}, u32[]{:S(2)}, u32[]{:S(2)}) collective-permute-start(bf16[48,16,128]{2,1,0:T(8,128)(2,1)S(1)} %get-tuple-element.40), channel_id=1, source_target_pairs={{0,16},{16,32},{32,48},{48,64},{64,80},{80,96},{96,112},{112,128},... | collective-permute-start | bytes 589832 | tf_op jit(solution)/shard_map/ppermute | solution.py:43
  89.5 0.7 collective-permute-start.9
  90.2 1.9 %collective-permute-done.8.below = bf16[48,16,128]{2,1,0:T(8,128)(2,1)S(1)} collective-permute-done((bf16[48,16,128]{2,1,0:T(8,128)(2,1)S(1)}, bf16[48,16,128]{2,1,0:T(8,128)(2,1)S(1)}, u32[]{:S(2)}, u32[]{:S(2)}) %collective-permute-start.8) | collective-permute-done | bytes 196640 | tf_op jit(solution)/shard_map/ppermute | solution.py:43
  92.1 2.8 %collective-permute-done.9.above = bf16[48,16,128]{2,1,0:T(8,128)(2,1)S(1)} collective-permute-done((bf16[48,16,128]{2,1,0:T(8,128)(2,1)S(1)}, bf16[48,16,128]{2,1,0:T(8,128)(2,1)S(1)}, u32[]{:S(2)}, u32[]{:S(2)}) %collective-permute-start.9) | collective-permute-done | bytes 196640 | tf_op jit(solution)/shard_map/ppermute | solution.py:43
  94.9 3.9 %cut_windows.1 = bf16[16,216,128]{2,1,0:T(8,128)(2,1)} custom-call(s32[16,128]{1,0:T(8,128)S(1)} %get-tuple-element.42.rows, bf16[48,24,128]{2,1,0:T(8,128)(2,1)S(1)} %get-tuple-element.41.wide, bf16[48,16,128]{2,1,0:T(8,128)(2,1)S(1)} %collective-permute-done.8.below, bf16[48,16,128]{2,1,0:T(8,128)(2,1)S(1)} %collective-permute-done.9.above), custom_call_target="tpu_custom_call" | custom-call | tf_op jit(solution)/shard_map/cut_windows/pallas_call | solution.py:524
  98.8 6.3 %all-to-all-start.1 = ((bf16[16,216,128]{2,1,0:T(8,128)(2,1)}), bf16[16,216,128]{2,1,0:T(8,128)(2,1)S(1)}, u32[]{:S(2)}, u32[]{:S(2)}) async-start(bf16[16,216,128]{2,1,0:T(8,128)(2,1)} %cut_windows.1), calls=%async_computation.1 | async-start | bytes 1769472 | tf_op jit(solution)/shard_map/all_to_all | solution.py:588
  105.2 0.7 copy.50
  105.9 23.8 %all-to-all-done.1.windows = bf16[16,216,128]{2,1,0:T(8,128)(2,1)S(1)} async-done(((bf16[16,216,128]{2,1,0:T(8,128)(2,1)}), bf16[16,216,128]{2,1,0:T(8,128)(2,1)S(1)}, u32[]{:S(2)}, u32[]{:S(2)}) %all-to-all-start.1) | async-done | bytes 884768 | tf_op jit(solution)/shard_map/all_to_all | solution.py:588
  129.7 1.6 %apply_windows.1 = bf16[16,24,576]{2,1,0:T(8,128)(2,1)} custom-call(s32[3,16]{1,0:T(4,128)S(1)} %bitcast.17, bf16[16,216,128]{2,1,0:T(8,128)(2,1)S(1)} %all-to-all-done.1.windows, bf16[16,24,576]{2,1,0:T(8,128)(2,1)S(1)} %copy-done), custom_call_target="tpu_custom_call" | custom-call | tf_op jit(solution)/shard_map/apply_windows/pallas_call | solution.py:572
  (61 shorter events, 1.5 us)
Async XLA Ops:
  2.9 10.3 %copy-start.3 = (f32[8,64]{1,0:T(8,128)S(1)}, f32[8,64]{1,0:T(8,128)}, u32[]{:S(2)}) copy-start(f32[8,64]{1,0:T(8,128)} %param.14) | copy-start | bytes 6148
  3.0 35.3 %all-to-all-start = ((bf16[16,224,128]{2,1,0:T(8,128)(2,1)}), bf16[16,224,128]{2,1,0:T(8,128)(2,1)S(1)}, u32[]{:S(2)}, u32[]{:S(2)}) async-start(bf16[16,224,128]{2,1,0:T(8,128)(2,1)} %pack_boxes.1), calls=%async_computation | async-start | bytes 1835008 | tf_op jit(solution)/shard_map/all_to_all | solution.py:588
  12.9 0.7 copy-start.4
  13.0 1.0 copy-start.5
  13.5 1.8 %copy-start.2 = (f32[64,64]{1,0:T(8,128)S(1)}, f32[64,64]{1,0:T(8,128)}, u32[]{:S(2)}) copy-start(f32[64,64]{1,0:T(8,128)} %param.16) | copy-start | bytes 49156
  13.6 1.9 %copy-start.6 = (f32[64]{0:T(128)S(1)}, f32[64]{0:T(128)}, u32[]{:S(2)}) copy-start(f32[64]{0:T(128)} %param.17) | copy-start | bytes 772
  13.6 2.0 %copy-start.7 = (f32[64]{0:T(128)S(1)}, f32[64]{0:T(128)}, u32[]{:S(2)}) copy-start(f32[64]{0:T(128)} %param.18) | copy-start | bytes 772
  41.4 5.4 %collective-permute-start = (bf16[48,24,128]{2,1,0:T(8,128)(2,1)S(1)}, bf16[48,24,128]{2,1,0:T(8,128)(2,1)S(1)}, u32[]{:S(2)}, u32[]{:S(2)}) collective-permute-start(bf16[48,24,128]{2,1,0:T(8,128)(2,1)S(1)} %get-tuple-element.26), channel_id=1, source_target_pairs={{0,16},{16,32},{32,48},{48,64},{64,80},{80,96},{96,112},{112,128},... | collective-permute-start | bytes 884744 | tf_op jit(solution)/shard_map/ppermute | solution.py:43
  41.4 5.4 %collective-permute-start.1 = (bf16[48,16,128]{2,1,0:T(8,128)(2,1)S(1)}, bf16[48,16,128]{2,1,0:T(8,128)(2,1)S(1)}, u32[]{:S(2)}, u32[]{:S(2)}) collective-permute-start(bf16[48,16,128]{2,1,0:T(8,128)(2,1)S(1)} %get-tuple-element.27), channel_id=1, source_target_pairs={{0,240},{16,0},{32,16},{48,32},{64,48},{80,64},{96,80},{112,96},{1... | collective-permute-start | bytes 589832 | tf_op jit(solution)/shard_map/ppermute | solution.py:43
  47.1 9.1 %collective-permute-start.2 = (bf16[648,128]{1,0:T(8,128)(2,1)S(1)}, bf16[648,128]{1,0:T(8,128)(2,1)S(1)}, u32[]{:S(2)}, u32[]{:S(2)}) collective-permute-start(bf16[648,128]{1,0:T(8,128)(2,1)S(1)} %get-tuple-element.29), channel_id=1, source_target_pairs={{0,3},{1,2},{2,5},{3,4},{4,7},{5,6},{6,9},{7,8},{8,11},{9,10},{10,... | collective-permute-start | bytes 497672 | tf_op jit(solution)/shard_map/ppermute | solution.py:53
  49.6 8.7 %collective-permute-start.3 = (bf16[648,128]{1,0:T(8,128)(2,1)S(1)}, bf16[648,128]{1,0:T(8,128)(2,1)S(1)}, u32[]{:S(2)}, u32[]{:S(2)}) collective-permute-start(bf16[648,128]{1,0:T(8,128)(2,1)S(1)} %get-tuple-element.30), channel_id=1, source_target_pairs={{0,15},{1,14},{2,1},{3,0},{4,3},{5,2},{6,5},{7,4},{8,7},{9,6},{10,... | collective-permute-start | bytes 497672 | tf_op jit(solution)/shard_map/ppermute | solution.py:53
  58.5 5.8 %collective-permute-start.4 = (bf16[864,128]{1,0:T(8,128)(2,1)S(1)}, bf16[864,128]{1,0:T(8,128)(2,1)S(1)}, u32[]{:S(2)}, u32[]{:S(2)}) collective-permute-start(bf16[864,128]{1,0:T(8,128)(2,1)S(1)} %get-tuple-element.32), channel_id=1, source_target_pairs={{0,1},{1,0},{2,3},{3,2},{4,5},{5,4},{6,7},{7,6},{8,9},{9,8},{10,11... | collective-permute-start | bytes 663560 | tf_op jit(solution)/shard_map/ppermute | solution.py:43
  76.6 5.1 %collective-permute-start.5 = (bf16[12,24,128]{2,1,0:T(8,128)(2,1)S(1)}, bf16[12,24,128]{2,1,0:T(8,128)(2,1)S(1)}, u32[]{:S(2)}, u32[]{:S(2)}) collective-permute-start(bf16[12,24,128]{2,1,0:T(8,128)(2,1)S(1)} %smooth_and_network.1.own), channel_id=1, source_target_pairs={{0,14},{1,3},{2,0},{3,5},{4,2},{5,7},{6,4},{7,9},{8,6},{9,11},{10,... | collective-permute-start | bytes 221192 | tf_op jit(solution)/shard_map/ppermute | solution.py:53
  80.2 6.5 %collective-permute-start.6 = (bf16[12,24,128]{2,1,0:T(8,128)(2,1)S(1)}, bf16[12,24,128]{2,1,0:T(8,128)(2,1)S(1)}, u32[]{:S(2)}, u32[]{:S(2)}) collective-permute-start(bf16[12,24,128]{2,1,0:T(8,128)(2,1)S(1)} %smooth_and_network.1.own), channel_id=1, source_target_pairs={{0,15},{1,2},{2,1},{3,4},{4,3},{5,6},{6,5},{7,8},{8,7},{9,10},{10,... | collective-permute-start | bytes 221192 | tf_op jit(solution)/shard_map/ppermute | solution.py:53
  81.2 5.6 %collective-permute-start.7 = (bf16[12,24,128]{2,1,0:T(8,128)(2,1)S(1)}, bf16[12,24,128]{2,1,0:T(8,128)(2,1)S(1)}, u32[]{:S(2)}, u32[]{:S(2)}) collective-permute-start(bf16[12,24,128]{2,1,0:T(8,128)(2,1)S(1)} %smooth_and_network.1.own), channel_id=1, source_target_pairs={{0,1},{1,0},{2,3},{3,2},{4,5},{5,4},{6,7},{7,6},{8,9},{9,8},{10,11... | collective-permute-start | bytes 221192 | tf_op jit(solution)/shard_map/ppermute | solution.py:43
  86.9 5.2 %collective-permute-start.8 = (bf16[48,16,128]{2,1,0:T(8,128)(2,1)S(1)}, bf16[48,16,128]{2,1,0:T(8,128)(2,1)S(1)}, u32[]{:S(2)}, u32[]{:S(2)}) collective-permute-start(bf16[48,16,128]{2,1,0:T(8,128)(2,1)S(1)} %get-tuple-element.40), channel_id=1, source_target_pairs={{0,16},{16,32},{32,48},{48,64},{64,80},{80,96},{96,112},{112,128},... | collective-permute-start | bytes 589832 | tf_op jit(solution)/shard_map/ppermute | solution.py:43
  89.5 5.4 %collective-permute-start.9 = (bf16[48,16,128]{2,1,0:T(8,128)(2,1)S(1)}, bf16[48,16,128]{2,1,0:T(8,128)(2,1)S(1)}, u32[]{:S(2)}, u32[]{:S(2)}) collective-permute-start(bf16[48,16,128]{2,1,0:T(8,128)(2,1)S(1)} %get-tuple-element.43), channel_id=1, source_target_pairs={{0,240},{16,0},{32,16},{48,32},{64,48},{80,64},{96,80},{112,96},{1... | collective-permute-start | bytes 589832 | tf_op jit(solution)/shard_map/ppermute | solution.py:43
  98.8 31.0 %copy-start = (bf16[16,24,576]{2,1,0:T(8,128)(2,1)S(1)}, bf16[16,24,576]{2,1,0:T(8,128)(2,1)}, u32[]{:S(2)}) copy-start(bf16[16,24,576]{2,1,0:T(8,128)(2,1)} %orbitals.3) | copy-start | bytes 1327108
  98.8 31.0 %copy-start.1 = (s32[16,3]{0,1:T(4,128)S(1)}, s32[16,3]{0,1:T(4,128)}, u32[]{:S(2)}) copy-start(s32[16,3]{0,1:T(4,128)} %param.12) | copy-start | bytes 580
  98.8 30.9 %all-to-all-start.1 = ((bf16[16,216,128]{2,1,0:T(8,128)(2,1)}), bf16[16,216,128]{2,1,0:T(8,128)(2,1)S(1)}, u32[]{:S(2)}, u32[]{:S(2)}) async-start(bf16[16,216,128]{2,1,0:T(8,128)(2,1)} %cut_windows.1), calls=%async_computation.1 | async-start | bytes 1769472 | tf_op jit(solution)/shard_map/all_to_all | solution.py:588

commit v8 on v7

--- a/solution.py
+++ b/solution.py
@@ -451,7 +451,7 @@
     )
 
 
-def widen_body(position, far, near, partner, own, wide, first_planes, last_planes):
+def widen_body(position, near, far, partner, own, wide, first_planes, last_planes):
     orb = position[0]
     wide[pl.ds(HALF + HALF * orb, HALF)] = own[...]
     wide[pl.ds(2 * HALF - HALF * orb, HALF)] = partner[...]
@@ -461,7 +461,7 @@
     last_planes[...] = wide[...].astype(f32)[:, CZ - 16 :, :].astype(bf16)
 
 
-def widen(position, far, near, partner, own):
+def widen(position, near, far, partner, own):
     return pl.pallas_call(
         widen_body,
         name="widen_rows",
@@ -473,7 +473,7 @@
         in_specs=[SMEM] + [VMEM] * 4,
         out_specs=(VMEM,) * 3,
         compiler_params=ROOM,
-    )(position, far, near, partner, own)
+    )(position, near, far, partner, own)
 
 
 def cut_body(rows, wide, below, above, windows, reach, cuts, offsets, offsets_sem, sems):
@@ -606,7 +606,7 @@
     far = across_rows(half, (-1, 1), 0)
     near = across_rows(half, (-1, 1), 1)
     partner = shifted(half, "orb", 1)
-    wide, first_planes, last_planes = widen(position, far, near, partner, half)
+    wide, first_planes, last_planes = widen(position, near, far, partner, half)
     below = shifted(last_planes, "gz", 1)
     above = shifted(first_planes, "gz", -1)
     windows = cut(offsets, wide, below, above)

time: 132 us -> 130 us (0.985)
  waiting for transfers between devices: 71.3 us -> 69.9 us
    ppermute x4, waiting for transfers between devices: 11.8 us -> 10.3 us  [across_rows(): return lax.ppermute(x, ('gy', 'orb'), pairs)]
  transfers between devices with their start and end apart: 12 -> 12, of which waited for: 10 -> 10; matrix products, arithmetic and copies ran while one was open for 3% -> 4% of each run, Pallas kernels for 0% -> 0%
where the time goes in v8:
time: 130 us
  waiting for transfers between devices  69.9 us (54%)
  starting transfers between devices  29.9 us (23%)
  Pallas kernels  23.5 us (18%)
  local copies, waits for them, and re-layouts  3.22 us (2%)
  between operations  1.91 us (1%)
  other arithmetic  1.56 us (1%)
    all_to_all x2, waiting for transfers between devices, exchange(): return lax.all_to_all(x, axis, split_axis=0, concat_axis=0, tiled=True)  45.1 us
    all_to_all x2, starting transfers between devices, exchange(): return lax.all_to_all(x, axis, split_axis=0, concat_axis=0, tiled=True)  16.3 us
    ppermute x6, waiting for transfers between devices, shifted(): return lax.ppermute(x, axis, [(i, (i + by) % count) for i in range(count)])  14.5 us
    pallas_call x1, Pallas kernels, model(): pl.pallas_call(model_body, name='smooth_and_network', out_shape=jax.Shape...  12.3 us
    ppermute x4, waiting for transfers between devices, across_rows(): return lax.ppermute(x, ('gy', 'orb'), pairs)  10.3 us
    ppermute x4, starting transfers between devices, across_rows(): return lax.ppermute(x, ('gy', 'orb'), pairs)  9.04 us
    ppermute x6, starting transfers between devices, shifted(): return lax.ppermute(x, axis, [(i, (i + by) % count) for i in range(count)])  4.54 us
    pallas_call x1, Pallas kernels, cut(): pl.pallas_call(cut_body, name='cut_windows', out_shape=jax.ShapeDtypeStru...  3.92 us
  transfers between devices with their start and end apart: 12, of which 10 were waited for; matrix products, arithmetic and copies ran while one was open for 4% of the time, Pallas kernels for 0%

profile of v8, /device:TPU:1, one launch (start us, length us, event | category | flops | bytes accessed | tf_op | source)
XLA Modules:
  0.0 130.0 jit_solution(13118263382679500716)
XLA Ops:
  0.6 2.3 %pack_boxes.1 = bf16[16,224,128]{2,1,0:T(8,128)(2,1)} custom-call(s32[3,16]{1,0:T(4,128)} %bitcast.16, f32[16]{0:T(128)} %occupation_in.1, bf16[16,24,576]{2,1,0:T(8,128)(2,1)} %orbitals.3), custom_call_target="tpu_custom_call" | custom-call | tf_op jit(solution)/shard_map/pack_boxes/pallas_call | solution.py:126
  3.0 10.0 %all-to-all-start = ((bf16[16,224,128]{2,1,0:T(8,128)(2,1)}), bf16[16,224,128]{2,1,0:T(8,128)(2,1)S(1)}, u32[]{:S(2)}, u32[]{:S(2)}) async-start(bf16[16,224,128]{2,1,0:T(8,128)(2,1)} %pack_boxes.1), calls=%async_computation | async-start | bytes 1835008 | tf_op jit(solution)/shard_map/all_to_all | solution.py:588
  13.3 0.1 broadcast_multiply_fusion
  13.3 0.1 mul.76
  13.5 0.1 copy.43
  13.8 0.1 copy.45
  13.9 0.2 fusion.15
  14.2 0.1 div.142
  14.5 0.1 div.133
  14.6 0.1 broadcast_in_dim.74
  14.7 0.1 copy.42
  14.9 0.1 copy.46
  15.0 0.2 copy.47
  15.3 0.1 broadcast_multiply_fusion.1
  15.4 0.1 mul.84
  15.7 0.1 broadcast_in_dim.81
  15.9 0.3 concatenate.31.first_table
  16.3 0.2 fusion.14
  16.6 0.2 fusion.4
  16.8 0.1 fusion.1.column_table
  17.0 21.3 %all-to-all-done.received = bf16[16,224,128]{2,1,0:T(8,128)(2,1)S(1)} async-done(((bf16[16,224,128]{2,1,0:T(8,128)(2,1)}), bf16[16,224,128]{2,1,0:T(8,128)(2,1)S(1)}, u32[]{:S(2)}, u32[]{:S(2)}) %all-to-all-start) | async-done | bytes 917536 | tf_op jit(solution)/shard_map/all_to_all | solution.py:588
  38.4 3.0 %deposit_boxes.1 = (f32[48,40,128]{2,1,0:T(8,128)S(1)}, bf16[48,24,128]{2,1,0:T(8,128)(2,1)S(1)}, bf16[48,16,128]{2,1,0:T(8,128)(2,1)S(1)}, s32[16,128]{1,0:T(8,128)S(1)}) custom-call(bf16[16,224,128]{2,1,0:T(8,128)(2,1)S(1)} %all-to-all-done.received), custom_call_target="tpu_custom_call" | custom-call | tf_op jit(solution)/shard_map/deposit_boxes/pallas_call | solution.py:195
  41.4 0.5 collective-permute-start.1
  41.9 4.9 %collective-permute-done.1.above = bf16[48,16,128]{2,1,0:T(8,128)(2,1)S(1)} collective-permute-done((bf16[48,16,128]{2,1,0:T(8,128)(2,1)S(1)}, bf16[48,16,128]{2,1,0:T(8,128)(2,1)S(1)}, u32[]{:S(2)}, u32[]{:S(2)}) %collective-permute-start.1) | collective-permute-done | bytes 196640 | tf_op jit(solution)/shard_map/ppermute | solution.py:43
  46.8 0.2 fold_planes.1
  47.1 2.6 %collective-permute-start.2 = (bf16[648,128]{1,0:T(8,128)(2,1)S(1)}, bf16[648,128]{1,0:T(8,128)(2,1)S(1)}, u32[]{:S(2)}, u32[]{:S(2)}) collective-permute-start(bf16[648,128]{1,0:T(8,128)(2,1)S(1)} %get-tuple-element.29), channel_id=1, source_target_pairs={{0,3},{1,2},{2,5},{3,4},{4,7},{5,6},{6,9},{7,8},{8,11},{9,10},{10,... | collective-permute-start | bytes 497672 | tf_op jit(solution)/shard_map/ppermute | solution.py:53
  49.6 2.5 %collective-permute-start.3 = (bf16[648,128]{1,0:T(8,128)(2,1)S(1)}, bf16[648,128]{1,0:T(8,128)(2,1)S(1)}, u32[]{:S(2)}, u32[]{:S(2)}) collective-permute-start(bf16[648,128]{1,0:T(8,128)(2,1)S(1)} %get-tuple-element.30), channel_id=1, source_target_pairs={{0,15},{1,14},{2,1},{3,0},{4,3},{5,2},{6,5},{7,4},{8,7},{9,6},{10,... | collective-permute-start | bytes 497672 | tf_op jit(solution)/shard_map/ppermute | solution.py:53
  52.2 4.0 %collective-permute-done.2.left = bf16[648,128]{1,0:T(8,128)(2,1)S(1)} collective-permute-done((bf16[648,128]{1,0:T(8,128)(2,1)S(1)}, bf16[648,128]{1,0:T(8,128)(2,1)S(1)}, u32[]{:S(2)}, u32[]{:S(2)}) %collective-permute-start.2) | collective-permute-done | bytes 165920 | tf_op jit(solution)/shard_map/ppermute | solution.py:53
  56.2 2.1 %collective-permute-done.3.right = bf16[648,128]{1,0:T(8,128)(2,1)S(1)} collective-permute-done((bf16[648,128]{1,0:T(8,128)(2,1)S(1)}, bf16[648,128]{1,0:T(8,128)(2,1)S(1)}, u32[]{:S(2)}, u32[]{:S(2)}) %collective-permute-start.3) | collective-permute-done | bytes 165920 | tf_op jit(solution)/shard_map/ppermute | solution.py:53
  58.3 0.2 fold_rows.1
  58.5 0.1 collective-permute-start.4
  59.3 0.1 copy.49.plane_table
  59.4 4.9 %collective-permute-done.4.other = bf16[864,128]{1,0:T(8,128)(2,1)S(1)} collective-permute-done((bf16[864,128]{1,0:T(8,128)(2,1)S(1)}, bf16[864,128]{1,0:T(8,128)(2,1)S(1)}, u32[]{:S(2)}, u32[]{:S(2)}) %collective-permute-start.4) | collective-permute-done | bytes 221216 | tf_op jit(solution)/shard_map/ppermute | solution.py:43
  64.3 12.3 %smooth_and_network.1.own = bf16[12,24,128]{2,1,0:T(8,128)(2,1)S(1)} custom-call(f32[8,13]{1,0:T(8,128)S(1)} %fusion.13.taps, f32[24,36,128]{2,1,0:T(8,128)S(1)} %get-tuple-element.31.kept, bf16[864,128]{1,0:T(8,128)(2,1)S(1)} %collective-permute-done.4.other, bf16[384,36]{1,0:T(8,128)(2,1)S(1)} %copy.49.plane_table, ...), custom_call_target="tpu_custom_call" | custom-call | tf_op jit(solution)/shard_map/smooth_and_network/pallas_call | solution.py:374
  76.6 3.7 %collective-permute-start.5 = (bf16[12,24,128]{2,1,0:T(8,128)(2,1)S(1)}, bf16[12,24,128]{2,1,0:T(8,128)(2,1)S(1)}, u32[]{:S(2)}, u32[]{:S(2)}) collective-permute-start(bf16[12,24,128]{2,1,0:T(8,128)(2,1)S(1)} %smooth_and_network.1.own), channel_id=1, source_target_pairs={{0,15},{1,2},{2,1},{3,4},{4,3},{5,6},{6,5},{7,8},{8,7},{9,10},{10,... | collective-permute-start | bytes 221192 | tf_op jit(solution)/shard_map/ppermute | solution.py:53
  80.3 0.3 collective-permute-start.6
  80.5 0.4 collective-permute-start.7
  80.9 2.2 %collective-permute-done.5.near = bf16[12,24,128]{2,1,0:T(8,128)(2,1)S(1)} collective-permute-done((bf16[12,24,128]{2,1,0:T(8,128)(2,1)S(1)}, bf16[12,24,128]{2,1,0:T(8,128)(2,1)S(1)}, u32[]{:S(2)}, u32[]{:S(2)}) %collective-permute-start.5) | collective-permute-done | bytes 73760 | tf_op jit(solution)/shard_map/ppermute | solution.py:53
  83.2 1.9 %collective-permute-done.6.far = bf16[12,24,128]{2,1,0:T(8,128)(2,1)S(1)} collective-permute-done((bf16[12,24,128]{2,1,0:T(8,128)(2,1)S(1)}, bf16[12,24,128]{2,1,0:T(8,128)(2,1)S(1)}, u32[]{:S(2)}, u32[]{:S(2)}) %collective-permute-start.6) | collective-permute-done | bytes 73760 | tf_op jit(solution)/shard_map/ppermute | solution.py:53
  85.2 2.8 %collective-permute-start.8 = (bf16[48,16,128]{2,1,0:T(8,128)(2,1)S(1)}, bf16[48,16,128]{2,1,0:T(8,128)(2,1)S(1)}, u32[]{:S(2)}, u32[]{:S(2)}) collective-permute-start(bf16[48,16,128]{2,1,0:T(8,128)(2,1)S(1)} %get-tuple-element.40), channel_id=1, source_target_pairs={{0,16},{16,32},{32,48},{48,64},{64,80},{80,96},{96,112},{112,128},... | collective-permute-start | bytes 589832 | tf_op jit(solution)/shard_map/ppermute | solution.py:43
  87.9 0.7 collective-permute-start.9
  88.7 1.9 %collective-permute-done.8.below = bf16[48,16,128]{2,1,0:T(8,128)(2,1)S(1)} collective-permute-done((bf16[48,16,128]{2,1,0:T(8,128)(2,1)S(1)}, bf16[48,16,128]{2,1,0:T(8,128)(2,1)S(1)}, u32[]{:S(2)}, u32[]{:S(2)}) %collective-permute-start.8) | collective-permute-done | bytes 196640 | tf_op jit(solution)/shard_map/ppermute | solution.py:43
  90.6 2.8 %collective-permute-done.9.above = bf16[48,16,128]{2,1,0:T(8,128)(2,1)S(1)} collective-permute-done((bf16[48,16,128]{2,1,0:T(8,128)(2,1)S(1)}, bf16[48,16,128]{2,1,0:T(8,128)(2,1)S(1)}, u32[]{:S(2)}, u32[]{:S(2)}) %collective-permute-start.9) | collective-permute-done | bytes 196640 | tf_op jit(solution)/shard_map/ppermute | solution.py:43
  93.3 3.9 %cut_windows.1 = bf16[16,216,128]{2,1,0:T(8,128)(2,1)} custom-call(s32[16,128]{1,0:T(8,128)S(1)} %get-tuple-element.42.rows, bf16[48,24,128]{2,1,0:T(8,128)(2,1)S(1)} %get-tuple-element.41.wide, bf16[48,16,128]{2,1,0:T(8,128)(2,1)S(1)} %collective-permute-done.8.below, bf16[48,16,128]{2,1,0:T(8,128)(2,1)S(1)} %collective-permute-done.9.above), custom_call_target="tpu_custom_call" | custom-call | tf_op jit(solution)/shard_map/cut_windows/pallas_call | solution.py:524
  97.3 6.3 %all-to-all-start.1 = ((bf16[16,216,128]{2,1,0:T(8,128)(2,1)}), bf16[16,216,128]{2,1,0:T(8,128)(2,1)S(1)}, u32[]{:S(2)}, u32[]{:S(2)}) async-start(bf16[16,216,128]{2,1,0:T(8,128)(2,1)} %cut_windows.1), calls=%async_computation.1 | async-start | bytes 1769472 | tf_op jit(solution)/shard_map/all_to_all | solution.py:588
  103.7 0.7 copy.50
  104.4 23.8 %all-to-all-done.1.windows = bf16[16,216,128]{2,1,0:T(8,128)(2,1)S(1)} async-done(((bf16[16,216,128]{2,1,0:T(8,128)(2,1)}), bf16[16,216,128]{2,1,0:T(8,128)(2,1)S(1)}, u32[]{:S(2)}, u32[]{:S(2)}) %all-to-all-start.1) | async-done | bytes 884768 | tf_op jit(solution)/shard_map/all_to_all | solution.py:588
  128.2 1.6 %apply_windows.1 = bf16[16,24,576]{2,1,0:T(8,128)(2,1)} custom-call(s32[3,16]{1,0:T(4,128)S(1)} %bitcast.17, bf16[16,216,128]{2,1,0:T(8,128)(2,1)S(1)} %all-to-all-done.1.windows, bf16[16,24,576]{2,1,0:T(8,128)(2,1)S(1)} %copy-done), custom_call_target="tpu_custom_call" | custom-call | tf_op jit(solution)/shard_map/apply_windows/pallas_call | solution.py:572
  (61 shorter events, 1.5 us)
Async XLA Ops:
  2.9 10.3 %copy-start.3 = (f32[8,64]{1,0:T(8,128)S(1)}, f32[8,64]{1,0:T(8,128)}, u32[]{:S(2)}) copy-start(f32[8,64]{1,0:T(8,128)} %param.14) | copy-start | bytes 6148
  3.0 35.3 %all-to-all-start = ((bf16[16,224,128]{2,1,0:T(8,128)(2,1)}), bf16[16,224,128]{2,1,0:T(8,128)(2,1)S(1)}, u32[]{:S(2)}, u32[]{:S(2)}) async-start(bf16[16,224,128]{2,1,0:T(8,128)(2,1)} %pack_boxes.1), calls=%async_computation | async-start | bytes 1835008 | tf_op jit(solution)/shard_map/all_to_all | solution.py:588
  12.9 0.7 copy-start.4
  13.0 1.0 copy-start.5
  13.5 1.8 %copy-start.2 = (f32[64,64]{1,0:T(8,128)S(1)}, f32[64,64]{1,0:T(8,128)}, u32[]{:S(2)}) copy-start(f32[64,64]{1,0:T(8,128)} %param.16) | copy-start | bytes 49156
  13.6 1.9 %copy-start.6 = (f32[64]{0:T(128)S(1)}, f32[64]{0:T(128)}, u32[]{:S(2)}) copy-start(f32[64]{0:T(128)} %param.17) | copy-start | bytes 772
  13.6 2.0 %copy-start.7 = (f32[64]{0:T(128)S(1)}, f32[64]{0:T(128)}, u32[]{:S(2)}) copy-start(f32[64]{0:T(128)} %param.18) | copy-start | bytes 772
  41.4 5.4 %collective-permute-start = (bf16[48,24,128]{2,1,0:T(8,128)(2,1)S(1)}, bf16[48,24,128]{2,1,0:T(8,128)(2,1)S(1)}, u32[]{:S(2)}, u32[]{:S(2)}) collective-permute-start(bf16[48,24,128]{2,1,0:T(8,128)(2,1)S(1)} %get-tuple-element.26), channel_id=1, source_target_pairs={{0,16},{16,32},{32,48},{48,64},{64,80},{80,96},{96,112},{112,128},... | collective-permute-start | bytes 884744 | tf_op jit(solution)/shard_map/ppermute | solution.py:43
  41.4 5.4 %collective-permute-start.1 = (bf16[48,16,128]{2,1,0:T(8,128)(2,1)S(1)}, bf16[48,16,128]{2,1,0:T(8,128)(2,1)S(1)}, u32[]{:S(2)}, u32[]{:S(2)}) collective-permute-start(bf16[48,16,128]{2,1,0:T(8,128)(2,1)S(1)} %get-tuple-element.27), channel_id=1, source_target_pairs={{0,240},{16,0},{32,16},{48,32},{64,48},{80,64},{96,80},{112,96},{1... | collective-permute-start | bytes 589832 | tf_op jit(solution)/shard_map/ppermute | solution.py:43
  47.1 9.1 %collective-permute-start.2 = (bf16[648,128]{1,0:T(8,128)(2,1)S(1)}, bf16[648,128]{1,0:T(8,128)(2,1)S(1)}, u32[]{:S(2)}, u32[]{:S(2)}) collective-permute-start(bf16[648,128]{1,0:T(8,128)(2,1)S(1)} %get-tuple-element.29), channel_id=1, source_target_pairs={{0,3},{1,2},{2,5},{3,4},{4,7},{5,6},{6,9},{7,8},{8,11},{9,10},{10,... | collective-permute-start | bytes 497672 | tf_op jit(solution)/shard_map/ppermute | solution.py:53
  49.6 8.7 %collective-permute-start.3 = (bf16[648,128]{1,0:T(8,128)(2,1)S(1)}, bf16[648,128]{1,0:T(8,128)(2,1)S(1)}, u32[]{:S(2)}, u32[]{:S(2)}) collective-permute-start(bf16[648,128]{1,0:T(8,128)(2,1)S(1)} %get-tuple-element.30), channel_id=1, source_target_pairs={{0,15},{1,14},{2,1},{3,0},{4,3},{5,2},{6,5},{7,4},{8,7},{9,6},{10,... | collective-permute-start | bytes 497672 | tf_op jit(solution)/shard_map/ppermute | solution.py:53
  58.5 5.8 %collective-permute-start.4 = (bf16[864,128]{1,0:T(8,128)(2,1)S(1)}, bf16[864,128]{1,0:T(8,128)(2,1)S(1)}, u32[]{:S(2)}, u32[]{:S(2)}) collective-permute-start(bf16[864,128]{1,0:T(8,128)(2,1)S(1)} %get-tuple-element.32), channel_id=1, source_target_pairs={{0,1},{1,0},{2,3},{3,2},{4,5},{5,4},{6,7},{7,6},{8,9},{9,8},{10,11... | collective-permute-start | bytes 663560 | tf_op jit(solution)/shard_map/ppermute | solution.py:43
  76.6 6.6 %collective-permute-start.5 = (bf16[12,24,128]{2,1,0:T(8,128)(2,1)S(1)}, bf16[12,24,128]{2,1,0:T(8,128)(2,1)S(1)}, u32[]{:S(2)}, u32[]{:S(2)}) collective-permute-start(bf16[12,24,128]{2,1,0:T(8,128)(2,1)S(1)} %smooth_and_network.1.own), channel_id=1, source_target_pairs={{0,15},{1,2},{2,1},{3,4},{4,3},{5,6},{6,5},{7,8},{8,7},{9,10},{10,... | collective-permute-start | bytes 221192 | tf_op jit(solution)/shard_map/ppermute | solution.py:53
  80.3 4.8 %collective-permute-start.6 = (bf16[12,24,128]{2,1,0:T(8,128)(2,1)S(1)}, bf16[12,24,128]{2,1,0:T(8,128)(2,1)S(1)}, u32[]{:S(2)}, u32[]{:S(2)}) collective-permute-start(bf16[12,24,128]{2,1,0:T(8,128)(2,1)S(1)} %smooth_and_network.1.own), channel_id=1, source_target_pairs={{0,14},{1,3},{2,0},{3,5},{4,2},{5,7},{6,4},{7,9},{8,6},{9,11},{10,... | collective-permute-start | bytes 221192 | tf_op jit(solution)/shard_map/ppermute | solution.py:53
  80.5 4.5 %collective-permute-start.7 = (bf16[12,24,128]{2,1,0:T(8,128)(2,1)S(1)}, bf16[12,24,128]{2,1,0:T(8,128)(2,1)S(1)}, u32[]{:S(2)}, u32[]{:S(2)}) collective-permute-start(bf16[12,24,128]{2,1,0:T(8,128)(2,1)S(1)} %smooth_and_network.1.own), channel_id=1, source_target_pairs={{0,1},{1,0},{2,3},{3,2},{4,5},{5,4},{6,7},{7,6},{8,9},{9,8},{10,11... | collective-permute-start | bytes 221192 | tf_op jit(solution)/shard_map/ppermute | solution.py:43
  85.2 5.4 %collective-permute-start.8 = (bf16[48,16,128]{2,1,0:T(8,128)(2,1)S(1)}, bf16[48,16,128]{2,1,0:T(8,128)(2,1)S(1)}, u32[]{:S(2)}, u32[]{:S(2)}) collective-permute-start(bf16[48,16,128]{2,1,0:T(8,128)(2,1)S(1)} %get-tuple-element.40), channel_id=1, source_target_pairs={{0,16},{16,32},{32,48},{48,64},{64,80},{80,96},{96,112},{112,128},... | collective-permute-start | bytes 589832 | tf_op jit(solution)/shard_map/ppermute | solution.py:43
  87.9 5.4 %collective-permute-start.9 = (bf16[48,16,128]{2,1,0:T(8,128)(2,1)S(1)}, bf16[48,16,128]{2,1,0:T(8,128)(2,1)S(1)}, u32[]{:S(2)}, u32[]{:S(2)}) collective-permute-start(bf16[48,16,128]{2,1,0:T(8,128)(2,1)S(1)} %get-tuple-element.43), channel_id=1, source_target_pairs={{0,240},{16,0},{32,16},{48,32},{64,48},{80,64},{96,80},{112,96},{1... | collective-permute-start | bytes 589832 | tf_op jit(solution)/shard_map/ppermute | solution.py:43
  97.3 31.0 %copy-start = (bf16[16,24,576]{2,1,0:T(8,128)(2,1)S(1)}, bf16[16,24,576]{2,1,0:T(8,128)(2,1)}, u32[]{:S(2)}) copy-start(bf16[16,24,576]{2,1,0:T(8,128)(2,1)} %orbitals.3) | copy-start | bytes 1327108
  97.3 30.9 %copy-start.1 = (s32[16,3]{0,1:T(4,128)S(1)}, s32[16,3]{0,1:T(4,128)}, u32[]{:S(2)}) copy-start(s32[16,3]{0,1:T(4,128)} %param.12) | copy-start | bytes 580
  97.3 30.9 %all-to-all-start.1 = ((bf16[16,216,128]{2,1,0:T(8,128)(2,1)}), bf16[16,216,128]{2,1,0:T(8,128)(2,1)S(1)}, u32[]{:S(2)}, u32[]{:S(2)}) async-start(bf16[16,216,128]{2,1,0:T(8,128)(2,1)} %cut_windows.1), calls=%async_computation.1 | async-start | bytes 1769472 | tf_op jit(solution)/shard_map/all_to_all | solution.py:588
